TPU v7x, 32 devices: a whole 2x2x4 slice. The times are simulated.
32 devices in a mesh: head: 4 (over y, x), inner: 4 (over z), outer: 2 (over core).
Axes of the slice: x: 2, y: 2, z: 4, core: 2. Of those that a mesh axis runs over, the one named last changes fastest.
Arguments:
- queries: bfloat16 [2048, 4096], P(('head', 'inner', 'outer')), may hold values from -9 to 9
- keys: bfloat16 [2048, 512], P(('head', 'inner', 'outer')), may hold values from -6 to 6
- values: bfloat16 [2048, 512], P(('head', 'inner', 'outer')), may hold values from -6 to 6
- grad_out: bfloat16 [2048, 4096], P(('head', 'inner', 'outer')), may hold values from -6 to 6
- block_order: int32 [32], replicated, may hold values from 0 to 31, as said below
Outputs:
- query_grad: bfloat16 [2048, 4096], P(('head', 'inner', 'outer'))
- key_grad: bfloat16 [2048, 512], P(('head', 'inner', 'outer'))
- value_grad: bfloat16 [2048, 512], P(('head', 'inner', 'outer'))
Inputs may be any that keep to these rules, and one draw needn't show every extreme that they name: `block_order`: each value appears once. For each r below 8, the values at b = r, 8 + r, ..., 24 + r are, in some order, j_k + 2 k * 8 and 2 (k + 1) * 8 - 1 - j_k for each k below 2, with j_k below 8.
All inputs are finite; a program needn't handle non-finite values.
Results may differ from a plain program's by a relative error of at most 0.033.
Values may be sent and summed in bfloat16 or wider, within the bound.
No kernel may reach another device: no remote copies, remote signals or barrier semaphores. Data moves between devices by JAX's collectives and lax.ppermute only.
A program may use at most 64 MiB of HBM per device.

v0:
```python
import jax
import jax.numpy as jnp
from jax import lax
from jax.sharding import PartitionSpec as P

HEADS = 32
KV_HEADS = 4
HEAD_DIM = 128


masked_score = -1e30


def from_behind(array, axis, by):
    length = lax.axis_size(axis)
    return lax.ppermute(array, axis, [(i, (i + by) % length) for i in range(length)])


def local(queries, keys, values, grad_out, block_order):
    inner_count = lax.axis_size("inner")
    outer_count = lax.axis_size("outer")
    circle_count = inner_count * outer_count
    block_rows = queries.shape[0]
    query_flat, key_flat, value_flat, grad_flat = (
        lax.all_to_all(queries, "head", split_axis=1, concat_axis=0, tiled=True),
        lax.all_to_all(keys, "head", split_axis=1, concat_axis=0, tiled=True),
        lax.all_to_all(values, "head", split_axis=1, concat_axis=0, tiled=True),
        lax.all_to_all(grad_out, "head", split_axis=1, concat_axis=0, tiled=True),
    )
    circle_rows = query_flat.shape[0]
    kv_local = key_flat.shape[1] // HEAD_DIM
    group_size = HEADS // KV_HEADS
    score_scale = HEAD_DIM ** (-0.5)
    query_heads = query_flat.reshape(circle_rows, kv_local, group_size, HEAD_DIM)
    grad_heads = grad_flat.reshape(circle_rows, kv_local, group_size, HEAD_DIM)
    kv_pair = jnp.stack(
        [
            key_flat.reshape(circle_rows, kv_local, HEAD_DIM),
            value_flat.reshape(circle_rows, kv_local, HEAD_DIM),
        ]
    )
    inner_rank = lax.axis_index("inner")
    outer_rank = lax.axis_index("outer")
    my_rank = inner_rank * outer_count + outer_rank
    span_rows = 2 * circle_rows
    span_count = circle_count // 2

    def positions(offset, length):
        global_row = offset + jnp.arange(length, dtype=jnp.int32)
        owner_rank = global_row // circle_rows
        local_row = global_row % circle_rows
        stored_block = local_row // block_rows * circle_count + owner_rank
        return jnp.take(block_order, stored_block) * block_rows + local_row % block_rows

    query_pos = positions(my_rank * circle_rows, circle_rows)

    def score_block(key_block, key_pos):
        scores_now = (
            jnp.einsum("qcgd,kcd->cgqk", query_heads, key_block, preferred_element_type=jnp.float32)
            * score_scale
        )
        return jnp.where(query_pos[:, None] >= key_pos[None, :], scores_now, masked_score)

    def forward_fold(state_in, segment, offset):
        top_score, weight_sum, weighted = state_in
        scores_now = score_block(segment[0], positions(offset, segment.shape[1]))
        top_next = jnp.maximum(top_score, jnp.max(scores_now, axis=-1))
        rescale = jnp.exp(top_score - top_next)
        probs = jnp.exp(scores_now - top_next[..., None])
        weight_sum = weight_sum * rescale + jnp.sum(probs, axis=-1)
        weighted = weighted * rescale[..., None] + jnp.einsum(
            "cgqk,kcd->cgqd",
            probs.astype(jnp.bfloat16),
            segment[1],
            preferred_element_type=jnp.float32,
        )
        return (top_next, weight_sum, weighted)

    gathered = lax.all_gather(kv_pair, ("inner", "outer"), axis=1, tiled=True)

    def forward_turn(turn_index, state_in):
        offset = (turn_index * span_rows).astype(jnp.int32)
        segment = lax.dynamic_slice_in_dim(gathered, offset, span_rows, 1)
        return forward_fold(state_in, segment, offset)

    initial = (
        jnp.full((kv_local, group_size, circle_rows), masked_score, jnp.float32),
        jnp.zeros((kv_local, group_size, circle_rows), jnp.float32),
        jnp.zeros((kv_local, group_size, circle_rows, HEAD_DIM), jnp.float32),
    )
    top_score, weight_sum, weighted = lax.fori_loop(0, span_count, forward_turn, initial)
    log_total = top_score + jnp.log(weight_sum)
    attended = weighted / weight_sum[..., None]
    row_dots = jnp.sum(
        jnp.transpose(grad_heads, (1, 2, 0, 3)).astype(jnp.float32) * attended, axis=-1
    )

    def grads_for(query_grad, key_block, value_block, key_pos):
        scores_now = score_block(key_block, key_pos)
        probs = jnp.exp(scores_now - log_total[..., None])
        probs_low = probs.astype(jnp.bfloat16)
        value_part = jnp.einsum(
            "cgqk,qcgd->kcd", probs_low, grad_heads, preferred_element_type=jnp.float32
        )
        prob_grad = jnp.einsum(
            "qcgd,kcd->cgqk", grad_heads, value_block, preferred_element_type=jnp.float32
        )
        score_low = (probs * (prob_grad - row_dots[..., None])).astype(jnp.bfloat16)
        query_grad = query_grad + jnp.einsum(
            "cgqk,kcd->qcgd", score_low, key_block, preferred_element_type=jnp.float32
        )
        key_part = jnp.einsum(
            "cgqk,qcgd->kcd", score_low, query_heads, preferred_element_type=jnp.float32
        )
        return (query_grad, jnp.stack([key_part, value_part]))

    query_start = jnp.zeros((circle_rows, kv_local, group_size, HEAD_DIM), jnp.float32)

    def visit_block(query_grad, pair_now, grads_now, owner_rank):
        query_grad, block_grads = grads_for(
            query_grad, pair_now[0], pair_now[1], positions(owner_rank * circle_rows, circle_rows)
        )
        return (query_grad, grads_now + block_grads)

    grads_start = jnp.zeros((2, circle_rows, kv_local, HEAD_DIM), jnp.float32)

    def circle_turn(turn_index, state_in):
        query_grad, pair_now, grads_now = state_in
        query_grad, grads_now = visit_block(
            query_grad, pair_now, grads_now, (my_rank - turn_index) % circle_count
        )
        pair_now = from_behind(pair_now, ("inner", "outer"), 1)
        grads_now = from_behind(grads_now.astype(jnp.bfloat16), ("inner", "outer"), 1).astype(
            grads_now.dtype
        )
        return (query_grad, pair_now, grads_now)

    query_grad, pair_end, kv_grads = lax.fori_loop(
        0, circle_count, circle_turn, (query_start, kv_pair, grads_start)
    )
    query_low = (
        (query_grad * score_scale)
        .astype(jnp.bfloat16)
        .reshape(circle_rows, kv_local * group_size * HEAD_DIM)
    )
    key_low = (
        (kv_grads[0] * score_scale).astype(jnp.bfloat16).reshape(circle_rows, kv_local * HEAD_DIM)
    )
    value_low = kv_grads[1].astype(jnp.bfloat16).reshape(circle_rows, kv_local * HEAD_DIM)
    query_back, key_back, value_back = (
        lax.all_to_all(query_low, "head", split_axis=0, concat_axis=1, tiled=True),
        lax.all_to_all(key_low, "head", split_axis=0, concat_axis=1, tiled=True),
        lax.all_to_all(value_low, "head", split_axis=0, concat_axis=1, tiled=True),
    )
    return (query_back, key_back, value_back)


def solution(mesh):
    in_specs = (
        P(("head", "inner", "outer"), None),
        P(("head", "inner", "outer"), None),
        P(("head", "inner", "outer"), None),
        P(("head", "inner", "outer"), None),
        P(),
    )
    out_specs = (
        P(("head", "inner", "outer"), None),
        P(("head", "inner", "outer"), None),
        P(("head", "inner", "outer"), None),
    )
    return jax.shard_map(local, mesh=mesh, in_specs=in_specs, out_specs=out_specs, check_vma=False)
```

profile of v0, /device:TPU:0, one launch (start us, length us, event | category | flops | bytes accessed | tf_op | source)
XLA Modules:
  0.0 469.6 jit_solution(7612734399201189421)
XLA Ops:
  8.7 5.2 %all-to-all-start = ((bf16[64,4,128]{2,0,1:T(8,128)(2,1)}), bf16[64,4,128]{2,0,1:T(8,128)(2,1)S(1)}, u32[]{:S(2)}, u32[]{:S(2)}) async-start(bf16[64,4,128]{2,0,1:T(8,128)(2,1)} %copy_bitcast_fusion.5), calls=%async_computation | async-start | bytes 131072 | tf_op jit(solution)/shard_map/all_to_all | solution.py:26
  14.7 4.0 all-to-all-done
  18.7 7.2 %all_to_all.115 = bf16[64,4,128]{2,0,1:T(8,128)(2,1)S(1)} all-to-all(bf16[64,4,128]{2,0,1:T(8,128)(2,1)S(1)} %copy_bitcast_fusion.4), channel_id=1, replica_groups=mesh['head'=4,'inner'=4,'outer'=2] {'head'}, dimensions={1} | all-to-all | bytes 131072 | tf_op jit(solution)/shard_map/all_to_all | solution.py:27
  28.4 3.5 all-to-all-start.2
  33.8 4.7 all-to-all-done.2
  38.4 3.5 all-to-all-start.3
  43.4 19.8 %fusion.51 = s32[256]{0:T(256)S(1)} fusion(s32[]{:T(128)} %bitcast.35, s32[]{:T(128)} %bitcast.34, s32[]{:T(128)} %bitcast.33, s32[]{:T(128)} %bitcast.32, s32[]{:T(128)} %bitcast.31, s32[]{:T(128)} %bitcast.30, s32[]{:T(128)} %bitcast.29, s32[]{:T(128)} %bitcast.28, s32[]{:T(128)} %bitcast.27, s32[]{:T(128)} %bitcast.26, s32[]{:T(128)} %bitcast.25, ...), kind=kLoop, calls=%fused_computation.219 | loop fusion | flops 28672 | bytes 1156 | tf_op jit(solution)/shard_map/add | solution.py:53
  63.6 127.2 %while.42 = (s32[]{:T(128)}, f32[1,8,256]{2,1,0:T(8,128)S(1)}, f32[1,8,256]{2,1,0:T(8,128)S(1)}, f32[1,8,256,128]{3,2,1,0:T(8,128)}, s32[256]{0:T(256)S(1)}, /*i...) while((s32[]{:T(128)}, f32[1,8,256]{2,1,0:T(8,128)S(1)}, ...), condition=%wide.region_3.5_spmd.clone, body=%wide.region_0.4_spmd.clone.sunk | while | flops 549679104 | bytes 32934564 | solution.py:91
  64.3 4.4 compare_select_fusion.79
  70.2 15.6 %fusion.93 = s32[512]{0:T(512)S(1)} fusion(pred[512]{0:T(512)(128)(4,1)S(1)} %get-tuple-element.1062, pred[512]{0:T(512)(128)(4,1)S(1)} %get-tuple-element.1063, pred[512]{0:T(512)(128)(4,1)S(1)} %get-tuple-element.1064, pred[512]{0:T(512)(128)(4,1)S(1)} %get-tuple-element.1065, pred[512]{0:T(512)(128)(4,1)S(1)} %get-tuple-element.1066, ...), kind=kLoop, calls=%fused_computation.147.clone.1 | loop fusion | flops 38400 | bytes 17000 | tf_op jit(solution)/shard_map/while/body/eval_jaxpr/add | solution.py:53
  86.0 3.6 fusion.94
  89.6 4.7 fusion.97
  95.9 4.4 compare_select_fusion.79
  101.8 15.6 %fusion.93 = s32[512]{0:T(512)S(1)} fusion(pred[512]{0:T(512)(128)(4,1)S(1)} %get-tuple-element.1062, pred[512]{0:T(512)(128)(4,1)S(1)} %get-tuple-element.1063, pred[512]{0:T(512)(128)(4,1)S(1)} %get-tuple-element.1064, pred[512]{0:T(512)(128)(4,1)S(1)} %get-tuple-element.1065, pred[512]{0:T(512)(128)(4,1)S(1)} %get-tuple-element.1066, ...), kind=kLoop, calls=%fused_computation.147.clone.1 | loop fusion | flops 38400 | bytes 17000 | tf_op jit(solution)/shard_map/while/body/eval_jaxpr/add | solution.py:53
  117.5 3.6 fusion.94
  121.2 5.0 %fusion.97 = f32[1,8,256,128]{3,2,1,0:T(8,128)} fusion(f32[512,256,8]{1,0,2:T(8,128)} %get-tuple-element.1120, f32[8,256]{1,0:T(8,128)S(1)} %bitcast.480, pred[256,512]{0,1:T(8,128)(4,1)S(1)} %broadcast_compare_fusion.4, f32[1,8,256,128]{3,2,1,0:T(8,128)} %get-tuple-element.1181, f32[8,256]{1,0:T(8,128)S(1)} %get-tuple-element.1121, ...), kind=kOutput, calls=%fused_computation.81.clone.1 | convolution fusion | flops 273416192 | bytes 6569993 | tf_op jit(solution)/shard_map/while/body/eval_jaxpr/cgqk,kcd->cgqd/dot_general | solution.py:71
  127.8 4.4 compare_select_fusion.79
  133.7 15.6 %fusion.93 = s32[512]{0:T(512)S(1)} fusion(pred[512]{0:T(512)(128)(4,1)S(1)} %get-tuple-element.1062, pred[512]{0:T(512)(128)(4,1)S(1)} %get-tuple-element.1063, pred[512]{0:T(512)(128)(4,1)S(1)} %get-tuple-element.1064, pred[512]{0:T(512)(128)(4,1)S(1)} %get-tuple-element.1065, pred[512]{0:T(512)(128)(4,1)S(1)} %get-tuple-element.1066, ...), kind=kLoop, calls=%fused_computation.147.clone.1 | loop fusion | flops 38400 | bytes 17000 | tf_op jit(solution)/shard_map/while/body/eval_jaxpr/add | solution.py:53
  149.4 3.6 fusion.94
  153.0 5.0 %fusion.97 = f32[1,8,256,128]{3,2,1,0:T(8,128)} fusion(f32[512,256,8]{1,0,2:T(8,128)} %get-tuple-element.1120, f32[8,256]{1,0:T(8,128)S(1)} %bitcast.480, pred[256,512]{0,1:T(8,128)(4,1)S(1)} %broadcast_compare_fusion.4, f32[1,8,256,128]{3,2,1,0:T(8,128)} %get-tuple-element.1181, f32[8,256]{1,0:T(8,128)S(1)} %get-tuple-element.1121, ...), kind=kOutput, calls=%fused_computation.81.clone.1 | convolution fusion | flops 273416192 | bytes 6569993 | tf_op jit(solution)/shard_map/while/body/eval_jaxpr/cgqk,kcd->cgqd/dot_general | solution.py:71
  159.7 4.4 compare_select_fusion.79
  165.6 15.6 %fusion.93 = s32[512]{0:T(512)S(1)} fusion(pred[512]{0:T(512)(128)(4,1)S(1)} %get-tuple-element.1062, pred[512]{0:T(512)(128)(4,1)S(1)} %get-tuple-element.1063, pred[512]{0:T(512)(128)(4,1)S(1)} %get-tuple-element.1064, pred[512]{0:T(512)(128)(4,1)S(1)} %get-tuple-element.1065, pred[512]{0:T(512)(128)(4,1)S(1)} %get-tuple-element.1066, ...), kind=kLoop, calls=%fused_computation.147.clone.1 | loop fusion | flops 38400 | bytes 17000 | tf_op jit(solution)/shard_map/while/body/eval_jaxpr/add | solution.py:53
  181.3 3.6 fusion.94
  184.9 5.0 %fusion.97 = f32[1,8,256,128]{3,2,1,0:T(8,128)} fusion(f32[512,256,8]{1,0,2:T(8,128)} %get-tuple-element.1120, f32[8,256]{1,0:T(8,128)S(1)} %bitcast.480, pred[256,512]{0,1:T(8,128)(4,1)S(1)} %broadcast_compare_fusion.4, f32[1,8,256,128]{3,2,1,0:T(8,128)} %get-tuple-element.1181, f32[8,256]{1,0:T(8,128)S(1)} %get-tuple-element.1121, ...), kind=kOutput, calls=%fused_computation.81.clone.1 | convolution fusion | flops 273416192 | bytes 6569993 | tf_op jit(solution)/shard_map/while/body/eval_jaxpr/cgqk,kcd->cgqd/dot_general | solution.py:71
  191.0 2.2 fusion.49
  193.3 240.5 %while.43 = (s32[]{:T(128)}, f32[256,1,8,128]{3,0,2,1:T(8,128)S(1)}, bf16[2,256,1,128]{3,1,2,0:T(8,128)(2,1)S(1)}, f32[2,256,1,128]{3,1,2,0:T(8,128)S(1)}, s32[2...) while((s32[]{:T(128)}, ...), condition=%wide.region_6.8_spmd.clone, body=%wide.region_5.7_spmd.clone.sunk | while | flops 675704832 | bytes 16600825 | solution.py:138
  194.9 20.1 %fusion.110 = s32[256]{0:T(256)S(1)} fusion(s32[]{:T(128)} %bitcast.445, s32[]{:T(128)} %bitcast.446, s32[]{:T(128)} %bitcast.447, s32[]{:T(128)} %bitcast.448, s32[]{:T(128)} %bitcast.449, s32[]{:T(128)} %bitcast.450, s32[]{:T(128)} %bitcast.451, s32[]{:T(128)} %bitcast.452, s32[]{:T(128)} %bitcast.453, s32[]{:T(128)} %bitcast.454, s32[]{:T(128)} %bitcast.455, ...), kind=kLoop, calls=%fused_computation.70.clone.1 | loop fusion | flops 28672 | bytes 1156 | tf_op jit(solution)/shard_map/while/body/eval_jaxpr/add | solution.py:53
  219.7 3.7 collective-permute-done.1
  224.9 20.1 %fusion.110 = s32[256]{0:T(256)S(1)} fusion(s32[]{:T(128)} %bitcast.445, s32[]{:T(128)} %bitcast.446, s32[]{:T(128)} %bitcast.447, s32[]{:T(128)} %bitcast.448, s32[]{:T(128)} %bitcast.449, s32[]{:T(128)} %bitcast.450, s32[]{:T(128)} %bitcast.451, s32[]{:T(128)} %bitcast.452, s32[]{:T(128)} %bitcast.453, s32[]{:T(128)} %bitcast.454, s32[]{:T(128)} %bitcast.455, ...), kind=kLoop, calls=%fused_computation.70.clone.1 | loop fusion | flops 28672 | bytes 1156 | tf_op jit(solution)/shard_map/while/body/eval_jaxpr/add | solution.py:53
  248.1 5.3 %collective-permute-done.1 = bf16[2,256,1,128]{3,1,2,0:T(8,128)(2,1)S(1)} collective-permute-done((bf16[2,256,1,128]{3,1,2,0:T(8,128)(2,1)S(1)}, bf16[2,256,1,128]{3,1,2,0:T(8,128)(2,1)S(1)}, u32[]{:S(2)}, u32[]{:S(2)}) %collective-permute-start.1) | collective-permute-done | bytes 131104 | tf_op jit(solution)/shard_map/while/body/eval_jaxpr/ppermute | solution.py:16
  255.0 20.1 %fusion.110 = s32[256]{0:T(256)S(1)} fusion(s32[]{:T(128)} %bitcast.445, s32[]{:T(128)} %bitcast.446, s32[]{:T(128)} %bitcast.447, s32[]{:T(128)} %bitcast.448, s32[]{:T(128)} %bitcast.449, s32[]{:T(128)} %bitcast.450, s32[]{:T(128)} %bitcast.451, s32[]{:T(128)} %bitcast.452, s32[]{:T(128)} %bitcast.453, s32[]{:T(128)} %bitcast.454, s32[]{:T(128)} %bitcast.455, ...), kind=kLoop, calls=%fused_computation.70.clone.1 | loop fusion | flops 28672 | bytes 1156 | tf_op jit(solution)/shard_map/while/body/eval_jaxpr/add | solution.py:53
  278.1 5.3 %collective-permute-done.1 = bf16[2,256,1,128]{3,1,2,0:T(8,128)(2,1)S(1)} collective-permute-done((bf16[2,256,1,128]{3,1,2,0:T(8,128)(2,1)S(1)}, bf16[2,256,1,128]{3,1,2,0:T(8,128)(2,1)S(1)}, u32[]{:S(2)}, u32[]{:S(2)}) %collective-permute-start.1) | collective-permute-done | bytes 131104 | tf_op jit(solution)/shard_map/while/body/eval_jaxpr/ppermute | solution.py:16
  285.1 20.1 %fusion.110 = s32[256]{0:T(256)S(1)} fusion(s32[]{:T(128)} %bitcast.445, s32[]{:T(128)} %bitcast.446, s32[]{:T(128)} %bitcast.447, s32[]{:T(128)} %bitcast.448, s32[]{:T(128)} %bitcast.449, s32[]{:T(128)} %bitcast.450, s32[]{:T(128)} %bitcast.451, s32[]{:T(128)} %bitcast.452, s32[]{:T(128)} %bitcast.453, s32[]{:T(128)} %bitcast.454, s32[]{:T(128)} %bitcast.455, ...), kind=kLoop, calls=%fused_computation.70.clone.1 | loop fusion | flops 28672 | bytes 1156 | tf_op jit(solution)/shard_map/while/body/eval_jaxpr/add | solution.py:53
  308.2 5.3 %collective-permute-done.1 = bf16[2,256,1,128]{3,1,2,0:T(8,128)(2,1)S(1)} collective-permute-done((bf16[2,256,1,128]{3,1,2,0:T(8,128)(2,1)S(1)}, bf16[2,256,1,128]{3,1,2,0:T(8,128)(2,1)S(1)}, u32[]{:S(2)}, u32[]{:S(2)}) %collective-permute-start.1) | collective-permute-done | bytes 131104 | tf_op jit(solution)/shard_map/while/body/eval_jaxpr/ppermute | solution.py:16
  315.1 20.1 %fusion.110 = s32[256]{0:T(256)S(1)} fusion(s32[]{:T(128)} %bitcast.445, s32[]{:T(128)} %bitcast.446, s32[]{:T(128)} %bitcast.447, s32[]{:T(128)} %bitcast.448, s32[]{:T(128)} %bitcast.449, s32[]{:T(128)} %bitcast.450, s32[]{:T(128)} %bitcast.451, s32[]{:T(128)} %bitcast.452, s32[]{:T(128)} %bitcast.453, s32[]{:T(128)} %bitcast.454, s32[]{:T(128)} %bitcast.455, ...), kind=kLoop, calls=%fused_computation.70.clone.1 | loop fusion | flops 28672 | bytes 1156 | tf_op jit(solution)/shard_map/while/body/eval_jaxpr/add | solution.py:53
  338.3 5.3 %collective-permute-done.1 = bf16[2,256,1,128]{3,1,2,0:T(8,128)(2,1)S(1)} collective-permute-done((bf16[2,256,1,128]{3,1,2,0:T(8,128)(2,1)S(1)}, bf16[2,256,1,128]{3,1,2,0:T(8,128)(2,1)S(1)}, u32[]{:S(2)}, u32[]{:S(2)}) %collective-permute-start.1) | collective-permute-done | bytes 131104 | tf_op jit(solution)/shard_map/while/body/eval_jaxpr/ppermute | solution.py:16
  345.2 20.1 %fusion.110 = s32[256]{0:T(256)S(1)} fusion(s32[]{:T(128)} %bitcast.445, s32[]{:T(128)} %bitcast.446, s32[]{:T(128)} %bitcast.447, s32[]{:T(128)} %bitcast.448, s32[]{:T(128)} %bitcast.449, s32[]{:T(128)} %bitcast.450, s32[]{:T(128)} %bitcast.451, s32[]{:T(128)} %bitcast.452, s32[]{:T(128)} %bitcast.453, s32[]{:T(128)} %bitcast.454, s32[]{:T(128)} %bitcast.455, ...), kind=kLoop, calls=%fused_computation.70.clone.1 | loop fusion | flops 28672 | bytes 1156 | tf_op jit(solution)/shard_map/while/body/eval_jaxpr/add | solution.py:53
  368.3 5.3 %collective-permute-done.1 = bf16[2,256,1,128]{3,1,2,0:T(8,128)(2,1)S(1)} collective-permute-done((bf16[2,256,1,128]{3,1,2,0:T(8,128)(2,1)S(1)}, bf16[2,256,1,128]{3,1,2,0:T(8,128)(2,1)S(1)}, u32[]{:S(2)}, u32[]{:S(2)}) %collective-permute-start.1) | collective-permute-done | bytes 131104 | tf_op jit(solution)/shard_map/while/body/eval_jaxpr/ppermute | solution.py:16
  375.2 20.1 %fusion.110 = s32[256]{0:T(256)S(1)} fusion(s32[]{:T(128)} %bitcast.445, s32[]{:T(128)} %bitcast.446, s32[]{:T(128)} %bitcast.447, s32[]{:T(128)} %bitcast.448, s32[]{:T(128)} %bitcast.449, s32[]{:T(128)} %bitcast.450, s32[]{:T(128)} %bitcast.451, s32[]{:T(128)} %bitcast.452, s32[]{:T(128)} %bitcast.453, s32[]{:T(128)} %bitcast.454, s32[]{:T(128)} %bitcast.455, ...), kind=kLoop, calls=%fused_computation.70.clone.1 | loop fusion | flops 28672 | bytes 1156 | tf_op jit(solution)/shard_map/while/body/eval_jaxpr/add | solution.py:53
  398.4 5.3 %collective-permute-done.1 = bf16[2,256,1,128]{3,1,2,0:T(8,128)(2,1)S(1)} collective-permute-done((bf16[2,256,1,128]{3,1,2,0:T(8,128)(2,1)S(1)}, bf16[2,256,1,128]{3,1,2,0:T(8,128)(2,1)S(1)}, u32[]{:S(2)}, u32[]{:S(2)}) %collective-permute-start.1) | collective-permute-done | bytes 131104 | tf_op jit(solution)/shard_map/while/body/eval_jaxpr/ppermute | solution.py:16
  405.3 20.1 %fusion.110 = s32[256]{0:T(256)S(1)} fusion(s32[]{:T(128)} %bitcast.445, s32[]{:T(128)} %bitcast.446, s32[]{:T(128)} %bitcast.447, s32[]{:T(128)} %bitcast.448, s32[]{:T(128)} %bitcast.449, s32[]{:T(128)} %bitcast.450, s32[]{:T(128)} %bitcast.451, s32[]{:T(128)} %bitcast.452, s32[]{:T(128)} %bitcast.453, s32[]{:T(128)} %bitcast.454, s32[]{:T(128)} %bitcast.455, ...), kind=kLoop, calls=%fused_computation.70.clone.1 | loop fusion | flops 28672 | bytes 1156 | tf_op jit(solution)/shard_map/while/body/eval_jaxpr/add | solution.py:53
  428.5 5.3 %collective-permute-done.1 = bf16[2,256,1,128]{3,1,2,0:T(8,128)(2,1)S(1)} collective-permute-done((bf16[2,256,1,128]{3,1,2,0:T(8,128)(2,1)S(1)}, bf16[2,256,1,128]{3,1,2,0:T(8,128)(2,1)S(1)}, u32[]{:S(2)}, u32[]{:S(2)}) %collective-permute-start.1) | collective-permute-done | bytes 131104 | tf_op jit(solution)/shard_map/while/body/eval_jaxpr/ppermute | solution.py:16
  434.4 4.1 all-to-all-start.6
  439.2 4.3 all-to-all-done.6
  443.5 3.3 all-to-all-start.5
  448.3 3.6 all-to-all-done.5
  451.9 3.5 all-to-all-start.4
  456.6 5.3 %all-to-all-done.4 = bf16[4,64,1024]{2,1,0:T(8,128)(2,1)S(1)} async-done(((bf16[4,64,1024]{2,1,0:T(8,128)(2,1)}), bf16[4,64,1024]{2,1,0:T(8,128)(2,1)S(1)}, u32[]{:S(2)}, u32[]{:S(2)}) %all-to-all-start.4) | async-done | bytes 524320 | tf_op jit(solution)/shard_map/all_to_all | solution.py:151
  (237 shorter events, 64.3 us)
Async XLA Ops:
  7.2 0.8 copy-start
  8.0 34.0 %copy-start.2 = (s32[32]{0:T(128)S(1)}, s32[32]{0:T(128)}, u32[]{:S(2)}) copy-start(s32[32]{0:T(128)} %param.15) | copy-start | bytes 388
  8.7 10.0 %all-to-all-start = ((bf16[64,4,128]{2,0,1:T(8,128)(2,1)}), bf16[64,4,128]{2,0,1:T(8,128)(2,1)S(1)}, u32[]{:S(2)}, u32[]{:S(2)}) async-start(bf16[64,4,128]{2,0,1:T(8,128)(2,1)} %copy_bitcast_fusion.5), calls=%async_computation | async-start | bytes 131072 | tf_op jit(solution)/shard_map/all_to_all | solution.py:26
  13.8 49.8 %all-gather.2.cloned.1.call-start = ((), (), s32[]{:S(2)}) async-start(), calls=%async_computation.7 | async-start | bytes 1179648 | tf_op jit(solution)/shard_map/all_gather | solution.py:79
  28.4 10.0 %all-to-all-start.2 = ((bf16[64,4,1024]{2,0,1:T(8,128)(2,1)}), bf16[64,4,1024]{2,0,1:T(8,128)(2,1)S(1)}, u32[]{:S(2)}, u32[]{:S(2)}) async-start(bf16[64,4,1024]{2,0,1:T(8,128)(2,1)} %bitcast.289), calls=%async_computation.2 | async-start | bytes 1048576 | tf_op jit(solution)/shard_map/all_to_all | solution.py:25
  38.4 24.9 %all-to-all-start.3 = ((bf16[64,4,1024]{2,0,1:T(8,128)(2,1)}), bf16[64,4,1024]{2,0,1:T(8,128)(2,1)S(1)}, u32[]{:S(2)}, u32[]{:S(2)}) async-start(bf16[64,4,1024]{2,0,1:T(8,128)(2,1)} %bitcast.288), calls=%async_computation.3 | async-start | bytes 1048576 | tf_op jit(solution)/shard_map/all_to_all | solution.py:28
  63.6 129.7 %copy-start.3 = (bf16[2,256,1,128]{3,1,2,0:T(8,128)(2,1)S(1)}, bf16[2,256,1,128]{3,1,2,0:T(8,128)(2,1)}, u32[]{:S(2)}) copy-start(bf16[2,256,1,128]{3,1,2,0:T(8,128)(2,1)} %pad_maximum_fusion) | copy-start | bytes 393220
  89.6 4.7 copy-start.1
  121.2 5.0 %copy-start.1 = (f32[512,256,8]{1,0,2:T(8,128)S(1)}, f32[512,256,8]{1,0,2:T(8,128)}, u32[]{:S(2)}) copy-start(f32[512,256,8]{1,0,2:T(8,128)} %get-tuple-element.1120) | copy-start | bytes 12582916 | tf_op jit(solution)/shard_map/while
  153.0 5.0 %copy-start.1 = (f32[512,256,8]{1,0,2:T(8,128)S(1)}, f32[512,256,8]{1,0,2:T(8,128)}, u32[]{:S(2)}) copy-start(f32[512,256,8]{1,0,2:T(8,128)} %get-tuple-element.1120) | copy-start | bytes 12582916 | tf_op jit(solution)/shard_map/while
  184.9 5.0 %copy-start.1 = (f32[512,256,8]{1,0,2:T(8,128)S(1)}, f32[512,256,8]{1,0,2:T(8,128)}, u32[]{:S(2)}) copy-start(f32[512,256,8]{1,0,2:T(8,128)} %get-tuple-element.1120) | copy-start | bytes 12582916 | tf_op jit(solution)/shard_map/while
  193.3 30.0 %collective-permute-start = (bf16[2,256,1,128]{3,1,2,0:T(8,128)(2,1)S(1)}, bf16[2,256,1,128]{3,1,2,0:T(8,128)(2,1)S(1)}, u32[]{:S(2)}, u32[]{:S(2)}) collective-permute-start(bf16[2,256,1,128]{3,1,2,0:T(8,128)(2,1)S(1)} %copy.113), channel_id=1, source_target_pairs={{0,1},{1,2},{2,3},{3,4},{4,5},{5,6},{6,7},{7,0},{8,9},{9,10},{10,1... | collective-permute-start | bytes 393224 | tf_op jit(solution)/shard_map/while/body/eval_jaxpr/ppermute | solution.py:16
  217.1 6.2 %collective-permute-start.1 = (bf16[2,256,1,128]{3,1,2,0:T(8,128)(2,1)S(1)}, bf16[2,256,1,128]{3,1,2,0:T(8,128)(2,1)S(1)}, u32[]{:S(2)}, u32[]{:S(2)}) collective-permute-start(bf16[2,256,1,128]{3,1,2,0:T(8,128)(2,1)S(1)} %fusion.114), channel_id=1, source_target_pairs={{0,1},{1,2},{2,3},{3,4},{4,5},{5,6},{6,7},{7,0},{8,9},{9,10},{10,1... | collective-permute-start | bytes 393224 | tf_op jit(solution)/shard_map/while/body/eval_jaxpr/ppermute | solution.py:16
  223.4 30.0 %collective-permute-start = (bf16[2,256,1,128]{3,1,2,0:T(8,128)(2,1)S(1)}, bf16[2,256,1,128]{3,1,2,0:T(8,128)(2,1)S(1)}, u32[]{:S(2)}, u32[]{:S(2)}) collective-permute-start(bf16[2,256,1,128]{3,1,2,0:T(8,128)(2,1)S(1)} %copy.113), channel_id=1, source_target_pairs={{0,1},{1,2},{2,3},{3,4},{4,5},{5,6},{6,7},{7,0},{8,9},{9,10},{10,1... | collective-permute-start | bytes 393224 | tf_op jit(solution)/shard_map/while/body/eval_jaxpr/ppermute | solution.py:16
  247.1 6.2 %collective-permute-start.1 = (bf16[2,256,1,128]{3,1,2,0:T(8,128)(2,1)S(1)}, bf16[2,256,1,128]{3,1,2,0:T(8,128)(2,1)S(1)}, u32[]{:S(2)}, u32[]{:S(2)}) collective-permute-start(bf16[2,256,1,128]{3,1,2,0:T(8,128)(2,1)S(1)} %fusion.114), channel_id=1, source_target_pairs={{0,1},{1,2},{2,3},{3,4},{4,5},{5,6},{6,7},{7,0},{8,9},{9,10},{10,1... | collective-permute-start | bytes 393224 | tf_op jit(solution)/shard_map/while/body/eval_jaxpr/ppermute | solution.py:16
  253.4 30.0 %collective-permute-start = (bf16[2,256,1,128]{3,1,2,0:T(8,128)(2,1)S(1)}, bf16[2,256,1,128]{3,1,2,0:T(8,128)(2,1)S(1)}, u32[]{:S(2)}, u32[]{:S(2)}) collective-permute-start(bf16[2,256,1,128]{3,1,2,0:T(8,128)(2,1)S(1)} %copy.113), channel_id=1, source_target_pairs={{0,1},{1,2},{2,3},{3,4},{4,5},{5,6},{6,7},{7,0},{8,9},{9,10},{10,1... | collective-permute-start | bytes 393224 | tf_op jit(solution)/shard_map/while/body/eval_jaxpr/ppermute | solution.py:16
  277.2 6.2 %collective-permute-start.1 = (bf16[2,256,1,128]{3,1,2,0:T(8,128)(2,1)S(1)}, bf16[2,256,1,128]{3,1,2,0:T(8,128)(2,1)S(1)}, u32[]{:S(2)}, u32[]{:S(2)}) collective-permute-start(bf16[2,256,1,128]{3,1,2,0:T(8,128)(2,1)S(1)} %fusion.114), channel_id=1, source_target_pairs={{0,1},{1,2},{2,3},{3,4},{4,5},{5,6},{6,7},{7,0},{8,9},{9,10},{10,1... | collective-permute-start | bytes 393224 | tf_op jit(solution)/shard_map/while/body/eval_jaxpr/ppermute | solution.py:16
  283.5 30.0 %collective-permute-start = (bf16[2,256,1,128]{3,1,2,0:T(8,128)(2,1)S(1)}, bf16[2,256,1,128]{3,1,2,0:T(8,128)(2,1)S(1)}, u32[]{:S(2)}, u32[]{:S(2)}) collective-permute-start(bf16[2,256,1,128]{3,1,2,0:T(8,128)(2,1)S(1)} %copy.113), channel_id=1, source_target_pairs={{0,1},{1,2},{2,3},{3,4},{4,5},{5,6},{6,7},{7,0},{8,9},{9,10},{10,1... | collective-permute-start | bytes 393224 | tf_op jit(solution)/shard_map/while/body/eval_jaxpr/ppermute | solution.py:16
  307.3 6.2 %collective-permute-start.1 = (bf16[2,256,1,128]{3,1,2,0:T(8,128)(2,1)S(1)}, bf16[2,256,1,128]{3,1,2,0:T(8,128)(2,1)S(1)}, u32[]{:S(2)}, u32[]{:S(2)}) collective-permute-start(bf16[2,256,1,128]{3,1,2,0:T(8,128)(2,1)S(1)} %fusion.114), channel_id=1, source_target_pairs={{0,1},{1,2},{2,3},{3,4},{4,5},{5,6},{6,7},{7,0},{8,9},{9,10},{10,1... | collective-permute-start | bytes 393224 | tf_op jit(solution)/shard_map/while/body/eval_jaxpr/ppermute | solution.py:16
  313.6 30.0 %collective-permute-start = (bf16[2,256,1,128]{3,1,2,0:T(8,128)(2,1)S(1)}, bf16[2,256,1,128]{3,1,2,0:T(8,128)(2,1)S(1)}, u32[]{:S(2)}, u32[]{:S(2)}) collective-permute-start(bf16[2,256,1,128]{3,1,2,0:T(8,128)(2,1)S(1)} %copy.113), channel_id=1, source_target_pairs={{0,1},{1,2},{2,3},{3,4},{4,5},{5,6},{6,7},{7,0},{8,9},{9,10},{10,1... | collective-permute-start | bytes 393224 | tf_op jit(solution)/shard_map/while/body/eval_jaxpr/ppermute | solution.py:16
  337.3 6.2 %collective-permute-start.1 = (bf16[2,256,1,128]{3,1,2,0:T(8,128)(2,1)S(1)}, bf16[2,256,1,128]{3,1,2,0:T(8,128)(2,1)S(1)}, u32[]{:S(2)}, u32[]{:S(2)}) collective-permute-start(bf16[2,256,1,128]{3,1,2,0:T(8,128)(2,1)S(1)} %fusion.114), channel_id=1, source_target_pairs={{0,1},{1,2},{2,3},{3,4},{4,5},{5,6},{6,7},{7,0},{8,9},{9,10},{10,1... | collective-permute-start | bytes 393224 | tf_op jit(solution)/shard_map/while/body/eval_jaxpr/ppermute | solution.py:16
  343.6 30.0 %collective-permute-start = (bf16[2,256,1,128]{3,1,2,0:T(8,128)(2,1)S(1)}, bf16[2,256,1,128]{3,1,2,0:T(8,128)(2,1)S(1)}, u32[]{:S(2)}, u32[]{:S(2)}) collective-permute-start(bf16[2,256,1,128]{3,1,2,0:T(8,128)(2,1)S(1)} %copy.113), channel_id=1, source_target_pairs={{0,1},{1,2},{2,3},{3,4},{4,5},{5,6},{6,7},{7,0},{8,9},{9,10},{10,1... | collective-permute-start | bytes 393224 | tf_op jit(solution)/shard_map/while/body/eval_jaxpr/ppermute | solution.py:16
  367.4 6.2 %collective-permute-start.1 = (bf16[2,256,1,128]{3,1,2,0:T(8,128)(2,1)S(1)}, bf16[2,256,1,128]{3,1,2,0:T(8,128)(2,1)S(1)}, u32[]{:S(2)}, u32[]{:S(2)}) collective-permute-start(bf16[2,256,1,128]{3,1,2,0:T(8,128)(2,1)S(1)} %fusion.114), channel_id=1, source_target_pairs={{0,1},{1,2},{2,3},{3,4},{4,5},{5,6},{6,7},{7,0},{8,9},{9,10},{10,1... | collective-permute-start | bytes 393224 | tf_op jit(solution)/shard_map/while/body/eval_jaxpr/ppermute | solution.py:16
  373.7 30.0 %collective-permute-start = (bf16[2,256,1,128]{3,1,2,0:T(8,128)(2,1)S(1)}, bf16[2,256,1,128]{3,1,2,0:T(8,128)(2,1)S(1)}, u32[]{:S(2)}, u32[]{:S(2)}) collective-permute-start(bf16[2,256,1,128]{3,1,2,0:T(8,128)(2,1)S(1)} %copy.113), channel_id=1, source_target_pairs={{0,1},{1,2},{2,3},{3,4},{4,5},{5,6},{6,7},{7,0},{8,9},{9,10},{10,1... | collective-permute-start | bytes 393224 | tf_op jit(solution)/shard_map/while/body/eval_jaxpr/ppermute | solution.py:16
  397.4 6.2 %collective-permute-start.1 = (bf16[2,256,1,128]{3,1,2,0:T(8,128)(2,1)S(1)}, bf16[2,256,1,128]{3,1,2,0:T(8,128)(2,1)S(1)}, u32[]{:S(2)}, u32[]{:S(2)}) collective-permute-start(bf16[2,256,1,128]{3,1,2,0:T(8,128)(2,1)S(1)} %fusion.114), channel_id=1, source_target_pairs={{0,1},{1,2},{2,3},{3,4},{4,5},{5,6},{6,7},{7,0},{8,9},{9,10},{10,1... | collective-permute-start | bytes 393224 | tf_op jit(solution)/shard_map/while/body/eval_jaxpr/ppermute | solution.py:16
  403.8 30.0 %collective-permute-start = (bf16[2,256,1,128]{3,1,2,0:T(8,128)(2,1)S(1)}, bf16[2,256,1,128]{3,1,2,0:T(8,128)(2,1)S(1)}, u32[]{:S(2)}, u32[]{:S(2)}) collective-permute-start(bf16[2,256,1,128]{3,1,2,0:T(8,128)(2,1)S(1)} %copy.113), channel_id=1, source_target_pairs={{0,1},{1,2},{2,3},{3,4},{4,5},{5,6},{6,7},{7,0},{8,9},{9,10},{10,1... | collective-permute-start | bytes 393224 | tf_op jit(solution)/shard_map/while/body/eval_jaxpr/ppermute | solution.py:16
  427.5 6.2 %collective-permute-start.1 = (bf16[2,256,1,128]{3,1,2,0:T(8,128)(2,1)S(1)}, bf16[2,256,1,128]{3,1,2,0:T(8,128)(2,1)S(1)}, u32[]{:S(2)}, u32[]{:S(2)}) collective-permute-start(bf16[2,256,1,128]{3,1,2,0:T(8,128)(2,1)S(1)} %fusion.114), channel_id=1, source_target_pairs={{0,1},{1,2},{2,3},{3,4},{4,5},{5,6},{6,7},{7,0},{8,9},{9,10},{10,1... | collective-permute-start | bytes 393224 | tf_op jit(solution)/shard_map/while/body/eval_jaxpr/ppermute | solution.py:16
  434.4 9.1 %all-to-all-start.6 = ((bf16[4,64,128]{2,1,0:T(8,128)(2,1)}), bf16[4,64,128]{2,1,0:T(8,128)(2,1)S(1)}, u32[]{:S(2)}, u32[]{:S(2)}) async-start(bf16[4,64,128]{2,1,0:T(8,128)(2,1)} %bitcast.44), calls=%async_computation.6 | async-start | bytes 131072 | tf_op jit(solution)/shard_map/all_to_all | solution.py:153
  443.5 8.4 %all-to-all-start.5 = ((bf16[4,64,128]{2,1,0:T(8,128)(2,1)}), bf16[4,64,128]{2,1,0:T(8,128)(2,1)S(1)}, u32[]{:S(2)}, u32[]{:S(2)}) async-start(bf16[4,64,128]{2,1,0:T(8,128)(2,1)} %bitcast.42), calls=%async_computation.5 | async-start | bytes 131072 | tf_op jit(solution)/shard_map/all_to_all | solution.py:152
  451.9 10.0 %all-to-all-start.4 = ((bf16[4,64,1024]{2,1,0:T(8,128)(2,1)}), bf16[4,64,1024]{2,1,0:T(8,128)(2,1)S(1)}, u32[]{:S(2)}, u32[]{:S(2)}) async-start(bf16[4,64,1024]{2,1,0:T(8,128)(2,1)} %all_to_all.98), calls=%async_computation.4 | async-start | bytes 1048576 | tf_op jit(solution)/shard_map/all_to_all | solution.py:151
Sparse Core Ops, SparseCore 0:
  26.7 21.7 all-gather.1
where the time goes:
time: 474 us; the launch traced here: 470 us
  other arithmetic  273 us (58%)
  waiting for transfers between devices  62.7 us (13%)
  matrix products  56.4 us (12%)
  local copies, waits for them, and re-layouts  29.6 us (6%)
  starting transfers between devices  25.5 us (5%)
  between operations  14.2 us (3%)
  blocking collectives  7.2 us (2%)
    add x13, other arithmetic, positions(): jnp.take(block_order, stored_block) * block_rows + local_row % block_rows  243 us
    ppermute x16, waiting for transfers between devices, from_behind(): lax.ppermute(array, axis, [(i, (i + by) % length) for i in range(length)])  40.8 us
    gather x56, other arithmetic, positions(): jnp.take(block_order, stored_block) * block_rows + local_row % block_rows  20.6 us
    dot_general x4, matrix products, forward_fold(): jnp.einsum('cgqk,kcd->cgqd', probs.astype(jnp.bfloat16), segment[1], pref...  19.6 us
    dot_general x12, matrix products, score_block(): jnp.einsum('qcgd,kcd->cgqk', query_heads, key_block, preferred_element_ty...  19.3 us
    gather x26, local copies, waits for them, and re-layouts, positions(): jnp.take(block_order, stored_block) * block_rows + local_row % block_rows  18.7 us
  transfers between devices with their start and end apart: 23, of which 13 were waited for; matrix products, arithmetic and copies ran while one was open for 48% of the time, Pallas kernels for 0%

commit v1 on v0

v1 whole, which is shorter than its diff:
```python
import functools

import jax
import jax.numpy as jnp
from jax import lax
from jax.experimental import pallas as pl
from jax.experimental.pallas import tpu as pltpu
from jax.sharding import PartitionSpec as P

HEADS = 32
KV_HEADS = 4
HEAD_DIM = 128
GROUP = HEADS // KV_HEADS
SCALE = HEAD_DIM ** (-0.5)
LOG2E = 1.4426950408889634
masked_score = -1e30
VMEM_LIMIT = 60 * 1024 * 1024

NT = (((1,), (1,)), ((), ()))
NN = (((1,), (0,)), ((), ()))


def dot(a, b, dims):
    return lax.dot_general(a, b, dims, preferred_element_type=jnp.float32)


def exchange(array, axis, by):
    length = lax.axis_size(axis)
    return lax.ppermute(array, axis, [(i, i ^ by) for i in range(length)])


def call(body, outs, args, in_spaces, out_space, scratch=()):
    return pl.pallas_call(
        body,
        out_shape=outs,
        in_specs=[pl.BlockSpec(memory_space=s) for s in in_spaces],
        out_specs=[pl.BlockSpec(memory_space=out_space) for _ in outs],
        scratch_shapes=list(scratch),
        compiler_params=pltpu.CompilerParams(vmem_limit_bytes=VMEM_LIMIT),
    )(*args)


def pack_kv(heads, keys_ref, values_ref, *outs):
    me = lax.axis_index("head")
    for i in range(heads):
        columns = pl.ds(pl.multiple_of((me ^ i) * HEAD_DIM, HEAD_DIM), HEAD_DIM)
        outs[i][:, :HEAD_DIM] = keys_ref[:, columns]
        outs[i][:, HEAD_DIM:] = values_ref[:, columns]


def pack_rows(heads, rows_ref, *refs):
    outs, sem = refs[:-1], refs[-1]
    me = lax.axis_index("head")
    width = rows_ref.shape[1] // heads
    copies = []
    for i in range(1, heads):
        columns = pl.ds(pl.multiple_of((me ^ i) * width, width), width)
        copies.append(pltpu.make_async_copy(rows_ref.at[:, columns], outs[i - 1], sem.at[i - 1]))
    for copy in copies:
        copy.start()
    for copy in copies:
        copy.wait()


def join_kv(*refs):
    out = refs[-1]
    me = lax.axis_index("head")
    rows = refs[0].shape[0]
    for i, ref in enumerate(refs[:-1]):
        out[pl.ds(pl.multiple_of((me ^ i) * rows, rows), rows), :] = ref[...]


def main_body(heads, inner, outer, rows_now, order_ref, *refs):
    it = iter(refs)
    q_full = next(it)
    g_full = next(it)
    q_got = [next(it) for _ in range(heads - 1)]
    g_got = [next(it) for _ in range(heads - 1)]
    bundles = [[next(it) for _ in range(inner)] for _ in range(outer)]
    dq_outs = [next(it) for _ in range(heads)]
    same_out = next(it)
    other_outs = [next(it) for _ in range(outer - 1)]
    keys, values, queries, grads, key_t, s_ref, p_ref, dk_ref, dv_ref, dq_ref = it

    block = q_full.shape[0]
    ranks = inner * outer
    chunk = ranks * block
    width = GROUP * HEAD_DIM
    me = lax.axis_index("head")
    z = lax.axis_index("inner")
    o = lax.axis_index("outer")
    rank = z * outer + o

    for e in range(outer):
        for s in range(inner):
            other = (z ^ s) * outer + (o ^ e)
            for a in range(heads):
                at = pl.ds(pl.multiple_of(order_ref[a * ranks + other] * block, block), block)
                keys[at, :] = bundles[e][s][a * block : (a + 1) * block, :HEAD_DIM]
                values[at, :] = bundles[e][s][a * block : (a + 1) * block, HEAD_DIM:]

    place = [order_ref[(me ^ i) * ranks + rank] for i in range(heads)]
    level_of = [p // ranks for p in place]
    for i in range(heads):
        for g in range(GROUP):
            rows = slice(g * block, (g + 1) * block)
            if i == 0:
                cols = pl.ds(pl.multiple_of(me * width + g * HEAD_DIM, HEAD_DIM), HEAD_DIM)
                queries[level_of[0], rows, :] = q_full[:, cols]
                grads[level_of[0], rows, :] = g_full[:, cols]
            else:
                cols = slice(g * HEAD_DIM, (g + 1) * HEAD_DIM)
                queries[level_of[i], rows, :] = q_got[i - 1][:, cols]
                grads[level_of[i], rows, :] = g_got[i - 1][:, cols]

    for c in range(heads):
        key_t[:, c * chunk : (c + 1) * chunk] = keys[c * chunk : (c + 1) * chunk, :].T

    all_rows = GROUP * block
    for level in reversed(range(heads)):
        position = sum(jnp.where(level_of[i] == level, place[i], 0) for i in range(heads))
        shift = position * block - level * chunk
        for r in range(0, all_rows, rows_now):
            q = queries[level, r : r + rows_now, :]
            g = grads[level, r : r + rows_now, :]
            top = None
            for c in range(level + 1):
                span = slice(c * chunk, (c + 1) * chunk)
                s = dot(keys[span, :], q, NT)
                if c == level:
                    u = lax.broadcasted_iota(jnp.int32, s.shape, 0)
                    t = lax.broadcasted_iota(jnp.int32, s.shape, 1) % block
                    s = jnp.where(u <= t + shift, s, masked_score)
                s_ref[span, :] = s
                now = jnp.max(s, axis=0, keepdims=True)
                top = now if top is None else jnp.maximum(top, now)
            total = None
            for c in range(level + 1):
                span = slice(c * chunk, (c + 1) * chunk)
                e = jnp.exp2((s_ref[span, :] - top) * (SCALE * LOG2E))
                s_ref[span, :] = e
                now = jnp.sum(e, axis=0, keepdims=True)
                total = now if total is None else total + now
            inverse = 1.0 / total
            dots = None
            for c in range(level + 1):
                span = slice(c * chunk, (c + 1) * chunk)
                p = s_ref[span, :] * inverse
                s_ref[span, :] = p
                low = p.astype(jnp.bfloat16)
                part = dot(low, g, NN)
                if level == heads - 1 and r == 0:
                    dv_ref[span, :] = part
                else:
                    dv_ref[span, :] += part
                dp = dot(values[span, :], g, NT)
                p_ref[span, :] = dp
                now = jnp.sum(low.astype(jnp.float32) * dp, axis=0, keepdims=True)
                dots = now if dots is None else dots + now
            dq = None
            for c in range(level + 1):
                span = slice(c * chunk, (c + 1) * chunk)
                ds = (s_ref[span, :] * (p_ref[span, :] - dots)).astype(jnp.bfloat16)
                part = dot(ds, q, NN)
                if level == heads - 1 and r == 0:
                    dk_ref[span, :] = part
                else:
                    dk_ref[span, :] += part
                part = dot(key_t[:, span], ds, NN)
                dq = part if dq is None else dq + part
            dq_ref[level, r : r + rows_now, :] = (dq * SCALE).T.astype(jnp.bfloat16)

    for i in range(heads):
        for g in range(GROUP):
            dq_outs[i][:, g * HEAD_DIM : (g + 1) * HEAD_DIM] = dq_ref[
                level_of[i], g * block : (g + 1) * block, :
            ]
    for e in range(outer):
        out = same_out if e == 0 else other_outs[e - 1]
        for s in range(inner):
            other = (z ^ s) * outer + (o ^ e)
            for a in range(heads):
                at = pl.ds(pl.multiple_of(order_ref[a * ranks + other] * block, block), block)
                rows = slice((s * heads + a) * block, (s * heads + a + 1) * block)
                out[rows, :HEAD_DIM] = dk_ref[at, :].astype(out.dtype)
                out[rows, HEAD_DIM:] = dv_ref[at, :].astype(out.dtype)


def sum_cores(parts, *refs):
    ins, outs = refs[:parts], refs[parts:]
    rows = outs[0].shape[0]
    for s, out in enumerate(outs):
        span = slice(s * rows, (s + 1) * rows)
        total = ins[0][span, :].astype(jnp.float32)
        for ref in ins[1:]:
            total = total + ref[span, :].astype(jnp.float32)
        out[...] = total.astype(out.dtype)


def sum_inner(parts, *refs):
    ins, outs = refs[:parts], refs[parts:]
    me = lax.axis_index("head")
    rows = outs[0].shape[0]
    for i, out in enumerate(outs):
        at = pl.ds(pl.multiple_of((me ^ i) * rows, rows), rows)
        total = ins[0][at, :].astype(jnp.float32)
        for ref in ins[1:]:
            total = total + ref[at, :].astype(jnp.float32)
        out[:, :HEAD_DIM] = (total[:, :HEAD_DIM] * SCALE).astype(out.dtype)
        out[:, HEAD_DIM:] = total[:, HEAD_DIM:].astype(out.dtype)


def place_kv(heads, *refs):
    ins, (dk, dv) = refs[:heads], refs[heads:]
    me = lax.axis_index("head")
    for i, ref in enumerate(ins):
        columns = pl.ds(pl.multiple_of((me ^ i) * HEAD_DIM, HEAD_DIM), HEAD_DIM)
        dk[:, columns] = ref[:, :HEAD_DIM]
        dv[:, columns] = ref[:, HEAD_DIM:]


def place_rows(heads, *refs):
    ins, out, sem = refs[:heads], refs[heads], refs[heads + 1]
    me = lax.axis_index("head")
    width = ins[0].shape[1]
    copies = []
    for i in range(heads):
        columns = pl.ds(pl.multiple_of((me ^ i) * width, width), width)
        copies.append(pltpu.make_async_copy(ins[i], out.at[:, columns], sem.at[i]))
    for copy in copies:
        copy.start()
    for copy in copies:
        copy.wait()


def local(queries, keys, values, grad_out, block_order):
    heads = lax.axis_size("head")
    inner = lax.axis_size("inner")
    outer = lax.axis_size("outer")
    block = queries.shape[0]
    ranks = inner * outer
    chunk = ranks * block
    tokens = heads * chunk
    bf16, f32 = jnp.bfloat16, jnp.float32
    V, A, S = pltpu.VMEM, pl.ANY, pltpu.SMEM
    shape = jax.ShapeDtypeStruct
    width = GROUP * HEAD_DIM
    dma = pltpu.SemaphoreType.DMA

    kv_packed = call(
        functools.partial(pack_kv, heads),
        [shape((block, 2 * HEAD_DIM), bf16)] * heads,
        (keys, values), [V] * 2, V,
    )
    kv_got = [kv_packed[0]] + [exchange(kv_packed[i], "head", i) for i in range(1, heads)]
    rows_shape = [shape((block, width), bf16)] * (heads - 1)
    pack = functools.partial(pack_rows, heads)
    q_packed = call(pack, rows_shape, (queries,), [A], A, [dma((heads - 1,))])
    g_packed = call(pack, rows_shape, (grad_out,), [A], A, [dma((heads - 1,))])
    q_got = [exchange(x, "head", i + 1) for i, x in enumerate(q_packed)]
    g_got = [exchange(x, "head", i + 1) for i, x in enumerate(g_packed)]
    mine = call(join_kv, [shape((heads * block, 2 * HEAD_DIM), bf16)], kv_got, [V] * heads, V)[0]
    same = [mine] + [exchange(mine, "inner", s) for s in range(1, inner)]
    bundles = list(same)
    for e in range(1, outer):
        bundles += [exchange(x, "outer", e) for x in same]

    rows_now = GROUP * block if chunk <= 512 else GROUP * block // 2
    results = call(
        functools.partial(main_body, heads, inner, outer, rows_now),
        [shape((block, width), bf16)] * heads
        + [shape((inner * heads * block, 2 * HEAD_DIM), bf16)] * outer,
        (block_order, queries, grad_out, *q_got, *g_got, *bundles),
        [S] + [V] * (2 + 2 * (heads - 1) + inner * outer), V,
        [
            V((tokens, HEAD_DIM), bf16), V((tokens, HEAD_DIM), bf16),
            V((heads, GROUP * block, HEAD_DIM), bf16), V((heads, GROUP * block, HEAD_DIM), bf16),
            V((HEAD_DIM, tokens), bf16),
            V((tokens, rows_now), f32), V((tokens, rows_now), f32),
            V((tokens, HEAD_DIM), f32), V((tokens, HEAD_DIM), f32),
            V((heads, GROUP * block, HEAD_DIM), bf16),
        ],
    )
    dq_parts, same_part, other_parts = results[:heads], results[heads], results[heads + 1 :]
    core_parts = [same_part] + [exchange(x, "outer", e + 1) for e, x in enumerate(other_parts)]
    sums = call(
        functools.partial(sum_cores, outer),
        [shape((heads * block, 2 * HEAD_DIM), bf16)] * inner,
        core_parts, [V] * outer, V,
    )
    inner_parts = [sums[0]] + [exchange(sums[s], "inner", s) for s in range(1, inner)]
    back = call(
        functools.partial(sum_inner, inner),
        [shape((block, 2 * HEAD_DIM), bf16)] * heads,
        inner_parts, [V] * inner, V,
    )
    dq_got = [dq_parts[0]] + [exchange(dq_parts[i], "head", i) for i in range(1, heads)]
    query_back = call(
        functools.partial(place_rows, heads),
        [shape(queries.shape, bf16)], dq_got, [A] * heads, A, [dma((heads,))],
    )[0]
    back_got = [back[0]] + [exchange(back[i], "head", i) for i in range(1, heads)]
    key_back, value_back = call(
        functools.partial(place_kv, heads),
        [shape(keys.shape, bf16)] * 2, back_got, [V] * heads, V,
    )
    return query_back, key_back, value_back


def solution(mesh):
    rows = P(("head", "inner", "outer"), None)
    return jax.shard_map(
        local, mesh=mesh, in_specs=(rows,) * 4 + (P(),), out_specs=(rows,) * 3, check_vma=False
    )
```

time: 474 us -> 116 us (0.24)
  other arithmetic: 273 us -> 0 us
  Pallas kernels: 0 us -> 64.5 us
  matrix products: 56.4 us -> 0 us
  waiting for transfers between devices: 62.7 us -> 13.8 us
  local copies, waits for them, and re-layouts: 29.6 us -> 4.35 us
  between operations: 14.2 us -> 0.92 us
  blocking collectives: 7.2 us -> 0 us
  starting transfers between devices: 25.5 us -> 31.9 us
    add x18 -> x0, other arithmetic: 243 us -> none  [the longest x13 243 us: positions(): jnp.take(block_order, stored_block) * block_rows + local_row % block_rows]
    pallas_call x0 -> x9, Pallas kernels: none -> 64.5 us  [call(): pl.pallas_call(body, out_shape=outs, in_specs=[pl.BlockSpec(memory_space=...]
    dot_general x48 -> x0, matrix products: 56.4 us -> none  [the longest x4 19.6 us: forward_fold(): jnp.einsum('cgqk,kcd->cgqd', probs.astype(jnp.bfloat16), segment[1], pref...]
    ppermute x16 -> x26, starting transfers between devices: 2.58 us -> 31.9 us  [exchange(): return lax.ppermute(array, axis, [(i, i ^ by) for i in range(length)])]
    ppermute x16 -> x26, waiting for transfers between devices: 40.8 us -> 13.8 us  [exchange(): return lax.ppermute(array, axis, [(i, i ^ by) for i in range(length)])]
    all_to_all x6 -> x0, starting transfers between devices: 23 us -> none  [the longest x1 5.16 us: local(): lax.all_to_all(keys, 'head', split_axis=1, concat_axis=0, tiled=True)]
    all_to_all x6 -> x0, waiting for transfers between devices: 21.8 us -> none  [the longest x1 5.27 us: local(): lax.all_to_all(query_low, 'head', split_axis=0, concat_axis=1, tiled=True)]
    gather x56 -> x0, other arithmetic: 20.6 us -> none  [positions(): jnp.take(block_order, stored_block) * block_rows + local_row % block_rows]
  transfers between devices with their start and end apart: 23 -> 26, of which waited for: 13 -> 8; matrix products, arithmetic and copies ran while one was open for 48% -> 0% of each run, Pallas kernels for 0% -> 30%
where the time goes in v1:
time: 116 us; the launch traced here: 115 us
  Pallas kernels  64.5 us (56%)
  starting transfers between devices  31.9 us (28%)
  waiting for transfers between devices  13.8 us (12%)
  local copies, waits for them, and re-layouts  4.35 us (4%)
    pallas_call x9, Pallas kernels, call(): pl.pallas_call(body, out_shape=outs, in_specs=[pl.BlockSpec(memory_space=...  64.5 us
    ppermute x26, starting transfers between devices, exchange(): return lax.ppermute(array, axis, [(i, i ^ by) for i in range(length)])  31.9 us
    ppermute x26, waiting for transfers between devices, exchange(): return lax.ppermute(array, axis, [(i, i ^ by) for i in range(length)])  13.8 us
    unnamed x60, local copies, waits for them, and re-layouts  4.35 us
  transfers between devices with their start and end apart: 26, of which 8 were waited for; matrix products, arithmetic and copies ran while one was open for 0% of the time, Pallas kernels for 30%

profile of v1, /device:TPU:0, one launch (start us, length us, event | category | flops | bytes accessed | tf_op | source)
XLA Modules:
  0.0 115.4 jit_solution(18280402273776723008)
XLA Ops:
  0.6 13.1 %shard_map.76 = (bf16[64,1024]{1,0:T(8,128)(2,1)}, bf16[64,1024]{1,0:T(8,128)(2,1)}, bf16[64,1024]{1,0:T(8,128)(2,1)}) custom-call(bf16[64,4096]{1,0:T(8,128)(2,1)} %refs_0_.1), custom_call_target="tpu_custom_call" | custom-call | tf_op jit(solution)/shard_map/pallas_call | solution.py:33
  13.7 3.0 %collective-permute-start = (bf16[64,1024]{1,0:T(8,128)(2,1)}, bf16[64,1024]{1,0:T(8,128)(2,1)S(1)}, u32[]{:S(2)}, u32[]{:S(2)}) collective-permute-start(bf16[64,1024]{1,0:T(8,128)(2,1)} %get-tuple-element.29), channel_id=1, source_target_pairs={{0,8},{8,0},{16,24},{24,16},{1,9},{9,1},{17,25},{25,17},{2,10},{10... | collective-permute-start | bytes 393224 | tf_op jit(solution)/shard_map/ppermute | solution.py:29
  16.7 1.5 %collective-permute-start.1 = (bf16[64,1024]{1,0:T(8,128)(2,1)}, bf16[64,1024]{1,0:T(8,128)(2,1)S(1)}, u32[]{:S(2)}, u32[]{:S(2)}) collective-permute-start(bf16[64,1024]{1,0:T(8,128)(2,1)} %get-tuple-element.30), channel_id=1, source_target_pairs={{0,16},{8,24},{16,0},{24,8},{1,17},{9,25},{17,1},{25,9},{2,18},{10... | collective-permute-start | bytes 393224 | tf_op jit(solution)/shard_map/ppermute | solution.py:29
  18.2 1.5 %shard_map.78 = (bf16[64,256]{1,0:T(8,128)(2,1)}, bf16[64,256]{1,0:T(8,128)(2,1)}, bf16[64,256]{1,0:T(8,128)(2,1)}, bf16[64,256]{1,0:T(8,128)(2,1)}) custom-call(bf16[64,512]{1,0:T(8,128)(2,1)} %keys_ref.1, bf16[64,512]{1,0:T(8,128)(2,1)} %values_ref.1), custom_call_target="tpu_custom_call" | custom-call | tf_op jit(solution)/shard_map/pallas_call | solution.py:33
  19.8 1.9 %collective-permute-start.6 = (bf16[64,256]{1,0:T(8,128)(2,1)}, bf16[64,256]{1,0:T(8,128)(2,1)S(1)}, u32[]{:S(2)}, u32[]{:S(2)}) collective-permute-start(bf16[64,256]{1,0:T(8,128)(2,1)} %get-tuple-element.36), channel_id=1, source_target_pairs={{0,8},{8,0},{16,24},{24,16},{1,9},{9,1},{17,25},{25,17},{2,10},{10... | collective-permute-start | bytes 98312 | tf_op jit(solution)/shard_map/ppermute | solution.py:29
  21.7 1.5 %collective-permute-start.7 = (bf16[64,256]{1,0:T(8,128)(2,1)}, bf16[64,256]{1,0:T(8,128)(2,1)S(1)}, u32[]{:S(2)}, u32[]{:S(2)}) collective-permute-start(bf16[64,256]{1,0:T(8,128)(2,1)} %get-tuple-element.37), channel_id=1, source_target_pairs={{0,16},{8,24},{16,0},{24,8},{1,17},{9,25},{17,1},{25,9},{2,18},{10... | collective-permute-start | bytes 98312 | tf_op jit(solution)/shard_map/ppermute | solution.py:29
  23.2 0.7 collective-permute-done.6.refs_1_
  24.0 2.8 %collective-permute-start.8 = (bf16[64,256]{1,0:T(8,128)(2,1)}, bf16[64,256]{1,0:T(8,128)(2,1)S(1)}, u32[]{:S(2)}, u32[]{:S(2)}) collective-permute-start(bf16[64,256]{1,0:T(8,128)(2,1)} %get-tuple-element.38), channel_id=1, source_target_pairs={{0,24},{8,16},{16,8},{24,0},{1,25},{9,17},{17,9},{25,1},{2,26},{10... | collective-permute-start | bytes 98312 | tf_op jit(solution)/shard_map/ppermute | solution.py:29
  26.8 13.0 %shard_map.77 = (bf16[64,1024]{1,0:T(8,128)(2,1)}, bf16[64,1024]{1,0:T(8,128)(2,1)}, bf16[64,1024]{1,0:T(8,128)(2,1)}) custom-call(bf16[64,4096]{1,0:T(8,128)(2,1)} %refs_1_.1), custom_call_target="tpu_custom_call" | custom-call | tf_op jit(solution)/shard_map/pallas_call | solution.py:33
  39.9 0.6 collective-permute-start.3
  40.5 0.1 collective-permute-start.4
  40.6 0.5 copy-done.25
  41.1 1.5 %shard_map.79.refs_8_ = bf16[256,256]{1,0:T(8,128)(2,1)} custom-call(bf16[64,256]{1,0:T(8,128)(2,1)} %get-tuple-element.35.refs_0_, bf16[64,256]{1,0:T(8,128)(2,1)} %copy-done.23, bf16[64,256]{1,0:T(8,128)(2,1)} %copy-done.24, bf16[64,256]{1,0:T(8,128)(2,1)} %copy-done.25), custom_call_target="tpu_custom_call" | custom-call | tf_op jit(solution)/shard_map/pallas_call | solution.py:33
  42.6 3.6 %collective-permute-start.11 = (bf16[256,256]{1,0:T(8,128)(2,1)}, bf16[256,256]{1,0:T(8,128)(2,1)S(1)}, u32[]{:S(2)}, u32[]{:S(2)}) collective-permute-start(bf16[256,256]{1,0:T(8,128)(2,1)} %shard_map.79.refs_8_), channel_id=1, source_target_pairs={{0,6},{2,4},{4,2},{6,0},{1,7},{3,5},{5,3},{7,1},{8,14},{10,12},{12... | collective-permute-start | bytes 393224 | tf_op jit(solution)/shard_map/ppermute | solution.py:29
  46.2 0.8 collective-permute-start.9
  47.0 2.4 %collective-permute-start.5 = (bf16[64,1024]{1,0:T(8,128)(2,1)S(1)}, bf16[64,1024]{1,0:T(8,128)(2,1)S(1)}, u32[]{:S(2)}, u32[]{:S(2)}) collective-permute-start(bf16[64,1024]{1,0:T(8,128)(2,1)S(1)} %copy-done.29), channel_id=1, source_target_pairs={{0,24},{8,16},{16,8},{24,0},{1,25},{9,17},{17,9},{25,1},{2,26},{10... | collective-permute-start | bytes 393224 | tf_op jit(solution)/shard_map/ppermute | solution.py:29
  49.4 0.9 collective-permute-done.11.refs_11_
  50.4 5.4 %collective-permute-done.10.refs_10_ = bf16[256,256]{1,0:T(8,128)(2,1)S(1)} collective-permute-done((bf16[256,256]{1,0:T(8,128)(2,1)}, bf16[256,256]{1,0:T(8,128)(2,1)S(1)}, u32[]{:S(2)}, u32[]{:S(2)}) %collective-permute-start.10) | collective-permute-done | bytes 131104 | tf_op jit(solution)/shard_map/ppermute | solution.py:29
  55.7 0.5 collective-permute-start.13
  56.3 0.8 collective-permute-done.14.refs_14_
  57.1 0.2 collective-permute-done.13.refs_13_
  57.3 0.4 copy-done.12
  57.7 0.6 copy-done.13
  58.4 13.0 %shard_map.80 = (bf16[64,1024]{1,0:T(8,128)(2,1)}, bf16[64,1024]{1,0:T(8,128)(2,1)}, bf16[64,1024]{1,0:T(8,128)(2,1)}, bf16[64,1024]{1,0:T(8,128)(2,1)}, bf16[10...) custom-call(s32[32]{0:T(128)} %order_ref.1, bf16[64,4096]{1,0:T(8,128)(2,1)} %refs_0_.1, bf16[64,4096]{1,0:T(8,128)(2,1)} %refs_1_.1, ...), custom_call_target="tpu_custom_call" | custom-call | tf_op jit(solution)/shard_map/pallas_call | solution.py:33
  71.3 0.1 collective-permute-start.19
  71.5 2.0 %collective-permute-done.19.refs_1_ = bf16[1024,256]{1,0:T(8,128)(2,1)S(1)} collective-permute-done((bf16[1024,256]{1,0:T(8,128)(2,1)}, bf16[1024,256]{1,0:T(8,128)(2,1)S(1)}, u32[]{:S(2)}, u32[]{:S(2)}) %collective-permute-start.19) | collective-permute-done | bytes 524320 | tf_op jit(solution)/shard_map/ppermute | solution.py:29
  73.4 0.8 copy-done
  74.2 2.1 %shard_map.82 = (bf16[256,256]{1,0:T(8,128)(2,1)}, bf16[256,256]{1,0:T(8,128)(2,1)}, bf16[256,256]{1,0:T(8,128)(2,1)}, bf16[256,256]{1,0:T(8,128)(2,1)}) custom-call(bf16[1024,256]{1,0:T(8,128)(2,1)} %get-tuple-element.43.refs_0_, bf16[1024,256]{1,0:T(8,128)(2,1)} %copy-done), custom_call_target="tpu_custom_call" | custom-call | tf_op jit(solution)/shard_map/pallas_call | solution.py:33
  76.4 3.0 %collective-permute-start.21 = (bf16[256,256]{1,0:T(8,128)(2,1)}, bf16[256,256]{1,0:T(8,128)(2,1)S(1)}, u32[]{:S(2)}, u32[]{:S(2)}) collective-permute-start(bf16[256,256]{1,0:T(8,128)(2,1)} %get-tuple-element.47), channel_id=1, source_target_pairs={{0,4},{2,6},{4,0},{6,2},{1,5},{3,7},{5,1},{7,3},{8,12},{10,14},{12... | collective-permute-start | bytes 393224 | tf_op jit(solution)/shard_map/ppermute | solution.py:29
  79.4 1.3 %collective-permute-start.22 = (bf16[256,256]{1,0:T(8,128)(2,1)}, bf16[256,256]{1,0:T(8,128)(2,1)S(1)}, u32[]{:S(2)}, u32[]{:S(2)}) collective-permute-start(bf16[256,256]{1,0:T(8,128)(2,1)} %get-tuple-element.48), channel_id=1, source_target_pairs={{0,6},{2,4},{4,2},{6,0},{1,7},{3,5},{5,3},{7,1},{8,14},{10,12},{12... | collective-permute-start | bytes 393224 | tf_op jit(solution)/shard_map/ppermute | solution.py:29
  80.7 1.6 %collective-permute-start.16 = (bf16[64,1024]{1,0:T(8,128)(2,1)S(1)}, bf16[64,1024]{1,0:T(8,128)(2,1)S(1)}, u32[]{:S(2)}, u32[]{:S(2)}) collective-permute-start(bf16[64,1024]{1,0:T(8,128)(2,1)S(1)} %copy-done.28), channel_id=1, source_target_pairs={{0,8},{8,0},{16,24},{24,16},{1,9},{9,1},{17,25},{25,17},{2,10},{10... | collective-permute-start | bytes 393224 | tf_op jit(solution)/shard_map/ppermute | solution.py:29
  82.4 1.2 %collective-permute-start.17 = (bf16[64,1024]{1,0:T(8,128)(2,1)S(1)}, bf16[64,1024]{1,0:T(8,128)(2,1)S(1)}, u32[]{:S(2)}, u32[]{:S(2)}) collective-permute-start(bf16[64,1024]{1,0:T(8,128)(2,1)S(1)} %copy-done.27), channel_id=1, source_target_pairs={{0,16},{8,24},{16,0},{24,8},{1,17},{9,25},{17,1},{25,9},{2,18},{10... | collective-permute-start | bytes 393224 | tf_op jit(solution)/shard_map/ppermute | solution.py:29
  83.5 0.9 collective-permute-done.20.refs_1_
  84.4 2.2 %collective-permute-start.18 = (bf16[64,1024]{1,0:T(8,128)(2,1)S(1)}, bf16[64,1024]{1,0:T(8,128)(2,1)S(1)}, u32[]{:S(2)}, u32[]{:S(2)}) collective-permute-start(bf16[64,1024]{1,0:T(8,128)(2,1)S(1)} %copy-done.26), channel_id=1, source_target_pairs={{0,24},{8,16},{16,8},{24,0},{1,25},{9,17},{17,9},{25,1},{2,26},{10... | collective-permute-start | bytes 393224 | tf_op jit(solution)/shard_map/ppermute | solution.py:29
  86.6 2.9 %collective-permute-done.21.refs_2_ = bf16[256,256]{1,0:T(8,128)(2,1)S(1)} collective-permute-done((bf16[256,256]{1,0:T(8,128)(2,1)}, bf16[256,256]{1,0:T(8,128)(2,1)S(1)}, u32[]{:S(2)}, u32[]{:S(2)}) %collective-permute-start.21) | collective-permute-done | bytes 131104 | tf_op jit(solution)/shard_map/ppermute | solution.py:29
  89.6 0.6 copy-done.15
  90.2 0.0 copy-done.16
  90.3 1.8 %shard_map.83 = (bf16[64,256]{1,0:T(8,128)(2,1)}, bf16[64,256]{1,0:T(8,128)(2,1)}, bf16[64,256]{1,0:T(8,128)(2,1)}, bf16[64,256]{1,0:T(8,128)(2,1)}) custom-call(bf16[256,256]{1,0:T(8,128)(2,1)} %get-tuple-element.45.refs_0_, bf16[256,256]{1,0:T(8,128)(2,1)} %copy-done.14, bf16[256,256]{1,0:T(8,128)(2,1)} %copy-done.15, bf16[256,256]{1,0:T(8,128)(2,1)} %copy-done.16), custom_call_target="tpu_custom_call" | custom-call | tf_op jit(solution)/shard_map/pallas_call | solution.py:33
  92.1 1.6 %collective-permute-start.23 = (bf16[64,256]{1,0:T(8,128)(2,1)}, bf16[64,256]{1,0:T(8,128)(2,1)S(1)}, u32[]{:S(2)}, u32[]{:S(2)}) collective-permute-start(bf16[64,256]{1,0:T(8,128)(2,1)} %get-tuple-element.50), channel_id=1, source_target_pairs={{0,8},{8,0},{16,24},{24,16},{1,9},{9,1},{17,25},{25,17},{2,10},{10... | collective-permute-start | bytes 98312 | tf_op jit(solution)/shard_map/ppermute | solution.py:29
  93.7 1.2 %collective-permute-start.24 = (bf16[64,256]{1,0:T(8,128)(2,1)}, bf16[64,256]{1,0:T(8,128)(2,1)S(1)}, u32[]{:S(2)}, u32[]{:S(2)}) collective-permute-start(bf16[64,256]{1,0:T(8,128)(2,1)} %get-tuple-element.51), channel_id=1, source_target_pairs={{0,16},{8,24},{16,0},{24,8},{1,17},{9,25},{17,1},{25,9},{2,18},{10... | collective-permute-start | bytes 98312 | tf_op jit(solution)/shard_map/ppermute | solution.py:29
  94.9 0.7 collective-permute-start.25
  95.6 0.6 copy-done.18
  96.2 0.1 copy-done.19
  96.3 17.0 %shard_map.81 = bf16[64,4096]{1,0:T(8,128)(2,1)} custom-call(bf16[64,1024]{1,0:T(8,128)(2,1)} %get-tuple-element.39.refs_0_, bf16[64,1024]{1,0:T(8,128)(2,1)} %copy-done.17, bf16[64,1024]{1,0:T(8,128)(2,1)} %copy-done.18, bf16[64,1024]{1,0:T(8,128)(2,1)} %copy-done.19), custom_call_target="tpu_custom_call" | custom-call | tf_op jit(solution)/shard_map/pallas_call | solution.py:33
  113.4 0.6 copy-done.20
  113.9 0.0 copy-done.21
  113.9 0.0 copy-done.22
  114.0 1.5 %shard_map.84 = (bf16[64,512]{1,0:T(8,128)(2,1)}, bf16[64,512]{1,0:T(8,128)(2,1)}) custom-call(bf16[64,256]{1,0:T(8,128)(2,1)} %get-tuple-element.49.refs_0_, bf16[64,256]{1,0:T(8,128)(2,1)} %copy-done.20, bf16[64,256]{1,0:T(8,128)(2,1)} %copy-done.21, bf16[64,256]{1,0:T(8,128)(2,1)} %copy-done.22), custom_call_target="tpu_custom_call" | custom-call | tf_op jit(solution)/shard_map/pallas_call | solution.py:33
  (73 shorter events, 0.2 us)
Async XLA Ops:
  13.7 28.9 %collective-permute-start = (bf16[64,1024]{1,0:T(8,128)(2,1)}, bf16[64,1024]{1,0:T(8,128)(2,1)S(1)}, u32[]{:S(2)}, u32[]{:S(2)}) collective-permute-start(bf16[64,1024]{1,0:T(8,128)(2,1)} %get-tuple-element.29), channel_id=1, source_target_pairs={{0,8},{8,0},{16,24},{24,16},{1,9},{9,1},{17,25},{25,17},{2,10},{10... | collective-permute-start | bytes 393224 | tf_op jit(solution)/shard_map/ppermute | solution.py:29
  16.7 29.5 %collective-permute-start.1 = (bf16[64,1024]{1,0:T(8,128)(2,1)}, bf16[64,1024]{1,0:T(8,128)(2,1)S(1)}, u32[]{:S(2)}, u32[]{:S(2)}) collective-permute-start(bf16[64,1024]{1,0:T(8,128)(2,1)} %get-tuple-element.30), channel_id=1, source_target_pairs={{0,16},{8,24},{16,0},{24,8},{1,17},{9,25},{17,1},{25,9},{2,18},{10... | collective-permute-start | bytes 393224 | tf_op jit(solution)/shard_map/ppermute | solution.py:29
  18.2 28.0 %collective-permute-start.2 = (bf16[64,1024]{1,0:T(8,128)(2,1)}, bf16[64,1024]{1,0:T(8,128)(2,1)S(1)}, u32[]{:S(2)}, u32[]{:S(2)}) collective-permute-start(bf16[64,1024]{1,0:T(8,128)(2,1)} %get-tuple-element.31), channel_id=1, source_target_pairs={{0,24},{8,16},{16,8},{24,0},{1,25},{9,17},{17,9},{25,1},{2,26},{10... | collective-permute-start | bytes 393224 | tf_op jit(solution)/shard_map/ppermute | solution.py:29
  19.8 4.2 %collective-permute-start.6 = (bf16[64,256]{1,0:T(8,128)(2,1)}, bf16[64,256]{1,0:T(8,128)(2,1)S(1)}, u32[]{:S(2)}, u32[]{:S(2)}) collective-permute-start(bf16[64,256]{1,0:T(8,128)(2,1)} %get-tuple-element.36), channel_id=1, source_target_pairs={{0,8},{8,0},{16,24},{24,16},{1,9},{9,1},{17,25},{25,17},{2,10},{10... | collective-permute-start | bytes 98312 | tf_op jit(solution)/shard_map/ppermute | solution.py:29
  21.7 18.1 %collective-permute-start.7 = (bf16[64,256]{1,0:T(8,128)(2,1)}, bf16[64,256]{1,0:T(8,128)(2,1)S(1)}, u32[]{:S(2)}, u32[]{:S(2)}) collective-permute-start(bf16[64,256]{1,0:T(8,128)(2,1)} %get-tuple-element.37), channel_id=1, source_target_pairs={{0,16},{8,24},{16,0},{24,8},{1,17},{9,25},{17,1},{25,9},{2,18},{10... | collective-permute-start | bytes 98312 | tf_op jit(solution)/shard_map/ppermute | solution.py:29
  24.0 15.9 %copy-start.23 = (bf16[64,256]{1,0:T(8,128)(2,1)}, bf16[64,256]{1,0:T(8,128)(2,1)S(1)}, u32[]{:S(2)}) copy-start(bf16[64,256]{1,0:T(8,128)(2,1)S(1)} %collective-permute-done.6.refs_1_) | copy-start | bytes 98308
  24.0 16.5 %collective-permute-start.8 = (bf16[64,256]{1,0:T(8,128)(2,1)}, bf16[64,256]{1,0:T(8,128)(2,1)S(1)}, u32[]{:S(2)}, u32[]{:S(2)}) collective-permute-start(bf16[64,256]{1,0:T(8,128)(2,1)} %get-tuple-element.38), channel_id=1, source_target_pairs={{0,24},{8,16},{16,8},{24,0},{1,25},{9,17},{17,9},{25,1},{2,26},{10... | collective-permute-start | bytes 98312 | tf_op jit(solution)/shard_map/ppermute | solution.py:29
  39.9 0.7 copy-start.24
  39.9 7.1 %collective-permute-start.3 = (bf16[64,1024]{1,0:T(8,128)(2,1)}, bf16[64,1024]{1,0:T(8,128)(2,1)S(1)}, u32[]{:S(2)}, u32[]{:S(2)}) collective-permute-start(bf16[64,1024]{1,0:T(8,128)(2,1)} %get-tuple-element.32), channel_id=1, source_target_pairs={{0,8},{8,0},{16,24},{24,16},{1,9},{9,1},{17,25},{25,17},{2,10},{10... | collective-permute-start | bytes 393224 | tf_op jit(solution)/shard_map/ppermute | solution.py:29
  40.5 9.0 %collective-permute-start.4 = (bf16[64,1024]{1,0:T(8,128)(2,1)}, bf16[64,1024]{1,0:T(8,128)(2,1)S(1)}, u32[]{:S(2)}, u32[]{:S(2)}) collective-permute-start(bf16[64,1024]{1,0:T(8,128)(2,1)} %get-tuple-element.33), channel_id=1, source_target_pairs={{0,16},{8,24},{16,0},{24,8},{1,17},{9,25},{17,1},{25,9},{2,18},{10... | collective-permute-start | bytes 393224 | tf_op jit(solution)/shard_map/ppermute | solution.py:29
  41.1 5.9 %copy-start.29 = (bf16[64,1024]{1,0:T(8,128)(2,1)S(1)}, bf16[64,1024]{1,0:T(8,128)(2,1)}, u32[]{:S(2)}) copy-start(bf16[64,1024]{1,0:T(8,128)(2,1)} %get-tuple-element.34) | copy-start | bytes 393220
  42.6 14.7 %copy-start.1 = (bf16[64,1024]{1,0:T(8,128)(2,1)}, bf16[64,1024]{1,0:T(8,128)(2,1)S(1)}, u32[]{:S(2)}) copy-start(bf16[64,1024]{1,0:T(8,128)(2,1)S(1)} %collective-permute-done.refs_2_) | copy-start | bytes 393220
  42.6 7.8 %collective-permute-start.11 = (bf16[256,256]{1,0:T(8,128)(2,1)}, bf16[256,256]{1,0:T(8,128)(2,1)S(1)}, u32[]{:S(2)}, u32[]{:S(2)}) collective-permute-start(bf16[256,256]{1,0:T(8,128)(2,1)} %shard_map.79.refs_8_), channel_id=1, source_target_pairs={{0,6},{2,4},{4,2},{6,0},{1,7},{3,5},{5,3},{7,1},{8,14},{10,12},{12... | collective-permute-start | bytes 393224 | tf_op jit(solution)/shard_map/ppermute | solution.py:29
  46.2 11.1 %copy-start.2 = (bf16[64,1024]{1,0:T(8,128)(2,1)}, bf16[64,1024]{1,0:T(8,128)(2,1)S(1)}, u32[]{:S(2)}) copy-start(bf16[64,1024]{1,0:T(8,128)(2,1)S(1)} %collective-permute-done.1.refs_3_) | copy-start | bytes 393220
  46.2 9.5 %collective-permute-start.10 = (bf16[256,256]{1,0:T(8,128)(2,1)}, bf16[256,256]{1,0:T(8,128)(2,1)S(1)}, u32[]{:S(2)}, u32[]{:S(2)}) collective-permute-start(bf16[256,256]{1,0:T(8,128)(2,1)} %shard_map.79.refs_8_), channel_id=1, source_target_pairs={{0,4},{2,6},{4,0},{6,2},{1,5},{3,7},{5,1},{7,3},{8,12},{10,14},{12... | collective-permute-start | bytes 393224 | tf_op jit(solution)/shard_map/ppermute | solution.py:29
  46.2 11.0 %copy-start.3 = (bf16[64,1024]{1,0:T(8,128)(2,1)}, bf16[64,1024]{1,0:T(8,128)(2,1)S(1)}, u32[]{:S(2)}) copy-start(bf16[64,1024]{1,0:T(8,128)(2,1)S(1)} %collective-permute-done.2.refs_4_) | copy-start | bytes 393220
  46.2 9.5 %collective-permute-start.9 = (bf16[256,256]{1,0:T(8,128)(2,1)}, bf16[256,256]{1,0:T(8,128)(2,1)S(1)}, u32[]{:S(2)}, u32[]{:S(2)}) collective-permute-start(bf16[256,256]{1,0:T(8,128)(2,1)} %shard_map.79.refs_8_), channel_id=1, source_target_pairs={{0,2},{2,0},{4,6},{6,4},{1,3},{3,1},{5,7},{7,5},{8,10},{10,8},{12,... | collective-permute-start | bytes 393224 | tf_op jit(solution)/shard_map/ppermute | solution.py:29
  47.0 10.3 %copy-start.4 = (bf16[64,1024]{1,0:T(8,128)(2,1)}, bf16[64,1024]{1,0:T(8,128)(2,1)S(1)}, u32[]{:S(2)}) copy-start(bf16[64,1024]{1,0:T(8,128)(2,1)S(1)} %collective-permute-done.3.refs_5_) | copy-start | bytes 393220
  47.0 9.2 %collective-permute-start.5 = (bf16[64,1024]{1,0:T(8,128)(2,1)S(1)}, bf16[64,1024]{1,0:T(8,128)(2,1)S(1)}, u32[]{:S(2)}, u32[]{:S(2)}) collective-permute-start(bf16[64,1024]{1,0:T(8,128)(2,1)S(1)} %copy-done.29), channel_id=1, source_target_pairs={{0,24},{8,16},{16,8},{24,0},{1,25},{9,17},{17,9},{25,1},{2,26},{10... | collective-permute-start | bytes 393224 | tf_op jit(solution)/shard_map/ppermute | solution.py:29
  49.4 7.8 %copy-start.5 = (bf16[64,1024]{1,0:T(8,128)(2,1)}, bf16[64,1024]{1,0:T(8,128)(2,1)S(1)}, u32[]{:S(2)}) copy-start(bf16[64,1024]{1,0:T(8,128)(2,1)S(1)} %collective-permute-done.4.refs_6_) | copy-start | bytes 393220
  49.4 6.8 %collective-permute-start.12 = (bf16[256,256]{1,0:T(8,128)(2,1)}, bf16[256,256]{1,0:T(8,128)(2,1)S(1)}, u32[]{:S(2)}, u32[]{:S(2)}) collective-permute-start(bf16[256,256]{1,0:T(8,128)(2,1)} %shard_map.79.refs_8_), channel_id=1, source_target_pairs={{0,1},{1,0},{2,3},{3,2},{4,5},{5,4},{6,7},{7,6},{8,9},{9,8},{10,11... | collective-permute-start | bytes 393224 | tf_op jit(solution)/shard_map/ppermute | solution.py:29
  50.4 6.9 %copy-start.6 = (bf16[256,256]{1,0:T(8,128)(2,1)}, bf16[256,256]{1,0:T(8,128)(2,1)S(1)}, u32[]{:S(2)}) copy-start(bf16[256,256]{1,0:T(8,128)(2,1)S(1)} %collective-permute-done.11.refs_11_) | copy-start | bytes 393220
  50.4 5.9 %collective-permute-start.15 = (bf16[256,256]{1,0:T(8,128)(2,1)S(1)}, bf16[256,256]{1,0:T(8,128)(2,1)S(1)}, u32[]{:S(2)}, u32[]{:S(2)}) collective-permute-start(bf16[256,256]{1,0:T(8,128)(2,1)S(1)} %collective-permute-done.11.refs_11_), channel_id=1, source_target_pairs={{0,1},{1,0},{2,3},{3,2},{4,5},{5,4},{6,7},{7,6},{8,9},{9,8},{10,11... | collective-permute-start | bytes 393224 | tf_op jit(solution)/shard_map/ppermute | solution.py:29
  55.7 1.6 %copy-start.7 = (bf16[256,256]{1,0:T(8,128)(2,1)}, bf16[256,256]{1,0:T(8,128)(2,1)S(1)}, u32[]{:S(2)}) copy-start(bf16[256,256]{1,0:T(8,128)(2,1)S(1)} %collective-permute-done.10.refs_10_) | copy-start | bytes 393220
  55.7 1.3 %collective-permute-start.14 = (bf16[256,256]{1,0:T(8,128)(2,1)S(1)}, bf16[256,256]{1,0:T(8,128)(2,1)S(1)}, u32[]{:S(2)}, u32[]{:S(2)}) collective-permute-start(bf16[256,256]{1,0:T(8,128)(2,1)S(1)} %collective-permute-done.10.refs_10_), channel_id=1, source_target_pairs={{0,1},{1,0},{2,3},{3,2},{4,5},{5,4},{6,7},{7,6},{8,9},{9,8},{10,11... | collective-permute-start | bytes 393224 | tf_op jit(solution)/shard_map/ppermute | solution.py:29
  55.7 1.6 %copy-start.8 = (bf16[256,256]{1,0:T(8,128)(2,1)}, bf16[256,256]{1,0:T(8,128)(2,1)S(1)}, u32[]{:S(2)}) copy-start(bf16[256,256]{1,0:T(8,128)(2,1)S(1)} %collective-permute-done.9.refs_9_) | copy-start | bytes 393220
  55.7 1.5 %collective-permute-start.13 = (bf16[256,256]{1,0:T(8,128)(2,1)S(1)}, bf16[256,256]{1,0:T(8,128)(2,1)S(1)}, u32[]{:S(2)}, u32[]{:S(2)}) collective-permute-start(bf16[256,256]{1,0:T(8,128)(2,1)S(1)} %collective-permute-done.9.refs_9_), channel_id=1, source_target_pairs={{0,1},{1,0},{2,3},{3,2},{4,5},{5,4},{6,7},{7,6},{8,9},{9,8},{10,11... | collective-permute-start | bytes 393224 | tf_op jit(solution)/shard_map/ppermute | solution.py:29
  56.2 1.1 copy-start.9
  56.2 1.1 copy-start.10
  56.3 1.1 copy-start.11
  71.3 2.1 %collective-permute-start.19 = (bf16[1024,256]{1,0:T(8,128)(2,1)}, bf16[1024,256]{1,0:T(8,128)(2,1)S(1)}, u32[]{:S(2)}, u32[]{:S(2)}) collective-permute-start(bf16[1024,256]{1,0:T(8,128)(2,1)} %get-tuple-element.44), channel_id=1, source_target_pairs={{0,1},{1,0},{2,3},{3,2},{4,5},{5,4},{6,7},{7,6},{8,9},{9,8},{10,11... | collective-permute-start | bytes 1572872 | tf_op jit(solution)/shard_map/ppermute | solution.py:29
  73.4 0.8 copy-start
  74.2 6.5 %copy-start.28 = (bf16[64,1024]{1,0:T(8,128)(2,1)S(1)}, bf16[64,1024]{1,0:T(8,128)(2,1)}, u32[]{:S(2)}) copy-start(bf16[64,1024]{1,0:T(8,128)(2,1)} %get-tuple-element.40) | copy-start | bytes 393220
  74.2 8.1 %copy-start.27 = (bf16[64,1024]{1,0:T(8,128)(2,1)S(1)}, bf16[64,1024]{1,0:T(8,128)(2,1)}, u32[]{:S(2)}) copy-start(bf16[64,1024]{1,0:T(8,128)(2,1)} %get-tuple-element.41) | copy-start | bytes 393220
  74.2 10.2 %copy-start.26 = (bf16[64,1024]{1,0:T(8,128)(2,1)S(1)}, bf16[64,1024]{1,0:T(8,128)(2,1)}, u32[]{:S(2)}) copy-start(bf16[64,1024]{1,0:T(8,128)(2,1)} %get-tuple-element.42) | copy-start | bytes 393220
  76.3 8.1 %collective-permute-start.20 = (bf16[256,256]{1,0:T(8,128)(2,1)}, bf16[256,256]{1,0:T(8,128)(2,1)S(1)}, u32[]{:S(2)}, u32[]{:S(2)}) collective-permute-start(bf16[256,256]{1,0:T(8,128)(2,1)} %get-tuple-element.46), channel_id=1, source_target_pairs={{0,2},{2,0},{4,6},{6,4},{1,3},{3,1},{5,7},{7,5},{8,10},{10,8},{12,... | collective-permute-start | bytes 393224 | tf_op jit(solution)/shard_map/ppermute | solution.py:29
  76.4 13.2 %collective-permute-start.21 = (bf16[256,256]{1,0:T(8,128)(2,1)}, bf16[256,256]{1,0:T(8,128)(2,1)S(1)}, u32[]{:S(2)}, u32[]{:S(2)}) collective-permute-start(bf16[256,256]{1,0:T(8,128)(2,1)} %get-tuple-element.47), channel_id=1, source_target_pairs={{0,4},{2,6},{4,0},{6,2},{1,5},{3,7},{5,1},{7,3},{8,12},{10,14},{12... | collective-permute-start | bytes 393224 | tf_op jit(solution)/shard_map/ppermute | solution.py:29
  79.4 10.2 %collective-permute-start.22 = (bf16[256,256]{1,0:T(8,128)(2,1)}, bf16[256,256]{1,0:T(8,128)(2,1)S(1)}, u32[]{:S(2)}, u32[]{:S(2)}) collective-permute-start(bf16[256,256]{1,0:T(8,128)(2,1)} %get-tuple-element.48), channel_id=1, source_target_pairs={{0,6},{2,4},{4,2},{6,0},{1,7},{3,5},{5,3},{7,1},{8,14},{10,12},{12... | collective-permute-start | bytes 393224 | tf_op jit(solution)/shard_map/ppermute | solution.py:29
  80.7 14.1 %collective-permute-start.16 = (bf16[64,1024]{1,0:T(8,128)(2,1)S(1)}, bf16[64,1024]{1,0:T(8,128)(2,1)S(1)}, u32[]{:S(2)}, u32[]{:S(2)}) collective-permute-start(bf16[64,1024]{1,0:T(8,128)(2,1)S(1)} %copy-done.28), channel_id=1, source_target_pairs={{0,8},{8,0},{16,24},{24,16},{1,9},{9,1},{17,25},{25,17},{2,10},{10... | collective-permute-start | bytes 393224 | tf_op jit(solution)/shard_map/ppermute | solution.py:29
  82.4 13.2 %collective-permute-start.17 = (bf16[64,1024]{1,0:T(8,128)(2,1)S(1)}, bf16[64,1024]{1,0:T(8,128)(2,1)S(1)}, u32[]{:S(2)}, u32[]{:S(2)}) collective-permute-start(bf16[64,1024]{1,0:T(8,128)(2,1)S(1)} %copy-done.27), channel_id=1, source_target_pairs={{0,16},{8,24},{16,0},{24,8},{1,17},{9,25},{17,1},{25,9},{2,18},{10... | collective-permute-start | bytes 393224 | tf_op jit(solution)/shard_map/ppermute | solution.py:29
  84.4 5.2 %copy-start.14 = (bf16[256,256]{1,0:T(8,128)(2,1)}, bf16[256,256]{1,0:T(8,128)(2,1)S(1)}, u32[]{:S(2)}) copy-start(bf16[256,256]{1,0:T(8,128)(2,1)S(1)} %collective-permute-done.20.refs_1_) | copy-start | bytes 393220
  84.4 11.1 %collective-permute-start.18 = (bf16[64,1024]{1,0:T(8,128)(2,1)S(1)}, bf16[64,1024]{1,0:T(8,128)(2,1)S(1)}, u32[]{:S(2)}, u32[]{:S(2)}) collective-permute-start(bf16[64,1024]{1,0:T(8,128)(2,1)S(1)} %copy-done.26), channel_id=1, source_target_pairs={{0,24},{8,16},{16,8},{24,0},{1,25},{9,17},{17,9},{25,1},{2,26},{10... | collective-permute-start | bytes 393224 | tf_op jit(solution)/shard_map/ppermute | solution.py:29
  89.6 0.7 copy-start.16
  92.1 21.2 %collective-permute-start.23 = (bf16[64,256]{1,0:T(8,128)(2,1)}, bf16[64,256]{1,0:T(8,128)(2,1)S(1)}, u32[]{:S(2)}, u32[]{:S(2)}) collective-permute-start(bf16[64,256]{1,0:T(8,128)(2,1)} %get-tuple-element.50), channel_id=1, source_target_pairs={{0,8},{8,0},{16,24},{24,16},{1,9},{9,1},{17,25},{25,17},{2,10},{10... | collective-permute-start | bytes 98312 | tf_op jit(solution)/shard_map/ppermute | solution.py:29
  93.7 19.6 %collective-permute-start.24 = (bf16[64,256]{1,0:T(8,128)(2,1)}, bf16[64,256]{1,0:T(8,128)(2,1)S(1)}, u32[]{:S(2)}, u32[]{:S(2)}) collective-permute-start(bf16[64,256]{1,0:T(8,128)(2,1)} %get-tuple-element.51), channel_id=1, source_target_pairs={{0,16},{8,24},{16,0},{24,8},{1,17},{9,25},{17,1},{25,9},{2,18},{10... | collective-permute-start | bytes 98312 | tf_op jit(solution)/shard_map/ppermute | solution.py:29
  94.9 0.7 copy-start.17
  94.9 18.5 %collective-permute-start.25 = (bf16[64,256]{1,0:T(8,128)(2,1)}, bf16[64,256]{1,0:T(8,128)(2,1)S(1)}, u32[]{:S(2)}, u32[]{:S(2)}) collective-permute-start(bf16[64,256]{1,0:T(8,128)(2,1)} %get-tuple-element.52), channel_id=1, source_target_pairs={{0,24},{8,16},{16,8},{24,0},{1,25},{9,17},{17,9},{25,1},{2,26},{10... | collective-permute-start | bytes 98312 | tf_op jit(solution)/shard_map/ppermute | solution.py:29
  95.6 0.7 copy-start.19
  (8 other events, 5.0 us)

commit v2 on v1

v2 whole, which is shorter than its diff:
```python
import functools

import jax
import jax.numpy as jnp
from jax import lax
from jax.experimental import pallas as pl
from jax.experimental.pallas import tpu as pltpu
from jax.sharding import PartitionSpec as P

HEADS = 32
KV_HEADS = 4
HEAD_DIM = 128
GROUP = HEADS // KV_HEADS
SCALE = HEAD_DIM ** (-0.5)
LOG2E = 1.4426950408889634
masked_score = -1e30

NT = (((1,), (1,)), ((), ()))
NN = (((1,), (0,)), ((), ()))


def dot(a, b, dims):
    return lax.dot_general(a, b, dims, preferred_element_type=jnp.float32)


def exchange(array, axis, by):
    length = lax.axis_size(axis)
    return lax.ppermute(array, axis, [(i, i ^ by) for i in range(length)])


def call(body, outs, args, scratch=(), limit=16):
    arrays, in_specs = [], []
    for array, where in args:
        if where is pltpu.VMEM:
            array = pltpu.with_memory_space_constraint(array, pltpu.VMEM)
        arrays.append(array)
        in_specs.append(pl.BlockSpec(memory_space=pltpu.VMEM if where is None else where))
    shapes, out_specs = [], []
    for dims, dtype, where in outs:
        pinned = where is pltpu.VMEM
        shapes.append(pltpu.VMEM(dims, dtype) if pinned else jax.ShapeDtypeStruct(dims, dtype))
        out_specs.append(pl.BlockSpec(memory_space=pltpu.VMEM if where is None else where))
    return pl.pallas_call(
        body,
        out_shape=shapes,
        in_specs=in_specs,
        out_specs=out_specs,
        scratch_shapes=list(scratch),
        compiler_params=pltpu.CompilerParams(vmem_limit_bytes=limit * 1024 * 1024),
    )(*arrays)


def pack_kv(heads, keys_ref, values_ref, *outs):
    me = lax.axis_index("head")
    for i in range(heads):
        columns = pl.ds(pl.multiple_of((me ^ i) * HEAD_DIM, HEAD_DIM), HEAD_DIM)
        outs[i][:, :HEAD_DIM] = keys_ref[:, columns]
        outs[i][:, HEAD_DIM:] = values_ref[:, columns]


def pack_rows(heads, q_ref, g_ref, *refs):
    outs, sem = refs[:-1], refs[-1]
    me = lax.axis_index("head")
    width = q_ref.shape[1] // heads
    copies = []
    for i in range(heads):
        columns = pl.ds(pl.multiple_of((me ^ i) * width, width), width)
        for j, ref in enumerate((q_ref, g_ref)):
            copies.append(pltpu.make_async_copy(ref.at[:, columns], outs[i].at[j], sem.at[i, j]))
    for copy in copies:
        copy.start()
    for copy in copies:
        copy.wait()


def join_kv(*refs):
    out = refs[-1]
    me = lax.axis_index("head")
    rows = refs[0].shape[0]
    for i, ref in enumerate(refs[:-1]):
        out[pl.ds(pl.multiple_of((me ^ i) * rows, rows), rows), :] = ref[...]


def main_body(heads, inner, outer, rows_now, order_ref, *refs):
    it = iter(refs)
    qg = [next(it) for _ in range(heads)]
    bundles = [[next(it) for _ in range(inner)] for _ in range(outer)]
    dq_outs = [next(it) for _ in range(heads)]
    same_out = next(it)
    other_outs = [next(it) for _ in range(outer - 1)]
    keys, values, queries, grads, key_t, s_ref, p_ref, dk_ref, dv_ref, dq_ref = it

    block = qg[0].shape[1]
    ranks = inner * outer
    chunk = ranks * block
    me = lax.axis_index("head")
    z = lax.axis_index("inner")
    o = lax.axis_index("outer")
    rank = z * outer + o

    for e in range(outer):
        for s in range(inner):
            other = (z ^ s) * outer + (o ^ e)
            for a in range(heads):
                at = pl.ds(pl.multiple_of(order_ref[a * ranks + other] * block, block), block)
                keys[at, :] = bundles[e][s][a * block : (a + 1) * block, :HEAD_DIM]
                values[at, :] = bundles[e][s][a * block : (a + 1) * block, HEAD_DIM:]

    place = [order_ref[(me ^ i) * ranks + rank] for i in range(heads)]
    level_of = [p // ranks for p in place]
    for i in range(heads):
        for g in range(GROUP):
            rows = slice(g * block, (g + 1) * block)
            cols = slice(g * HEAD_DIM, (g + 1) * HEAD_DIM)
            queries[level_of[i], rows, :] = qg[i][0, :, cols]
            grads[level_of[i], rows, :] = qg[i][1, :, cols]

    for c in range(heads):
        key_t[:, c * chunk : (c + 1) * chunk] = keys[c * chunk : (c + 1) * chunk, :].T

    dk_ref[...] = jnp.zeros_like(dk_ref)
    dv_ref[...] = jnp.zeros_like(dv_ref)
    all_rows = GROUP * block
    for level in range(heads):
        position = sum(jnp.where(level_of[i] == level, place[i], 0) for i in range(heads))
        shift = position * block - level * chunk

        def visit(r, level=level, shift=shift):
            here = pl.ds(pl.multiple_of(r * rows_now, rows_now), rows_now)
            q = queries[level, here, :]
            g = grads[level, here, :]
            top = None
            for c in range(level + 1):
                span = slice(c * chunk, (c + 1) * chunk)
                s = dot(keys[span, :], q, NT)
                if c == level:
                    u = lax.broadcasted_iota(jnp.int32, s.shape, 0)
                    t = lax.broadcasted_iota(jnp.int32, s.shape, 1) % block
                    s = jnp.where(u <= t + shift, s, masked_score)
                s_ref[span, :] = s
                now = jnp.max(s, axis=0, keepdims=True)
                top = now if top is None else jnp.maximum(top, now)
            total, dots = None, None
            for c in range(level + 1):
                span = slice(c * chunk, (c + 1) * chunk)
                e = jnp.exp2((s_ref[span, :] - top) * (SCALE * LOG2E))
                s_ref[span, :] = e
                now = jnp.sum(e, axis=0, keepdims=True)
                total = now if total is None else total + now
                dp = dot(values[span, :], g, NT)
                p_ref[span, :] = dp
                now = jnp.sum(e * dp, axis=0, keepdims=True)
                dots = now if dots is None else dots + now
            inverse = 1.0 / total
            dots = dots * inverse
            dq = None
            for c in range(level + 1):
                span = slice(c * chunk, (c + 1) * chunk)
                p = s_ref[span, :] * inverse
                dv_ref[span, :] += dot(p.astype(jnp.bfloat16), g, NN)
                ds = (p * (p_ref[span, :] - dots)).astype(jnp.bfloat16)
                dk_ref[span, :] += dot(ds, q, NN)
                part = dot(key_t[:, span], ds, NN)
                dq = part if dq is None else dq + part
            dq_ref[level, here, :] = (dq * SCALE).T.astype(jnp.bfloat16)

        if all_rows == rows_now:
            visit(0)
        else:
            pl.loop(0, all_rows // rows_now)(visit)

    for i in range(heads):
        for g in range(GROUP):
            dq_outs[i][:, g * HEAD_DIM : (g + 1) * HEAD_DIM] = dq_ref[
                level_of[i], g * block : (g + 1) * block, :
            ]
    for e in range(outer):
        out = same_out if e == 0 else other_outs[e - 1]
        for s in range(inner):
            other = (z ^ s) * outer + (o ^ e)
            for a in range(heads):
                at = pl.ds(pl.multiple_of(order_ref[a * ranks + other] * block, block), block)
                rows = slice((s * heads + a) * block, (s * heads + a + 1) * block)
                out[rows, :HEAD_DIM] = dk_ref[at, :].astype(out.dtype)
                out[rows, HEAD_DIM:] = dv_ref[at, :].astype(out.dtype)


def attend(qg, bundles, block_order, rows_now):
    heads, inner, outer = (lax.axis_size(n) for n in ("head", "inner", "outer"))
    block = qg[0].shape[1]
    tokens = heads * inner * outer * block
    rows = GROUP * block
    bf16, f32, V = jnp.bfloat16, jnp.float32, pltpu.VMEM
    return call(
        functools.partial(main_body, heads, inner, outer, rows_now),
        [((block, GROUP * HEAD_DIM), bf16, V)] * heads
        + [((inner * heads * block, 2 * HEAD_DIM), bf16, V)] * outer,
        [(block_order, pltpu.SMEM)] + [(x, V) for x in qg + bundles],
        [
            V((tokens, HEAD_DIM), bf16), V((tokens, HEAD_DIM), bf16),
            V((heads, rows, HEAD_DIM), bf16), V((heads, rows, HEAD_DIM), bf16),
            V((HEAD_DIM, tokens), bf16),
            V((tokens, rows_now), f32), V((tokens, rows_now), f32),
            V((tokens, HEAD_DIM), f32), V((tokens, HEAD_DIM), f32),
            V((heads, rows, HEAD_DIM), bf16),
        ],
        limit=24 if tokens <= 2048 else 44,
    )


def sum_cores(parts, *refs):
    ins, outs = refs[:parts], refs[parts:]
    rows = outs[0].shape[0]
    for s, out in enumerate(outs):
        span = slice(s * rows, (s + 1) * rows)
        total = ins[0][span, :].astype(jnp.float32)
        for ref in ins[1:]:
            total = total + ref[span, :].astype(jnp.float32)
        out[...] = total.astype(out.dtype)


def sum_inner(parts, *refs):
    ins, outs = refs[:parts], refs[parts:]
    me = lax.axis_index("head")
    rows = outs[0].shape[0]
    for i, out in enumerate(outs):
        at = pl.ds(pl.multiple_of((me ^ i) * rows, rows), rows)
        total = ins[0][at, :].astype(jnp.float32)
        for ref in ins[1:]:
            total = total + ref[at, :].astype(jnp.float32)
        out[:, :HEAD_DIM] = (total[:, :HEAD_DIM] * SCALE).astype(out.dtype)
        out[:, HEAD_DIM:] = total[:, HEAD_DIM:].astype(out.dtype)


def place_kv(heads, *refs):
    ins, (dk, dv) = refs[:heads], refs[heads:]
    me = lax.axis_index("head")
    for i, ref in enumerate(ins):
        columns = pl.ds(pl.multiple_of((me ^ i) * HEAD_DIM, HEAD_DIM), HEAD_DIM)
        dk[:, columns] = ref[:, :HEAD_DIM]
        dv[:, columns] = ref[:, HEAD_DIM:]


def place_rows(heads, *refs):
    ins, out, sem = refs[:heads], refs[heads], refs[heads + 1]
    me = lax.axis_index("head")
    width = ins[0].shape[1]
    copies = []
    for i in range(heads):
        columns = pl.ds(pl.multiple_of((me ^ i) * width, width), width)
        copies.append(pltpu.make_async_copy(ins[i], out.at[:, columns], sem.at[i]))
    for copy in copies:
        copy.start()
    for copy in copies:
        copy.wait()


def local(queries, keys, values, grad_out, block_order):
    heads, inner, outer = (lax.axis_size(n) for n in ("head", "inner", "outer"))
    block = queries.shape[0]
    chunk = inner * outer * block
    bf16 = jnp.bfloat16
    V, A = pltpu.VMEM, pl.ANY
    width = GROUP * HEAD_DIM
    dma = pltpu.SemaphoreType.DMA
    pair = 2 * HEAD_DIM

    kv_packed = call(
        functools.partial(pack_kv, heads),
        [((block, pair), bf16, V)] * heads,
        [(keys, None), (values, None)],
    )
    kv_packed, queries, grad_out = lax.optimization_barrier((kv_packed, queries, grad_out))
    kv_got = [kv_packed[0]] + [exchange(kv_packed[i], "head", i) for i in range(1, heads)]
    qg_packed = call(
        functools.partial(pack_rows, heads),
        [((2, block, width), bf16, V)] * heads,
        [(queries, A), (grad_out, A)],
        [dma((heads, 2))],
    )
    qg = [qg_packed[0]] + [exchange(qg_packed[i], "head", i) for i in range(1, heads)]
    mine = call(
        functools.partial(join_kv), [((heads * block, pair), bf16, V)], [(x, V) for x in kv_got]
    )[0]
    same = [mine] + [exchange(mine, "inner", s) for s in range(1, inner)]
    bundles = list(same)
    for e in range(1, outer):
        bundles += [exchange(x, "outer", e) for x in same]

    rows_now = GROUP * block if chunk <= 512 else GROUP * block // 2
    results = attend(qg, bundles, block_order, rows_now)
    dq_parts, same_part, other_parts = results[:heads], results[heads], results[heads + 1 :]
    core_parts = [same_part] + [exchange(x, "outer", e + 1) for e, x in enumerate(other_parts)]
    sums = call(
        functools.partial(sum_cores, outer),
        [((heads * block, pair), bf16, V)] * inner,
        [(x, V) for x in core_parts],
    )
    inner_parts = [sums[0]] + [exchange(sums[s], "inner", s) for s in range(1, inner)]
    dq_got = [dq_parts[0]] + [exchange(dq_parts[i], "head", i) for i in range(1, heads)]
    back = call(
        functools.partial(sum_inner, inner),
        [((block, pair), bf16, V)] * heads,
        [(x, V) for x in inner_parts],
    )
    back_got = [back[0]] + [exchange(back[i], "head", i) for i in range(1, heads)]
    query_back = call(
        functools.partial(place_rows, heads),
        [(queries.shape, bf16, A)], [(x, V) for x in dq_got], [dma((heads,))],
    )[0]
    key_back, value_back = call(
        functools.partial(place_kv, heads),
        [(keys.shape, bf16, None)] * 2, [(x, V) for x in back_got],
    )
    return query_back, key_back, value_back


def solution(mesh):
    rows = P(("head", "inner", "outer"), None)
    return jax.shard_map(
        local, mesh=mesh, in_specs=(rows,) * 4 + (P(),), out_specs=(rows,) * 3, check_vma=False
    )
```

time: 116 us -> 65.7 us (0.57)
  Pallas kernels: 64.5 us -> 12.4 us
  waiting for transfers between devices: 13.8 us -> 23.8 us
  starting transfers between devices: 31.9 us -> 24.6 us
    pallas_call x9 -> x8, Pallas kernels: 64.5 us -> 12.4 us  [call(): pl.pallas_call(body, out_shape=shapes, in_specs=in_specs, out_specs=out_s...]
    ppermute x26 -> x23, waiting for transfers between devices: 13.8 us -> 23.8 us  [exchange(): return lax.ppermute(array, axis, [(i, i ^ by) for i in range(length)])]
    ppermute x26 -> x23, starting transfers between devices: 31.9 us -> 24.6 us  [exchange(): return lax.ppermute(array, axis, [(i, i ^ by) for i in range(length)])]
    unnamed x60 -> x10, local copies, waits for them, and re-layouts: 4.35 us -> 3.76 us
  transfers between devices with their start and end apart: 26 -> 23, of which waited for: 8 -> 11; matrix products, arithmetic and copies ran while one was open for 0% -> 0% of each run, Pallas kernels for 30% -> 2%
where the time goes in v2:
time: 65.7 us; the launch traced here: 65.3 us
  starting transfers between devices  24.6 us (37%)
  waiting for transfers between devices  23.8 us (36%)
  Pallas kernels  12.4 us (19%)
  local copies, waits for them, and re-layouts  3.76 us (6%)
  between operations  0.76 us (1%)
    ppermute x23, starting transfers between devices, exchange(): return lax.ppermute(array, axis, [(i, i ^ by) for i in range(length)])  24.6 us
    ppermute x23, waiting for transfers between devices, exchange(): return lax.ppermute(array, axis, [(i, i ^ by) for i in range(length)])  23.8 us
    pallas_call x8, Pallas kernels, call(): pl.pallas_call(body, out_shape=shapes, in_specs=in_specs, out_specs=out_s...  12.4 us
    unnamed x10, local copies, waits for them, and re-layouts  3.76 us
  transfers between devices with their start and end apart: 23, of which 11 were waited for; matrix products, arithmetic and copies ran while one was open for 0% of the time, Pallas kernels for 2%

profile of v2, /device:TPU:0, one launch (start us, length us, event | category | flops | bytes accessed | tf_op | source)
XLA Modules:
  0.0 65.3 jit_solution(9110626676612495763)
XLA Ops:
  0.6 0.8 %copy-done.2 = bf16[64,512]{1,0:T(8,128)(2,1)S(1)} copy-done((bf16[64,512]{1,0:T(8,128)(2,1)S(1)}, bf16[64,512]{1,0:T(8,128)(2,1)}, u32[]{:S(2)}) %copy-start.2) | copy-done | bytes 65560
  1.5 0.8 %copy-done.3 = bf16[64,512]{1,0:T(8,128)(2,1)S(1)} copy-done((bf16[64,512]{1,0:T(8,128)(2,1)S(1)}, bf16[64,512]{1,0:T(8,128)(2,1)}, u32[]{:S(2)}) %copy-start.3) | copy-done | bytes 65560
  2.3 3.0 %collective-permute-start.3 = (bf16[64,256]{1,0:T(8,128)(2,1)S(1)}, bf16[64,256]{1,0:T(8,128)(2,1)S(1)}, u32[]{:S(2)}, u32[]{:S(2)}) collective-permute-start(bf16[64,256]{1,0:T(8,128)(2,1)S(1)} %get-tuple-element.44), channel_id=1, source_target_pairs={{0,8},{8,0},{16,24},{24,16},{1,9},{9,1},{17,25},{25,17},{2,10},{10... | collective-permute-start | bytes 98312 | tf_op jit(solution)/shard_map/ppermute | solution.py:28
  5.3 1.5 %collective-permute-start.4 = (bf16[64,256]{1,0:T(8,128)(2,1)S(1)}, bf16[64,256]{1,0:T(8,128)(2,1)S(1)}, u32[]{:S(2)}, u32[]{:S(2)}) collective-permute-start(bf16[64,256]{1,0:T(8,128)(2,1)S(1)} %get-tuple-element.45), channel_id=1, source_target_pairs={{0,16},{8,24},{16,0},{24,8},{1,17},{9,25},{17,1},{25,9},{2,18},{10... | collective-permute-start | bytes 98312 | tf_op jit(solution)/shard_map/ppermute | solution.py:28
  6.9 0.0 collective-permute-start.5
  6.9 0.4 collective-permute-done.3.refs_1_
  7.2 2.0 %collective-permute-done.4.refs_2_ = bf16[64,256]{1,0:T(8,128)(2,1)S(1)} collective-permute-done((bf16[64,256]{1,0:T(8,128)(2,1)S(1)}, bf16[64,256]{1,0:T(8,128)(2,1)S(1)}, u32[]{:S(2)}, u32[]{:S(2)}) %collective-permute-start.4) | collective-permute-done | bytes 32800 | tf_op jit(solution)/shard_map/ppermute | solution.py:28
  9.3 2.4 %collective-permute-done.5.refs_3_ = bf16[64,256]{1,0:T(8,128)(2,1)S(1)} collective-permute-done((bf16[64,256]{1,0:T(8,128)(2,1)S(1)}, bf16[64,256]{1,0:T(8,128)(2,1)S(1)}, u32[]{:S(2)}, u32[]{:S(2)}) %collective-permute-start.5) | collective-permute-done | bytes 32800 | tf_op jit(solution)/shard_map/ppermute | solution.py:28
  11.7 0.1 collective-permute-start.9
  11.8 3.7 %collective-permute-start.8 = (bf16[256,256]{1,0:T(8,128)(2,1)S(1)}, bf16[256,256]{1,0:T(8,128)(2,1)S(1)}, u32[]{:S(2)}, u32[]{:S(2)}) collective-permute-start(bf16[256,256]{1,0:T(8,128)(2,1)S(1)} %shard_map.78.refs_4_), channel_id=1, source_target_pairs={{0,6},{2,4},{4,2},{6,0},{1,7},{3,5},{5,3},{7,1},{8,14},{10,12},{12... | collective-permute-start | bytes 393224 | tf_op jit(solution)/shard_map/ppermute | solution.py:28
  15.4 1.0 %copy-done = bf16[64,4096]{1,0:T(8,128)(2,1)S(1)} copy-done((bf16[64,4096]{1,0:T(8,128)(2,1)S(1)}, bf16[64,4096]{1,0:T(8,128)(2,1)}, u32[]{:S(2)}) %copy-start) | copy-done | bytes 524312
  16.5 1.0 %copy-done.1 = bf16[64,4096]{1,0:T(8,128)(2,1)S(1)} copy-done((bf16[64,4096]{1,0:T(8,128)(2,1)S(1)}, bf16[64,4096]{1,0:T(8,128)(2,1)}, u32[]{:S(2)}) %copy-start.1) | copy-done | bytes 524312
  17.5 0.3 shard_map.77
  17.8 0.6 collective-permute-start
  18.4 0.5 collective-permute-start.1
  18.9 2.4 %collective-permute-start.2 = (bf16[2,64,1024]{2,1,0:T(8,128)(2,1)S(1)}, bf16[2,64,1024]{2,1,0:T(8,128)(2,1)S(1)}, u32[]{:S(2)}, u32[]{:S(2)}) collective-permute-start(bf16[2,64,1024]{2,1,0:T(8,128)(2,1)S(1)} %get-tuple-element.42), channel_id=1, source_target_pairs={{0,24},{8,16},{16,8},{24,0},{1,25},{9,17},{17,9},{25,1},{2,26},{10... | collective-permute-start | bytes 786440 | tf_op jit(solution)/shard_map/ppermute | solution.py:28
  21.4 0.0 collective-permute-done.9.refs_8_
  21.4 0.8 %collective-permute-start.6 = (bf16[256,256]{1,0:T(8,128)(2,1)S(1)}, bf16[256,256]{1,0:T(8,128)(2,1)S(1)}, u32[]{:S(2)}, u32[]{:S(2)}) collective-permute-start(bf16[256,256]{1,0:T(8,128)(2,1)S(1)} %shard_map.78.refs_4_), channel_id=1, source_target_pairs={{0,2},{2,0},{4,6},{6,4},{1,3},{3,1},{5,7},{7,5},{8,10},{10,8},{12,... | collective-permute-start | bytes 393224 | tf_op jit(solution)/shard_map/ppermute | solution.py:28
  22.1 6.7 %collective-permute-done.7.refs_6_ = bf16[256,256]{1,0:T(8,128)(2,1)S(1)} collective-permute-done((bf16[256,256]{1,0:T(8,128)(2,1)S(1)}, bf16[256,256]{1,0:T(8,128)(2,1)S(1)}, u32[]{:S(2)}, u32[]{:S(2)}) %collective-permute-start.7) | collective-permute-done | bytes 131104 | tf_op jit(solution)/shard_map/ppermute | solution.py:28
  28.8 0.1 collective-permute-done.6.refs_5_
  29.0 0.4 collective-permute-start.11
  29.4 0.1 collective-permute-start.10
  29.5 2.6 %collective-permute-done.1.refs_2_ = bf16[2,64,1024]{2,1,0:T(8,128)(2,1)S(1)} collective-permute-done((bf16[2,64,1024]{2,1,0:T(8,128)(2,1)S(1)}, bf16[2,64,1024]{2,1,0:T(8,128)(2,1)S(1)}, u32[]{:S(2)}, u32[]{:S(2)}) %collective-permute-start.1) | collective-permute-done | bytes 262176 | tf_op jit(solution)/shard_map/ppermute | solution.py:28
  32.1 0.0 collective-permute-done.2.refs_3_
  32.1 0.0 collective-permute-done.12.refs_11_
  32.1 0.0 collective-permute-done.11.refs_10_
  32.1 10.4 %shard_map.79 = (bf16[64,1024]{1,0:T(8,128)(2,1)S(1)}, bf16[64,1024]{1,0:T(8,128)(2,1)S(1)}, bf16[64,1024]{1,0:T(8,128)(2,1)S(1)}, bf16[64,1024]{1,0:T(8,128)(2,...) custom-call(s32[32]{0:T(128)S(1)} %copy-done.4, ...), custom_call_target="tpu_custom_call" | custom-call | tf_op jit(solution)/shard_map/pallas_call | solution.py:43
  42.6 0.1 collective-permute-start.16
  42.6 1.9 %collective-permute-done.16.refs_1_ = bf16[1024,256]{1,0:T(8,128)(2,1)S(1)} collective-permute-done((bf16[1024,256]{1,0:T(8,128)(2,1)S(1)}, bf16[1024,256]{1,0:T(8,128)(2,1)S(1)}, u32[]{:S(2)}, u32[]{:S(2)}) %collective-permute-start.16) | collective-permute-done | bytes 524320 | tf_op jit(solution)/shard_map/ppermute | solution.py:28
  44.5 0.1 shard_map.81
  44.7 0.1 collective-permute-start.17
  44.7 0.8 %collective-permute-start.18 = (bf16[256,256]{1,0:T(8,128)(2,1)S(1)}, bf16[256,256]{1,0:T(8,128)(2,1)S(1)}, u32[]{:S(2)}, u32[]{:S(2)}) collective-permute-start(bf16[256,256]{1,0:T(8,128)(2,1)S(1)} %get-tuple-element.55), channel_id=1, source_target_pairs={{0,4},{2,6},{4,0},{6,2},{1,5},{3,7},{5,1},{7,3},{8,12},{10,14},{12... | collective-permute-start | bytes 393224 | tf_op jit(solution)/shard_map/ppermute | solution.py:28
  45.6 3.6 %collective-permute-start.19 = (bf16[256,256]{1,0:T(8,128)(2,1)S(1)}, bf16[256,256]{1,0:T(8,128)(2,1)S(1)}, u32[]{:S(2)}, u32[]{:S(2)}) collective-permute-start(bf16[256,256]{1,0:T(8,128)(2,1)S(1)} %get-tuple-element.56), channel_id=1, source_target_pairs={{0,6},{2,4},{4,2},{6,0},{1,7},{3,5},{5,3},{7,1},{8,14},{10,12},{12... | collective-permute-start | bytes 393224 | tf_op jit(solution)/shard_map/ppermute | solution.py:28
  49.1 1.5 %collective-permute-start.13 = (bf16[64,1024]{1,0:T(8,128)(2,1)S(1)}, bf16[64,1024]{1,0:T(8,128)(2,1)S(1)}, u32[]{:S(2)}, u32[]{:S(2)}) collective-permute-start(bf16[64,1024]{1,0:T(8,128)(2,1)S(1)} %get-tuple-element.48), channel_id=1, source_target_pairs={{0,8},{8,0},{16,24},{24,16},{1,9},{9,1},{17,25},{25,17},{2,10},{10... | collective-permute-start | bytes 393224 | tf_op jit(solution)/shard_map/ppermute | solution.py:28
  50.6 0.5 collective-permute-start.14
  51.1 0.4 collective-permute-done.17.refs_1_
  51.5 1.4 %collective-permute-start.15 = (bf16[64,1024]{1,0:T(8,128)(2,1)S(1)}, bf16[64,1024]{1,0:T(8,128)(2,1)S(1)}, u32[]{:S(2)}, u32[]{:S(2)}) collective-permute-start(bf16[64,1024]{1,0:T(8,128)(2,1)S(1)} %get-tuple-element.50), channel_id=1, source_target_pairs={{0,24},{8,16},{16,8},{24,0},{1,25},{9,17},{17,9},{25,1},{2,26},{10... | collective-permute-start | bytes 393224 | tf_op jit(solution)/shard_map/ppermute | solution.py:28
  52.9 4.8 %collective-permute-done.18.refs_2_ = bf16[256,256]{1,0:T(8,128)(2,1)S(1)} collective-permute-done((bf16[256,256]{1,0:T(8,128)(2,1)S(1)}, bf16[256,256]{1,0:T(8,128)(2,1)S(1)}, u32[]{:S(2)}, u32[]{:S(2)}) %collective-permute-start.18) | collective-permute-done | bytes 131104 | tf_op jit(solution)/shard_map/ppermute | solution.py:28
  57.7 0.0 collective-permute-done.19.refs_3_
  57.7 0.1 shard_map.82
  57.8 1.6 %collective-permute-start.20 = (bf16[64,256]{1,0:T(8,128)(2,1)S(1)}, bf16[64,256]{1,0:T(8,128)(2,1)S(1)}, u32[]{:S(2)}, u32[]{:S(2)}) collective-permute-start(bf16[64,256]{1,0:T(8,128)(2,1)S(1)} %get-tuple-element.58), channel_id=1, source_target_pairs={{0,8},{8,0},{16,24},{24,16},{1,9},{9,1},{17,25},{25,17},{2,10},{10... | collective-permute-start | bytes 98312 | tf_op jit(solution)/shard_map/ppermute | solution.py:28
  59.3 0.5 collective-permute-start.21
  59.9 1.5 %collective-permute-start.22 = (bf16[64,256]{1,0:T(8,128)(2,1)S(1)}, bf16[64,256]{1,0:T(8,128)(2,1)S(1)}, u32[]{:S(2)}, u32[]{:S(2)}) collective-permute-start(bf16[64,256]{1,0:T(8,128)(2,1)S(1)} %get-tuple-element.60), channel_id=1, source_target_pairs={{0,24},{8,16},{16,8},{24,0},{1,25},{9,17},{17,9},{25,1},{2,26},{10... | collective-permute-start | bytes 98312 | tf_op jit(solution)/shard_map/ppermute | solution.py:28
  61.3 0.0 collective-permute-done.14.refs_2_
  61.4 0.8 %shard_map.80 = bf16[64,4096]{1,0:T(8,128)(2,1)} custom-call(bf16[64,1024]{1,0:T(8,128)(2,1)S(1)} %get-tuple-element.47.refs_0_, bf16[64,1024]{1,0:T(8,128)(2,1)S(1)} %collective-permute-done.13.refs_1_, bf16[64,1024]{1,0:T(8,128)(2,1)S(1)} %collective-permute-done.14.refs_2_, bf16[64,1024]{1,0:T(8,128)(2,1)S(1)} %collective-permute-done.15.refs_3_), custom_call_target="tpu_custom_call" | custom-call | tf_op jit(solution)/shard_map/pallas_call | solution.py:43
  62.2 1.1 %collective-permute-done.21.refs_2_ = bf16[64,256]{1,0:T(8,128)(2,1)S(1)} collective-permute-done((bf16[64,256]{1,0:T(8,128)(2,1)S(1)}, bf16[64,256]{1,0:T(8,128)(2,1)S(1)}, u32[]{:S(2)}, u32[]{:S(2)}) %collective-permute-start.21) | collective-permute-done | bytes 32800 | tf_op jit(solution)/shard_map/ppermute | solution.py:28
  63.3 1.4 %collective-permute-done.22.refs_3_ = bf16[64,256]{1,0:T(8,128)(2,1)S(1)} collective-permute-done((bf16[64,256]{1,0:T(8,128)(2,1)S(1)}, bf16[64,256]{1,0:T(8,128)(2,1)S(1)}, u32[]{:S(2)}, u32[]{:S(2)}) %collective-permute-start.22) | collective-permute-done | bytes 32800 | tf_op jit(solution)/shard_map/ppermute | solution.py:28
  64.7 0.7 %shard_map.83 = (bf16[64,512]{1,0:T(8,128)(2,1)}, bf16[64,512]{1,0:T(8,128)(2,1)}) custom-call(bf16[64,256]{1,0:T(8,128)(2,1)S(1)} %get-tuple-element.57.refs_0_, bf16[64,256]{1,0:T(8,128)(2,1)S(1)} %collective-permute-done.20.refs_1_, bf16[64,256]{1,0:T(8,128)(2,1)S(1)} %collective-permute-done.21.refs_2_, bf16[64,256]{1,0:T(8,128)(2,1)S(1)} %collective-permute-done.22.refs_3_), custom_call_target="tpu_custom_call" | custom-call | tf_op jit(solution)/shard_map/pallas_call | solution.py:43
  (16 shorter events, 0.1 us)
Async XLA Ops:
  0.6 0.8 %copy-start.2 = (bf16[64,512]{1,0:T(8,128)(2,1)S(1)}, bf16[64,512]{1,0:T(8,128)(2,1)}, u32[]{:S(2)}) copy-start(bf16[64,512]{1,0:T(8,128)(2,1)} %keys_ref.1) | copy-start | bytes 196612
  1.5 0.8 %copy-start.3 = (bf16[64,512]{1,0:T(8,128)(2,1)S(1)}, bf16[64,512]{1,0:T(8,128)(2,1)}, u32[]{:S(2)}) copy-start(bf16[64,512]{1,0:T(8,128)(2,1)} %values_ref.1) | copy-start | bytes 196612
  2.3 4.9 %collective-permute-start.3 = (bf16[64,256]{1,0:T(8,128)(2,1)S(1)}, bf16[64,256]{1,0:T(8,128)(2,1)S(1)}, u32[]{:S(2)}, u32[]{:S(2)}) collective-permute-start(bf16[64,256]{1,0:T(8,128)(2,1)S(1)} %get-tuple-element.44), channel_id=1, source_target_pairs={{0,8},{8,0},{16,24},{24,16},{1,9},{9,1},{17,25},{25,17},{2,10},{10... | collective-permute-start | bytes 98312 | tf_op jit(solution)/shard_map/ppermute | solution.py:28
  5.3 3.9 %collective-permute-start.4 = (bf16[64,256]{1,0:T(8,128)(2,1)S(1)}, bf16[64,256]{1,0:T(8,128)(2,1)S(1)}, u32[]{:S(2)}, u32[]{:S(2)}) collective-permute-start(bf16[64,256]{1,0:T(8,128)(2,1)S(1)} %get-tuple-element.45), channel_id=1, source_target_pairs={{0,16},{8,24},{16,0},{24,8},{1,17},{9,25},{17,1},{25,9},{2,18},{10... | collective-permute-start | bytes 98312 | tf_op jit(solution)/shard_map/ppermute | solution.py:28
  6.9 4.8 %collective-permute-start.5 = (bf16[64,256]{1,0:T(8,128)(2,1)S(1)}, bf16[64,256]{1,0:T(8,128)(2,1)S(1)}, u32[]{:S(2)}, u32[]{:S(2)}) collective-permute-start(bf16[64,256]{1,0:T(8,128)(2,1)S(1)} %get-tuple-element.46), channel_id=1, source_target_pairs={{0,24},{8,16},{16,8},{24,0},{1,25},{9,17},{17,9},{25,1},{2,26},{10... | collective-permute-start | bytes 98312 | tf_op jit(solution)/shard_map/ppermute | solution.py:28
  11.7 9.7 %collective-permute-start.9 = (bf16[256,256]{1,0:T(8,128)(2,1)S(1)}, bf16[256,256]{1,0:T(8,128)(2,1)S(1)}, u32[]{:S(2)}, u32[]{:S(2)}) collective-permute-start(bf16[256,256]{1,0:T(8,128)(2,1)S(1)} %shard_map.78.refs_4_), channel_id=1, source_target_pairs={{0,1},{1,0},{2,3},{3,2},{4,5},{5,4},{6,7},{7,6},{8,9},{9,8},{10,11... | collective-permute-start | bytes 393224 | tf_op jit(solution)/shard_map/ppermute | solution.py:28
  11.8 9.6 %collective-permute-start.8 = (bf16[256,256]{1,0:T(8,128)(2,1)S(1)}, bf16[256,256]{1,0:T(8,128)(2,1)S(1)}, u32[]{:S(2)}, u32[]{:S(2)}) collective-permute-start(bf16[256,256]{1,0:T(8,128)(2,1)S(1)} %shard_map.78.refs_4_), channel_id=1, source_target_pairs={{0,6},{2,4},{4,2},{6,0},{1,7},{3,5},{5,3},{7,1},{8,14},{10,12},{12... | collective-permute-start | bytes 393224 | tf_op jit(solution)/shard_map/ppermute | solution.py:28
  15.4 1.0 %copy-start = (bf16[64,4096]{1,0:T(8,128)(2,1)S(1)}, bf16[64,4096]{1,0:T(8,128)(2,1)}, u32[]{:S(2)}) copy-start(bf16[64,4096]{1,0:T(8,128)(2,1)} %q_ref) | copy-start | bytes 1572868
  16.5 1.0 %copy-start.1 = (bf16[64,4096]{1,0:T(8,128)(2,1)S(1)}, bf16[64,4096]{1,0:T(8,128)(2,1)}, u32[]{:S(2)}) copy-start(bf16[64,4096]{1,0:T(8,128)(2,1)} %g_ref) | copy-start | bytes 1572868
  17.8 11.6 %collective-permute-start = (bf16[2,64,1024]{2,1,0:T(8,128)(2,1)S(1)}, bf16[2,64,1024]{2,1,0:T(8,128)(2,1)S(1)}, u32[]{:S(2)}, u32[]{:S(2)}) collective-permute-start(bf16[2,64,1024]{2,1,0:T(8,128)(2,1)S(1)} %get-tuple-element.40), channel_id=1, source_target_pairs={{0,8},{8,0},{16,24},{24,16},{1,9},{9,1},{17,25},{25,17},{2,10},{10... | collective-permute-start | bytes 786440 | tf_op jit(solution)/shard_map/ppermute | solution.py:28
  18.4 13.7 %collective-permute-start.1 = (bf16[2,64,1024]{2,1,0:T(8,128)(2,1)S(1)}, bf16[2,64,1024]{2,1,0:T(8,128)(2,1)S(1)}, u32[]{:S(2)}, u32[]{:S(2)}) collective-permute-start(bf16[2,64,1024]{2,1,0:T(8,128)(2,1)S(1)} %get-tuple-element.41), channel_id=1, source_target_pairs={{0,16},{8,24},{16,0},{24,8},{1,17},{9,25},{17,1},{25,9},{2,18},{10... | collective-permute-start | bytes 786440 | tf_op jit(solution)/shard_map/ppermute | solution.py:28
  18.9 13.2 %copy-start.4 = (s32[32]{0:T(128)S(1)}, s32[32]{0:T(128)}, u32[]{:S(2)}) copy-start(s32[32]{0:T(128)} %order_ref.1) | copy-start | bytes 388
  18.9 13.2 %collective-permute-start.2 = (bf16[2,64,1024]{2,1,0:T(8,128)(2,1)S(1)}, bf16[2,64,1024]{2,1,0:T(8,128)(2,1)S(1)}, u32[]{:S(2)}, u32[]{:S(2)}) collective-permute-start(bf16[2,64,1024]{2,1,0:T(8,128)(2,1)S(1)} %get-tuple-element.42), channel_id=1, source_target_pairs={{0,24},{8,16},{16,8},{24,0},{1,25},{9,17},{17,9},{25,1},{2,26},{10... | collective-permute-start | bytes 786440 | tf_op jit(solution)/shard_map/ppermute | solution.py:28
  21.4 7.5 %collective-permute-start.7 = (bf16[256,256]{1,0:T(8,128)(2,1)S(1)}, bf16[256,256]{1,0:T(8,128)(2,1)S(1)}, u32[]{:S(2)}, u32[]{:S(2)}) collective-permute-start(bf16[256,256]{1,0:T(8,128)(2,1)S(1)} %shard_map.78.refs_4_), channel_id=1, source_target_pairs={{0,4},{2,6},{4,0},{6,2},{1,5},{3,7},{5,1},{7,3},{8,12},{10,14},{12... | collective-permute-start | bytes 393224 | tf_op jit(solution)/shard_map/ppermute | solution.py:28
  21.4 7.6 %collective-permute-start.6 = (bf16[256,256]{1,0:T(8,128)(2,1)S(1)}, bf16[256,256]{1,0:T(8,128)(2,1)S(1)}, u32[]{:S(2)}, u32[]{:S(2)}) collective-permute-start(bf16[256,256]{1,0:T(8,128)(2,1)S(1)} %shard_map.78.refs_4_), channel_id=1, source_target_pairs={{0,2},{2,0},{4,6},{6,4},{1,3},{3,1},{5,7},{7,5},{8,10},{10,8},{12,... | collective-permute-start | bytes 393224 | tf_op jit(solution)/shard_map/ppermute | solution.py:28
  28.8 3.3 %collective-permute-start.12 = (bf16[256,256]{1,0:T(8,128)(2,1)S(1)}, bf16[256,256]{1,0:T(8,128)(2,1)S(1)}, u32[]{:S(2)}, u32[]{:S(2)}) collective-permute-start(bf16[256,256]{1,0:T(8,128)(2,1)S(1)} %collective-permute-done.8.refs_7_), channel_id=1, source_target_pairs={{0,1},{1,0},{2,3},{3,2},{4,5},{5,4},{6,7},{7,6},{8,9},{9,8},{10,11... | collective-permute-start | bytes 393224 | tf_op jit(solution)/shard_map/ppermute | solution.py:28
  29.0 3.2 %collective-permute-start.11 = (bf16[256,256]{1,0:T(8,128)(2,1)S(1)}, bf16[256,256]{1,0:T(8,128)(2,1)S(1)}, u32[]{:S(2)}, u32[]{:S(2)}) collective-permute-start(bf16[256,256]{1,0:T(8,128)(2,1)S(1)} %collective-permute-done.7.refs_6_), channel_id=1, source_target_pairs={{0,1},{1,0},{2,3},{3,2},{4,5},{5,4},{6,7},{7,6},{8,9},{9,8},{10,11... | collective-permute-start | bytes 393224 | tf_op jit(solution)/shard_map/ppermute | solution.py:28
  29.4 2.8 %collective-permute-start.10 = (bf16[256,256]{1,0:T(8,128)(2,1)S(1)}, bf16[256,256]{1,0:T(8,128)(2,1)S(1)}, u32[]{:S(2)}, u32[]{:S(2)}) collective-permute-start(bf16[256,256]{1,0:T(8,128)(2,1)S(1)} %collective-permute-done.6.refs_5_), channel_id=1, source_target_pairs={{0,1},{1,0},{2,3},{3,2},{4,5},{5,4},{6,7},{7,6},{8,9},{9,8},{10,11... | collective-permute-start | bytes 393224 | tf_op jit(solution)/shard_map/ppermute | solution.py:28
  42.6 2.0 %collective-permute-start.16 = (bf16[1024,256]{1,0:T(8,128)(2,1)S(1)}, bf16[1024,256]{1,0:T(8,128)(2,1)S(1)}, u32[]{:S(2)}, u32[]{:S(2)}) collective-permute-start(bf16[1024,256]{1,0:T(8,128)(2,1)S(1)} %get-tuple-element.52), channel_id=1, source_target_pairs={{0,1},{1,0},{2,3},{3,2},{4,5},{5,4},{6,7},{7,6},{8,9},{9,8},{10,11... | collective-permute-start | bytes 1572872 | tf_op jit(solution)/shard_map/ppermute | solution.py:28
  44.7 6.8 %collective-permute-start.17 = (bf16[256,256]{1,0:T(8,128)(2,1)S(1)}, bf16[256,256]{1,0:T(8,128)(2,1)S(1)}, u32[]{:S(2)}, u32[]{:S(2)}) collective-permute-start(bf16[256,256]{1,0:T(8,128)(2,1)S(1)} %get-tuple-element.54), channel_id=1, source_target_pairs={{0,2},{2,0},{4,6},{6,4},{1,3},{3,1},{5,7},{7,5},{8,10},{10,8},{12,... | collective-permute-start | bytes 393224 | tf_op jit(solution)/shard_map/ppermute | solution.py:28
  44.7 13.0 %collective-permute-start.18 = (bf16[256,256]{1,0:T(8,128)(2,1)S(1)}, bf16[256,256]{1,0:T(8,128)(2,1)S(1)}, u32[]{:S(2)}, u32[]{:S(2)}) collective-permute-start(bf16[256,256]{1,0:T(8,128)(2,1)S(1)} %get-tuple-element.55), channel_id=1, source_target_pairs={{0,4},{2,6},{4,0},{6,2},{1,5},{3,7},{5,1},{7,3},{8,12},{10,14},{12... | collective-permute-start | bytes 393224 | tf_op jit(solution)/shard_map/ppermute | solution.py:28
  45.6 12.2 %collective-permute-start.19 = (bf16[256,256]{1,0:T(8,128)(2,1)S(1)}, bf16[256,256]{1,0:T(8,128)(2,1)S(1)}, u32[]{:S(2)}, u32[]{:S(2)}) collective-permute-start(bf16[256,256]{1,0:T(8,128)(2,1)S(1)} %get-tuple-element.56), channel_id=1, source_target_pairs={{0,6},{2,4},{4,2},{6,0},{1,7},{3,5},{5,3},{7,1},{8,14},{10,12},{12... | collective-permute-start | bytes 393224 | tf_op jit(solution)/shard_map/ppermute | solution.py:28
  49.1 10.7 %collective-permute-start.13 = (bf16[64,1024]{1,0:T(8,128)(2,1)S(1)}, bf16[64,1024]{1,0:T(8,128)(2,1)S(1)}, u32[]{:S(2)}, u32[]{:S(2)}) collective-permute-start(bf16[64,1024]{1,0:T(8,128)(2,1)S(1)} %get-tuple-element.48), channel_id=1, source_target_pairs={{0,8},{8,0},{16,24},{24,16},{1,9},{9,1},{17,25},{25,17},{2,10},{10... | collective-permute-start | bytes 393224 | tf_op jit(solution)/shard_map/ppermute | solution.py:28
  50.6 10.7 %collective-permute-start.14 = (bf16[64,1024]{1,0:T(8,128)(2,1)S(1)}, bf16[64,1024]{1,0:T(8,128)(2,1)S(1)}, u32[]{:S(2)}, u32[]{:S(2)}) collective-permute-start(bf16[64,1024]{1,0:T(8,128)(2,1)S(1)} %get-tuple-element.49), channel_id=1, source_target_pairs={{0,16},{8,24},{16,0},{24,8},{1,17},{9,25},{17,1},{25,9},{2,18},{10... | collective-permute-start | bytes 393224 | tf_op jit(solution)/shard_map/ppermute | solution.py:28
  51.5 9.9 %collective-permute-start.15 = (bf16[64,1024]{1,0:T(8,128)(2,1)S(1)}, bf16[64,1024]{1,0:T(8,128)(2,1)S(1)}, u32[]{:S(2)}, u32[]{:S(2)}) collective-permute-start(bf16[64,1024]{1,0:T(8,128)(2,1)S(1)} %get-tuple-element.50), channel_id=1, source_target_pairs={{0,24},{8,16},{16,8},{24,0},{1,25},{9,17},{17,9},{25,1},{2,26},{10... | collective-permute-start | bytes 393224 | tf_op jit(solution)/shard_map/ppermute | solution.py:28
  57.8 4.4 %collective-permute-start.20 = (bf16[64,256]{1,0:T(8,128)(2,1)S(1)}, bf16[64,256]{1,0:T(8,128)(2,1)S(1)}, u32[]{:S(2)}, u32[]{:S(2)}) collective-permute-start(bf16[64,256]{1,0:T(8,128)(2,1)S(1)} %get-tuple-element.58), channel_id=1, source_target_pairs={{0,8},{8,0},{16,24},{24,16},{1,9},{9,1},{17,25},{25,17},{2,10},{10... | collective-permute-start | bytes 98312 | tf_op jit(solution)/shard_map/ppermute | solution.py:28
  59.3 3.9 %collective-permute-start.21 = (bf16[64,256]{1,0:T(8,128)(2,1)S(1)}, bf16[64,256]{1,0:T(8,128)(2,1)S(1)}, u32[]{:S(2)}, u32[]{:S(2)}) collective-permute-start(bf16[64,256]{1,0:T(8,128)(2,1)S(1)} %get-tuple-element.59), channel_id=1, source_target_pairs={{0,16},{8,24},{16,0},{24,8},{1,17},{9,25},{17,1},{25,9},{2,18},{10... | collective-permute-start | bytes 98312 | tf_op jit(solution)/shard_map/ppermute | solution.py:28
  59.9 4.8 %collective-permute-start.22 = (bf16[64,256]{1,0:T(8,128)(2,1)S(1)}, bf16[64,256]{1,0:T(8,128)(2,1)S(1)}, u32[]{:S(2)}, u32[]{:S(2)}) collective-permute-start(bf16[64,256]{1,0:T(8,128)(2,1)S(1)} %get-tuple-element.60), channel_id=1, source_target_pairs={{0,24},{8,16},{16,8},{24,0},{1,25},{9,17},{17,9},{25,1},{2,26},{10... | collective-permute-start | bytes 98312 | tf_op jit(solution)/shard_map/ppermute | solution.py:28

commit v3 on v2

--- a/solution.py
+++ b/solution.py
@@ -28,11 +28,18 @@
     return lax.ppermute(array, axis, [(i, i ^ by) for i in range(length)])
 
 
+def trade(pieces, axis, order=None):
+    got = list(pieces)
+    for i in order or range(1, len(pieces)):
+        got[i] = exchange(pieces[i], axis, i)
+    return got
+
+
 def call(body, outs, args, scratch=(), limit=16):
     arrays, in_specs = [], []
     for array, where in args:
-        if where is pltpu.VMEM:
-            array = pltpu.with_memory_space_constraint(array, pltpu.VMEM)
+        if where in (pltpu.VMEM, pltpu.HBM):
+            array = pltpu.with_memory_space_constraint(array, where)
         arrays.append(array)
         in_specs.append(pl.BlockSpec(memory_space=pltpu.VMEM if where is None else where))
     shapes, out_specs = [], []
@@ -50,23 +57,16 @@
     )(*arrays)
 
 
-def pack_kv(heads, keys_ref, values_ref, *outs):
-    me = lax.axis_index("head")
-    for i in range(heads):
-        columns = pl.ds(pl.multiple_of((me ^ i) * HEAD_DIM, HEAD_DIM), HEAD_DIM)
-        outs[i][:, :HEAD_DIM] = keys_ref[:, columns]
-        outs[i][:, HEAD_DIM:] = values_ref[:, columns]
-
-
-def pack_rows(heads, q_ref, g_ref, *refs):
-    outs, sem = refs[:-1], refs[-1]
-    me = lax.axis_index("head")
-    width = q_ref.shape[1] // heads
+def pack(heads, *refs):
+    ins, outs, sem = refs[:2], refs[2:-1], refs[-1]
+    me = lax.axis_index("head")
+    width = ins[0].shape[1] // heads
     copies = []
-    for i in range(heads):
+    for i, out in enumerate(outs):
         columns = pl.ds(pl.multiple_of((me ^ i) * width, width), width)
-        for j, ref in enumerate((q_ref, g_ref)):
-            copies.append(pltpu.make_async_copy(ref.at[:, columns], outs[i].at[j], sem.at[i, j]))
+        for j, ref in enumerate(ins):
+            part = out.at[j] if len(out.shape) == 3 else out.at[:, j * width : (j + 1) * width]
+            copies.append(pltpu.make_async_copy(ref.at[:, columns], part, sem.at[i, j]))
     for copy in copies:
         copy.start()
     for copy in copies:
@@ -129,6 +129,7 @@
             here = pl.ds(pl.multiple_of(r * rows_now, rows_now), rows_now)
             q = queries[level, here, :]
             g = grads[level, here, :]
+            g_t = g.T
             top = None
             for c in range(level + 1):
                 span = slice(c * chunk, (c + 1) * chunk)
@@ -157,7 +158,7 @@
             for c in range(level + 1):
                 span = slice(c * chunk, (c + 1) * chunk)
                 p = s_ref[span, :] * inverse
-                dv_ref[span, :] += dot(p.astype(jnp.bfloat16), g, NN)
+                dv_ref[span, :] += dot(g_t, p.astype(jnp.bfloat16), NT).T
                 ds = (p * (p_ref[span, :] - dots)).astype(jnp.bfloat16)
                 dk_ref[span, :] += dot(ds, q, NN)
                 part = dot(key_t[:, span], ds, NN)
@@ -265,27 +266,30 @@
     dma = pltpu.SemaphoreType.DMA
     pair = 2 * HEAD_DIM
 
+    H = pltpu.HBM
     kv_packed = call(
-        functools.partial(pack_kv, heads),
-        [((block, pair), bf16, V)] * heads,
-        [(keys, None), (values, None)],
+        functools.partial(pack, heads),
+        [((block, pair), bf16, V)] * heads, [(keys, H), (values, H)], [dma((heads, 2))],
     )
     kv_packed, queries, grad_out = lax.optimization_barrier((kv_packed, queries, grad_out))
-    kv_got = [kv_packed[0]] + [exchange(kv_packed[i], "head", i) for i in range(1, heads)]
     qg_packed = call(
-        functools.partial(pack_rows, heads),
-        [((2, block, width), bf16, V)] * heads,
-        [(queries, A), (grad_out, A)],
-        [dma((heads, 2))],
-    )
-    qg = [qg_packed[0]] + [exchange(qg_packed[i], "head", i) for i in range(1, heads)]
+        functools.partial(pack, heads),
+        [((2, block, width), bf16, V)] * heads, [(queries, H), (grad_out, H)], [dma((heads, 2))],
+    )
+    far_first = list(reversed(range(1, heads)))
+    kv_got = trade(kv_packed, "head", far_first)
+    kv_got, qg_packed = lax.optimization_barrier((kv_got, qg_packed))
+    qg = [qg_packed[0]] + [exchange(qg_packed[i], "head", i) for i in range(1, heads - 1)]
+    last, qg = lax.optimization_barrier((qg_packed[-1], qg))
+    qg.append(exchange(last, "head", heads - 1))
     mine = call(
         functools.partial(join_kv), [((heads * block, pair), bf16, V)], [(x, V) for x in kv_got]
     )[0]
     same = [mine] + [exchange(mine, "inner", s) for s in range(1, inner)]
     bundles = list(same)
+    early, _ = lax.optimization_barrier((mine, qg[1:-1]))
     for e in range(1, outer):
-        bundles += [exchange(x, "outer", e) for x in same]
+        bundles += [exchange(x, "outer", e) for x in [early] + same[1:]]
 
     rows_now = GROUP * block if chunk <= 512 else GROUP * block // 2
     results = attend(qg, bundles, block_order, rows_now)
@@ -303,7 +307,7 @@
         [((block, pair), bf16, V)] * heads,
         [(x, V) for x in inner_parts],
     )
-    back_got = [back[0]] + [exchange(back[i], "head", i) for i in range(1, heads)]
+    back_got = trade(back, "head", far_first)
     query_back = call(
         functools.partial(place_rows, heads),
         [(queries.shape, bf16, A)], [(x, V) for x in dq_got], [dma((heads,))],

time: 65.7 us -> 60.4 us (0.919)
  waiting for transfers between devices: 23.8 us -> 19.9 us
  local copies, waits for them, and re-layouts: 3.76 us -> 0.01 us
  Pallas kernels: 12.4 us -> 14.1 us
  starting transfers between devices: 24.6 us -> 25.5 us
    ppermute x23, waiting for transfers between devices: 23.8 us -> 19.9 us  [exchange(): return lax.ppermute(array, axis, [(i, i ^ by) for i in range(length)])]
    unnamed x10 -> x2, local copies, waits for them, and re-layouts: 3.76 us -> 0.01 us
    pallas_call x8, Pallas kernels: 12.4 us -> 14.1 us  [call(): pl.pallas_call(body, out_shape=shapes, in_specs=in_specs, out_specs=out_s...]
    ppermute x23, starting transfers between devices: 24.6 us -> 25.5 us  [exchange(): return lax.ppermute(array, axis, [(i, i ^ by) for i in range(length)])]
  transfers between devices with their start and end apart: 23 -> 23, of which waited for: 11 -> 14; matrix products, arithmetic and copies ran while one was open for 0% -> 0% of each run, Pallas kernels for 2% -> 4%
where the time goes in v3:
time: 60.4 us; the launch traced here: 60.2 us
  starting transfers between devices  25.5 us (42%)
  waiting for transfers between devices  19.9 us (33%)
  Pallas kernels  14.1 us (23%)
  between operations  0.71 us (1%)
    ppermute x23, starting transfers between devices, exchange(): return lax.ppermute(array, axis, [(i, i ^ by) for i in range(length)])  25.5 us
    ppermute x23, waiting for transfers between devices, exchange(): return lax.ppermute(array, axis, [(i, i ^ by) for i in range(length)])  19.9 us
    pallas_call x8, Pallas kernels, call(): pl.pallas_call(body, out_shape=shapes, in_specs=in_specs, out_specs=out_s...  14.1 us
  transfers between devices with their start and end apart: 23, of which 14 were waited for; matrix products, arithmetic and copies ran while one was open for 0% of the time, Pallas kernels for 4%

profile of v3, /device:TPU:0, one launch (start us, length us, event | category | flops | bytes accessed | tf_op | source)
XLA Modules:
  0.0 60.2 jit_solution(8610372118959628887)
XLA Ops:
  0.6 0.9 %shard_map.76 = (bf16[64,256]{1,0:T(8,128)(2,1)S(1)}, bf16[64,256]{1,0:T(8,128)(2,1)S(1)}, bf16[64,256]{1,0:T(8,128)(2,1)S(1)}, bf16[64,256]{1,0:T(8,128)(2,1)S(1)}) custom-call(bf16[64,512]{1,0:T(8,128)(2,1)} %refs_0_.1, bf16[64,512]{1,0:T(8,128)(2,1)} %refs_1_.1), custom_call_target="tpu_custom_call" | custom-call | tf_op jit(solution)/shard_map/pallas_call | solution.py:50
  1.6 3.0 %collective-permute-start = (bf16[64,256]{1,0:T(8,128)(2,1)S(1)}, bf16[64,256]{1,0:T(8,128)(2,1)S(1)}, u32[]{:S(2)}, u32[]{:S(2)}) collective-permute-start(bf16[64,256]{1,0:T(8,128)(2,1)S(1)} %get-tuple-element.51), channel_id=1, source_target_pairs={{0,8},{8,0},{16,24},{24,16},{1,9},{9,1},{17,25},{25,17},{2,10},{10... | collective-permute-start | bytes 98312 | tf_op jit(solution)/shard_map/ppermute | solution.py:28
  4.6 1.5 %collective-permute-start.1 = (bf16[64,256]{1,0:T(8,128)(2,1)S(1)}, bf16[64,256]{1,0:T(8,128)(2,1)S(1)}, u32[]{:S(2)}, u32[]{:S(2)}) collective-permute-start(bf16[64,256]{1,0:T(8,128)(2,1)S(1)} %get-tuple-element.52), channel_id=1, source_target_pairs={{0,16},{8,24},{16,0},{24,8},{1,17},{9,25},{17,1},{25,9},{2,18},{10... | collective-permute-start | bytes 98312 | tf_op jit(solution)/shard_map/ppermute | solution.py:28
  6.1 0.0 collective-permute-start.2
  6.1 1.4 %shard_map.77 = (bf16[2,64,1024]{2,1,0:T(8,128)(2,1)S(1)}, bf16[2,64,1024]{2,1,0:T(8,128)(2,1)S(1)}, bf16[2,64,1024]{2,1,0:T(8,128)(2,1)S(1)}, bf16[2,64,1024]{2,1,0:T(8,128)(2,1)S(1)}) custom-call(bf16[64,4096]{1,0:T(8,128)(2,1)} %refs_0_.2, bf16[64,4096]{1,0:T(8,128)(2,1)} %refs_1_.2), custom_call_target="tpu_custom_call" | custom-call | tf_op jit(solution)/shard_map/pallas_call | solution.py:50
  7.5 0.0 collective-permute-done.refs_1_
  7.5 1.0 %collective-permute-done.1.refs_2_ = bf16[64,256]{1,0:T(8,128)(2,1)S(1)} collective-permute-done((bf16[64,256]{1,0:T(8,128)(2,1)S(1)}, bf16[64,256]{1,0:T(8,128)(2,1)S(1)}, u32[]{:S(2)}, u32[]{:S(2)}) %collective-permute-start.1) | collective-permute-done | bytes 32800 | tf_op jit(solution)/shard_map/ppermute | solution.py:28
  8.5 2.4 %collective-permute-done.2.refs_3_ = bf16[64,256]{1,0:T(8,128)(2,1)S(1)} collective-permute-done((bf16[64,256]{1,0:T(8,128)(2,1)S(1)}, bf16[64,256]{1,0:T(8,128)(2,1)S(1)}, u32[]{:S(2)}, u32[]{:S(2)}) %collective-permute-start.2) | collective-permute-done | bytes 32800 | tf_op jit(solution)/shard_map/ppermute | solution.py:28
  10.9 0.5 collective-permute-start.3
  11.4 0.1 collective-permute-start.4
  11.5 4.1 %collective-permute-start.8 = (bf16[256,256]{1,0:T(8,128)(2,1)S(1)}, bf16[256,256]{1,0:T(8,128)(2,1)S(1)}, u32[]{:S(2)}, u32[]{:S(2)}) collective-permute-start(bf16[256,256]{1,0:T(8,128)(2,1)S(1)} %shard_map.78.refs_4_), channel_id=1, source_target_pairs={{0,6},{2,4},{4,2},{6,0},{1,7},{3,5},{5,3},{7,1},{8,14},{10,12},{12... | collective-permute-start | bytes 393224 | tf_op jit(solution)/shard_map/ppermute | solution.py:28
  15.6 0.0 collective-permute-start.7
  15.6 0.6 %collective-permute-start.6 = (bf16[256,256]{1,0:T(8,128)(2,1)S(1)}, bf16[256,256]{1,0:T(8,128)(2,1)S(1)}, u32[]{:S(2)}, u32[]{:S(2)}) collective-permute-start(bf16[256,256]{1,0:T(8,128)(2,1)S(1)} %shard_map.78.refs_4_), channel_id=1, source_target_pairs={{0,2},{2,0},{4,6},{6,4},{1,3},{3,1},{5,7},{7,5},{8,10},{10,8},{12,... | collective-permute-start | bytes 393224 | tf_op jit(solution)/shard_map/ppermute | solution.py:28
  16.3 1.0 %collective-permute-done.3.refs_1_ = bf16[2,64,1024]{2,1,0:T(8,128)(2,1)S(1)} collective-permute-done((bf16[2,64,1024]{2,1,0:T(8,128)(2,1)S(1)}, bf16[2,64,1024]{2,1,0:T(8,128)(2,1)S(1)}, u32[]{:S(2)}, u32[]{:S(2)}) %collective-permute-start.3) | collective-permute-done | bytes 262176 | tf_op jit(solution)/shard_map/ppermute | solution.py:28
  17.3 0.5 collective-permute-done.4.refs_2_
  17.8 1.4 %collective-permute-start.5 = (bf16[2,64,1024]{2,1,0:T(8,128)(2,1)S(1)}, bf16[2,64,1024]{2,1,0:T(8,128)(2,1)S(1)}, u32[]{:S(2)}, u32[]{:S(2)}) collective-permute-start(bf16[2,64,1024]{2,1,0:T(8,128)(2,1)S(1)} %get-tuple-element.67), channel_id=1, source_target_pairs={{0,24},{8,16},{16,8},{24,0},{1,25},{9,17},{17,9},{25,1},{2,26},{10... | collective-permute-start | bytes 786440 | tf_op jit(solution)/shard_map/ppermute | solution.py:28
  19.2 0.3 collective-permute-done.8.refs_7_
  19.6 4.9 %collective-permute-done.7.refs_6_ = bf16[256,256]{1,0:T(8,128)(2,1)S(1)} collective-permute-done((bf16[256,256]{1,0:T(8,128)(2,1)S(1)}, bf16[256,256]{1,0:T(8,128)(2,1)S(1)}, u32[]{:S(2)}, u32[]{:S(2)}) %collective-permute-start.7) | collective-permute-done | bytes 131104 | tf_op jit(solution)/shard_map/ppermute | solution.py:28
  24.5 0.5 collective-permute-start.10
  25.0 0.0 collective-permute-start.9
  25.0 0.0 collective-permute-done.12.refs_11_
  25.0 0.8 %collective-permute-done.11.refs_10_ = bf16[256,256]{1,0:T(8,128)(2,1)S(1)} collective-permute-done((bf16[256,256]{1,0:T(8,128)(2,1)S(1)}, bf16[256,256]{1,0:T(8,128)(2,1)S(1)}, u32[]{:S(2)}, u32[]{:S(2)}) %collective-permute-start.11) | collective-permute-done | bytes 131104 | tf_op jit(solution)/shard_map/ppermute | solution.py:28
  25.8 0.2 collective-permute-done.10.refs_9_
  26.0 0.3 collective-permute-done.9.refs_8_
  26.4 10.1 %shard_map.79 = (bf16[64,1024]{1,0:T(8,128)(2,1)S(1)}, bf16[64,1024]{1,0:T(8,128)(2,1)S(1)}, bf16[64,1024]{1,0:T(8,128)(2,1)S(1)}, bf16[64,1024]{1,0:T(8,128)(2,...) custom-call(s32[32]{0:T(128)S(1)} %copy-done, bf16[2,64,1024]{2,1,0:T(8,128)(2,1)S(1)} %get-tuple-element.64.refs_0_, ...), custom_call_target="tpu_custom_call" | custom-call | tf_op jit(solution)/shard_map/pallas_call | solution.py:50
  36.4 0.3 collective-permute-start.16
  36.7 1.7 %collective-permute-done.16.refs_1_ = bf16[1024,256]{1,0:T(8,128)(2,1)S(1)} collective-permute-done((bf16[1024,256]{1,0:T(8,128)(2,1)S(1)}, bf16[1024,256]{1,0:T(8,128)(2,1)S(1)}, u32[]{:S(2)}, u32[]{:S(2)}) %collective-permute-start.16) | collective-permute-done | bytes 524320 | tf_op jit(solution)/shard_map/ppermute | solution.py:28
  38.4 0.1 shard_map.81
  38.5 0.4 collective-permute-start.17
  38.9 2.7 %collective-permute-start.18 = (bf16[256,256]{1,0:T(8,128)(2,1)S(1)}, bf16[256,256]{1,0:T(8,128)(2,1)S(1)}, u32[]{:S(2)}, u32[]{:S(2)}) collective-permute-start(bf16[256,256]{1,0:T(8,128)(2,1)S(1)} %get-tuple-element.81), channel_id=1, source_target_pairs={{0,4},{2,6},{4,0},{6,2},{1,5},{3,7},{5,1},{7,3},{8,12},{10,14},{12... | collective-permute-start | bytes 393224 | tf_op jit(solution)/shard_map/ppermute | solution.py:28
  41.7 1.3 %collective-permute-start.19 = (bf16[256,256]{1,0:T(8,128)(2,1)S(1)}, bf16[256,256]{1,0:T(8,128)(2,1)S(1)}, u32[]{:S(2)}, u32[]{:S(2)}) collective-permute-start(bf16[256,256]{1,0:T(8,128)(2,1)S(1)} %get-tuple-element.82), channel_id=1, source_target_pairs={{0,6},{2,4},{4,2},{6,0},{1,7},{3,5},{5,3},{7,1},{8,14},{10,12},{12... | collective-permute-start | bytes 393224 | tf_op jit(solution)/shard_map/ppermute | solution.py:28
  43.0 1.4 %collective-permute-start.13 = (bf16[64,1024]{1,0:T(8,128)(2,1)S(1)}, bf16[64,1024]{1,0:T(8,128)(2,1)S(1)}, u32[]{:S(2)}, u32[]{:S(2)}) collective-permute-start(bf16[64,1024]{1,0:T(8,128)(2,1)S(1)} %get-tuple-element.74), channel_id=1, source_target_pairs={{0,8},{8,0},{16,24},{24,16},{1,9},{9,1},{17,25},{25,17},{2,10},{10... | collective-permute-start | bytes 393224 | tf_op jit(solution)/shard_map/ppermute | solution.py:28
  44.4 1.5 %collective-permute-start.14 = (bf16[64,1024]{1,0:T(8,128)(2,1)S(1)}, bf16[64,1024]{1,0:T(8,128)(2,1)S(1)}, u32[]{:S(2)}, u32[]{:S(2)}) collective-permute-start(bf16[64,1024]{1,0:T(8,128)(2,1)S(1)} %get-tuple-element.75), channel_id=1, source_target_pairs={{0,16},{8,24},{16,0},{24,8},{1,17},{9,25},{17,1},{25,9},{2,18},{10... | collective-permute-start | bytes 393224 | tf_op jit(solution)/shard_map/ppermute | solution.py:28
  45.9 0.5 collective-permute-done.17.refs_1_
  46.4 2.5 %collective-permute-start.15 = (bf16[64,1024]{1,0:T(8,128)(2,1)S(1)}, bf16[64,1024]{1,0:T(8,128)(2,1)S(1)}, u32[]{:S(2)}, u32[]{:S(2)}) collective-permute-start(bf16[64,1024]{1,0:T(8,128)(2,1)S(1)} %get-tuple-element.76), channel_id=1, source_target_pairs={{0,24},{8,16},{16,8},{24,0},{1,25},{9,17},{17,9},{25,1},{2,26},{10... | collective-permute-start | bytes 393224 | tf_op jit(solution)/shard_map/ppermute | solution.py:28
  48.9 2.9 %collective-permute-done.18.refs_2_ = bf16[256,256]{1,0:T(8,128)(2,1)S(1)} collective-permute-done((bf16[256,256]{1,0:T(8,128)(2,1)S(1)}, bf16[256,256]{1,0:T(8,128)(2,1)S(1)}, u32[]{:S(2)}, u32[]{:S(2)}) %collective-permute-start.18) | collective-permute-done | bytes 131104 | tf_op jit(solution)/shard_map/ppermute | solution.py:28
  51.8 0.0 collective-permute-done.19.refs_3_
  51.8 0.1 shard_map.82
  51.9 1.5 %collective-permute-start.20 = (bf16[64,256]{1,0:T(8,128)(2,1)S(1)}, bf16[64,256]{1,0:T(8,128)(2,1)S(1)}, u32[]{:S(2)}, u32[]{:S(2)}) collective-permute-start(bf16[64,256]{1,0:T(8,128)(2,1)S(1)} %get-tuple-element.84), channel_id=1, source_target_pairs={{0,8},{8,0},{16,24},{24,16},{1,9},{9,1},{17,25},{25,17},{2,10},{10... | collective-permute-start | bytes 98312 | tf_op jit(solution)/shard_map/ppermute | solution.py:28
  53.4 1.3 %collective-permute-start.21 = (bf16[64,256]{1,0:T(8,128)(2,1)S(1)}, bf16[64,256]{1,0:T(8,128)(2,1)S(1)}, u32[]{:S(2)}, u32[]{:S(2)}) collective-permute-start(bf16[64,256]{1,0:T(8,128)(2,1)S(1)} %get-tuple-element.85), channel_id=1, source_target_pairs={{0,16},{8,24},{16,0},{24,8},{1,17},{9,25},{17,1},{25,9},{2,18},{10... | collective-permute-start | bytes 98312 | tf_op jit(solution)/shard_map/ppermute | solution.py:28
  54.7 0.7 %collective-permute-start.22 = (bf16[64,256]{1,0:T(8,128)(2,1)S(1)}, bf16[64,256]{1,0:T(8,128)(2,1)S(1)}, u32[]{:S(2)}, u32[]{:S(2)}) collective-permute-start(bf16[64,256]{1,0:T(8,128)(2,1)S(1)} %get-tuple-element.86), channel_id=1, source_target_pairs={{0,24},{8,16},{16,8},{24,0},{1,25},{9,17},{17,9},{25,1},{2,26},{10... | collective-permute-start | bytes 98312 | tf_op jit(solution)/shard_map/ppermute | solution.py:28
  55.5 0.0 collective-permute-done.14.refs_2_
  55.5 0.0 collective-permute-done.15.refs_3_
  55.5 0.8 %shard_map.80 = bf16[64,4096]{1,0:T(8,128)(2,1)} custom-call(bf16[64,1024]{1,0:T(8,128)(2,1)S(1)} %get-tuple-element.73.refs_0_, bf16[64,1024]{1,0:T(8,128)(2,1)S(1)} %collective-permute-done.13.refs_1_, bf16[64,1024]{1,0:T(8,128)(2,1)S(1)} %collective-permute-done.14.refs_2_, bf16[64,1024]{1,0:T(8,128)(2,1)S(1)} %collective-permute-done.15.refs_3_), custom_call_target="tpu_custom_call" | custom-call | tf_op jit(solution)/shard_map/pallas_call | solution.py:50
  56.3 0.0 collective-permute-done.20.refs_1_
  56.3 1.0 %collective-permute-done.21.refs_2_ = bf16[64,256]{1,0:T(8,128)(2,1)S(1)} collective-permute-done((bf16[64,256]{1,0:T(8,128)(2,1)S(1)}, bf16[64,256]{1,0:T(8,128)(2,1)S(1)}, u32[]{:S(2)}, u32[]{:S(2)}) %collective-permute-start.21) | collective-permute-done | bytes 32800 | tf_op jit(solution)/shard_map/ppermute | solution.py:28
  57.4 2.2 %collective-permute-done.22.refs_3_ = bf16[64,256]{1,0:T(8,128)(2,1)S(1)} collective-permute-done((bf16[64,256]{1,0:T(8,128)(2,1)S(1)}, bf16[64,256]{1,0:T(8,128)(2,1)S(1)}, u32[]{:S(2)}, u32[]{:S(2)}) %collective-permute-start.22) | collective-permute-done | bytes 32800 | tf_op jit(solution)/shard_map/ppermute | solution.py:28
  59.6 0.7 %shard_map.83 = (bf16[64,512]{1,0:T(8,128)(2,1)}, bf16[64,512]{1,0:T(8,128)(2,1)}) custom-call(bf16[64,256]{1,0:T(8,128)(2,1)S(1)} %get-tuple-element.83.refs_0_, bf16[64,256]{1,0:T(8,128)(2,1)S(1)} %collective-permute-done.20.refs_1_, bf16[64,256]{1,0:T(8,128)(2,1)S(1)} %collective-permute-done.21.refs_2_, bf16[64,256]{1,0:T(8,128)(2,1)S(1)} %collective-permute-done.22.refs_3_), custom_call_target="tpu_custom_call" | custom-call | tf_op jit(solution)/shard_map/pallas_call | solution.py:50
  (8 shorter events, 0.0 us)
Async XLA Ops:
  1.6 5.9 %collective-permute-start = (bf16[64,256]{1,0:T(8,128)(2,1)S(1)}, bf16[64,256]{1,0:T(8,128)(2,1)S(1)}, u32[]{:S(2)}, u32[]{:S(2)}) collective-permute-start(bf16[64,256]{1,0:T(8,128)(2,1)S(1)} %get-tuple-element.51), channel_id=1, source_target_pairs={{0,8},{8,0},{16,24},{24,16},{1,9},{9,1},{17,25},{25,17},{2,10},{10... | collective-permute-start | bytes 98312 | tf_op jit(solution)/shard_map/ppermute | solution.py:28
  4.6 3.9 %collective-permute-start.1 = (bf16[64,256]{1,0:T(8,128)(2,1)S(1)}, bf16[64,256]{1,0:T(8,128)(2,1)S(1)}, u32[]{:S(2)}, u32[]{:S(2)}) collective-permute-start(bf16[64,256]{1,0:T(8,128)(2,1)S(1)} %get-tuple-element.52), channel_id=1, source_target_pairs={{0,16},{8,24},{16,0},{24,8},{1,17},{9,25},{17,1},{25,9},{2,18},{10... | collective-permute-start | bytes 98312 | tf_op jit(solution)/shard_map/ppermute | solution.py:28
  6.1 4.8 %collective-permute-start.2 = (bf16[64,256]{1,0:T(8,128)(2,1)S(1)}, bf16[64,256]{1,0:T(8,128)(2,1)S(1)}, u32[]{:S(2)}, u32[]{:S(2)}) collective-permute-start(bf16[64,256]{1,0:T(8,128)(2,1)S(1)} %get-tuple-element.53), channel_id=1, source_target_pairs={{0,24},{8,16},{16,8},{24,0},{1,25},{9,17},{17,9},{25,1},{2,26},{10... | collective-permute-start | bytes 98312 | tf_op jit(solution)/shard_map/ppermute | solution.py:28
  10.9 15.5 %copy-start = (s32[32]{0:T(128)S(1)}, s32[32]{0:T(128)}, u32[]{:S(2)}) copy-start(s32[32]{0:T(128)} %order_ref.1) | copy-start | bytes 388
  10.9 6.4 %collective-permute-start.3 = (bf16[2,64,1024]{2,1,0:T(8,128)(2,1)S(1)}, bf16[2,64,1024]{2,1,0:T(8,128)(2,1)S(1)}, u32[]{:S(2)}, u32[]{:S(2)}) collective-permute-start(bf16[2,64,1024]{2,1,0:T(8,128)(2,1)S(1)} %get-tuple-element.62), channel_id=1, source_target_pairs={{0,8},{8,0},{16,24},{24,16},{1,9},{9,1},{17,25},{25,17},{2,10},{10... | collective-permute-start | bytes 786440 | tf_op jit(solution)/shard_map/ppermute | solution.py:28
  11.4 6.4 %collective-permute-start.4 = (bf16[2,64,1024]{2,1,0:T(8,128)(2,1)S(1)}, bf16[2,64,1024]{2,1,0:T(8,128)(2,1)S(1)}, u32[]{:S(2)}, u32[]{:S(2)}) collective-permute-start(bf16[2,64,1024]{2,1,0:T(8,128)(2,1)S(1)} %get-tuple-element.63), channel_id=1, source_target_pairs={{0,16},{8,24},{16,0},{24,8},{1,17},{9,25},{17,1},{25,9},{2,18},{10... | collective-permute-start | bytes 786440 | tf_op jit(solution)/shard_map/ppermute | solution.py:28
  11.5 8.1 %collective-permute-start.8 = (bf16[256,256]{1,0:T(8,128)(2,1)S(1)}, bf16[256,256]{1,0:T(8,128)(2,1)S(1)}, u32[]{:S(2)}, u32[]{:S(2)}) collective-permute-start(bf16[256,256]{1,0:T(8,128)(2,1)S(1)} %shard_map.78.refs_4_), channel_id=1, source_target_pairs={{0,6},{2,4},{4,2},{6,0},{1,7},{3,5},{5,3},{7,1},{8,14},{10,12},{12... | collective-permute-start | bytes 393224 | tf_op jit(solution)/shard_map/ppermute | solution.py:28
  15.6 8.9 %collective-permute-start.7 = (bf16[256,256]{1,0:T(8,128)(2,1)S(1)}, bf16[256,256]{1,0:T(8,128)(2,1)S(1)}, u32[]{:S(2)}, u32[]{:S(2)}) collective-permute-start(bf16[256,256]{1,0:T(8,128)(2,1)S(1)} %shard_map.78.refs_4_), channel_id=1, source_target_pairs={{0,4},{2,6},{4,0},{6,2},{1,5},{3,7},{5,1},{7,3},{8,12},{10,14},{12... | collective-permute-start | bytes 393224 | tf_op jit(solution)/shard_map/ppermute | solution.py:28
  15.6 8.9 %collective-permute-start.6 = (bf16[256,256]{1,0:T(8,128)(2,1)S(1)}, bf16[256,256]{1,0:T(8,128)(2,1)S(1)}, u32[]{:S(2)}, u32[]{:S(2)}) collective-permute-start(bf16[256,256]{1,0:T(8,128)(2,1)S(1)} %shard_map.78.refs_4_), channel_id=1, source_target_pairs={{0,2},{2,0},{4,6},{6,4},{1,3},{3,1},{5,7},{7,5},{8,10},{10,8},{12,... | collective-permute-start | bytes 393224 | tf_op jit(solution)/shard_map/ppermute | solution.py:28
  17.8 8.6 %collective-permute-start.5 = (bf16[2,64,1024]{2,1,0:T(8,128)(2,1)S(1)}, bf16[2,64,1024]{2,1,0:T(8,128)(2,1)S(1)}, u32[]{:S(2)}, u32[]{:S(2)}) collective-permute-start(bf16[2,64,1024]{2,1,0:T(8,128)(2,1)S(1)} %get-tuple-element.67), channel_id=1, source_target_pairs={{0,24},{8,16},{16,8},{24,0},{1,25},{9,17},{17,9},{25,1},{2,26},{10... | collective-permute-start | bytes 786440 | tf_op jit(solution)/shard_map/ppermute | solution.py:28
  19.6 5.4 %collective-permute-start.12 = (bf16[256,256]{1,0:T(8,128)(2,1)S(1)}, bf16[256,256]{1,0:T(8,128)(2,1)S(1)}, u32[]{:S(2)}, u32[]{:S(2)}) collective-permute-start(bf16[256,256]{1,0:T(8,128)(2,1)S(1)} %collective-permute-done.8.refs_7_), channel_id=1, source_target_pairs={{0,1},{1,0},{2,3},{3,2},{4,5},{5,4},{6,7},{7,6},{8,9},{9,8},{10,11... | collective-permute-start | bytes 393224 | tf_op jit(solution)/shard_map/ppermute | solution.py:28
  24.5 1.3 %collective-permute-start.11 = (bf16[256,256]{1,0:T(8,128)(2,1)S(1)}, bf16[256,256]{1,0:T(8,128)(2,1)S(1)}, u32[]{:S(2)}, u32[]{:S(2)}) collective-permute-start(bf16[256,256]{1,0:T(8,128)(2,1)S(1)} %collective-permute-done.7.refs_6_), channel_id=1, source_target_pairs={{0,1},{1,0},{2,3},{3,2},{4,5},{5,4},{6,7},{7,6},{8,9},{9,8},{10,11... | collective-permute-start | bytes 393224 | tf_op jit(solution)/shard_map/ppermute | solution.py:28
  24.5 1.5 %collective-permute-start.10 = (bf16[256,256]{1,0:T(8,128)(2,1)S(1)}, bf16[256,256]{1,0:T(8,128)(2,1)S(1)}, u32[]{:S(2)}, u32[]{:S(2)}) collective-permute-start(bf16[256,256]{1,0:T(8,128)(2,1)S(1)} %collective-permute-done.6.refs_5_), channel_id=1, source_target_pairs={{0,1},{1,0},{2,3},{3,2},{4,5},{5,4},{6,7},{7,6},{8,9},{9,8},{10,11... | collective-permute-start | bytes 393224 | tf_op jit(solution)/shard_map/ppermute | solution.py:28
  25.0 1.3 %collective-permute-start.9 = (bf16[256,256]{1,0:T(8,128)(2,1)S(1)}, bf16[256,256]{1,0:T(8,128)(2,1)S(1)}, u32[]{:S(2)}, u32[]{:S(2)}) collective-permute-start(bf16[256,256]{1,0:T(8,128)(2,1)S(1)} %shard_map.78.refs_4_), channel_id=1, source_target_pairs={{0,1},{1,0},{2,3},{3,2},{4,5},{5,4},{6,7},{7,6},{8,9},{9,8},{10,11... | collective-permute-start | bytes 393224 | tf_op jit(solution)/shard_map/ppermute | solution.py:28
  36.4 2.0 %collective-permute-start.16 = (bf16[1024,256]{1,0:T(8,128)(2,1)S(1)}, bf16[1024,256]{1,0:T(8,128)(2,1)S(1)}, u32[]{:S(2)}, u32[]{:S(2)}) collective-permute-start(bf16[1024,256]{1,0:T(8,128)(2,1)S(1)} %get-tuple-element.78), channel_id=1, source_target_pairs={{0,1},{1,0},{2,3},{3,2},{4,5},{5,4},{6,7},{7,6},{8,9},{9,8},{10,11... | collective-permute-start | bytes 1572872 | tf_op jit(solution)/shard_map/ppermute | solution.py:28
  38.5 7.9 %collective-permute-start.17 = (bf16[256,256]{1,0:T(8,128)(2,1)S(1)}, bf16[256,256]{1,0:T(8,128)(2,1)S(1)}, u32[]{:S(2)}, u32[]{:S(2)}) collective-permute-start(bf16[256,256]{1,0:T(8,128)(2,1)S(1)} %get-tuple-element.80), channel_id=1, source_target_pairs={{0,2},{2,0},{4,6},{6,4},{1,3},{3,1},{5,7},{7,5},{8,10},{10,8},{12,... | collective-permute-start | bytes 393224 | tf_op jit(solution)/shard_map/ppermute | solution.py:28
  38.9 12.9 %collective-permute-start.18 = (bf16[256,256]{1,0:T(8,128)(2,1)S(1)}, bf16[256,256]{1,0:T(8,128)(2,1)S(1)}, u32[]{:S(2)}, u32[]{:S(2)}) collective-permute-start(bf16[256,256]{1,0:T(8,128)(2,1)S(1)} %get-tuple-element.81), channel_id=1, source_target_pairs={{0,4},{2,6},{4,0},{6,2},{1,5},{3,7},{5,1},{7,3},{8,12},{10,14},{12... | collective-permute-start | bytes 393224 | tf_op jit(solution)/shard_map/ppermute | solution.py:28
  41.7 10.2 %collective-permute-start.19 = (bf16[256,256]{1,0:T(8,128)(2,1)S(1)}, bf16[256,256]{1,0:T(8,128)(2,1)S(1)}, u32[]{:S(2)}, u32[]{:S(2)}) collective-permute-start(bf16[256,256]{1,0:T(8,128)(2,1)S(1)} %get-tuple-element.82), channel_id=1, source_target_pairs={{0,6},{2,4},{4,2},{6,0},{1,7},{3,5},{5,3},{7,1},{8,14},{10,12},{12... | collective-permute-start | bytes 393224 | tf_op jit(solution)/shard_map/ppermute | solution.py:28
  43.0 11.7 %collective-permute-start.13 = (bf16[64,1024]{1,0:T(8,128)(2,1)S(1)}, bf16[64,1024]{1,0:T(8,128)(2,1)S(1)}, u32[]{:S(2)}, u32[]{:S(2)}) collective-permute-start(bf16[64,1024]{1,0:T(8,128)(2,1)S(1)} %get-tuple-element.74), channel_id=1, source_target_pairs={{0,8},{8,0},{16,24},{24,16},{1,9},{9,1},{17,25},{25,17},{2,10},{10... | collective-permute-start | bytes 393224 | tf_op jit(solution)/shard_map/ppermute | solution.py:28
  44.4 11.0 %collective-permute-start.14 = (bf16[64,1024]{1,0:T(8,128)(2,1)S(1)}, bf16[64,1024]{1,0:T(8,128)(2,1)S(1)}, u32[]{:S(2)}, u32[]{:S(2)}) collective-permute-start(bf16[64,1024]{1,0:T(8,128)(2,1)S(1)} %get-tuple-element.75), channel_id=1, source_target_pairs={{0,16},{8,24},{16,0},{24,8},{1,17},{9,25},{17,1},{25,9},{2,18},{10... | collective-permute-start | bytes 393224 | tf_op jit(solution)/shard_map/ppermute | solution.py:28
  46.4 9.1 %collective-permute-start.15 = (bf16[64,1024]{1,0:T(8,128)(2,1)S(1)}, bf16[64,1024]{1,0:T(8,128)(2,1)S(1)}, u32[]{:S(2)}, u32[]{:S(2)}) collective-permute-start(bf16[64,1024]{1,0:T(8,128)(2,1)S(1)} %get-tuple-element.76), channel_id=1, source_target_pairs={{0,24},{8,16},{16,8},{24,0},{1,25},{9,17},{17,9},{25,1},{2,26},{10... | collective-permute-start | bytes 393224 | tf_op jit(solution)/shard_map/ppermute | solution.py:28
  51.9 4.4 %collective-permute-start.20 = (bf16[64,256]{1,0:T(8,128)(2,1)S(1)}, bf16[64,256]{1,0:T(8,128)(2,1)S(1)}, u32[]{:S(2)}, u32[]{:S(2)}) collective-permute-start(bf16[64,256]{1,0:T(8,128)(2,1)S(1)} %get-tuple-element.84), channel_id=1, source_target_pairs={{0,8},{8,0},{16,24},{24,16},{1,9},{9,1},{17,25},{25,17},{2,10},{10... | collective-permute-start | bytes 98312 | tf_op jit(solution)/shard_map/ppermute | solution.py:28
  53.4 3.9 %collective-permute-start.21 = (bf16[64,256]{1,0:T(8,128)(2,1)S(1)}, bf16[64,256]{1,0:T(8,128)(2,1)S(1)}, u32[]{:S(2)}, u32[]{:S(2)}) collective-permute-start(bf16[64,256]{1,0:T(8,128)(2,1)S(1)} %get-tuple-element.85), channel_id=1, source_target_pairs={{0,16},{8,24},{16,0},{24,8},{1,17},{9,25},{17,1},{25,9},{2,18},{10... | collective-permute-start | bytes 98312 | tf_op jit(solution)/shard_map/ppermute | solution.py:28
  54.7 4.8 %collective-permute-start.22 = (bf16[64,256]{1,0:T(8,128)(2,1)S(1)}, bf16[64,256]{1,0:T(8,128)(2,1)S(1)}, u32[]{:S(2)}, u32[]{:S(2)}) collective-permute-start(bf16[64,256]{1,0:T(8,128)(2,1)S(1)} %get-tuple-element.86), channel_id=1, source_target_pairs={{0,24},{8,16},{16,8},{24,0},{1,25},{9,17},{17,9},{25,1},{2,26},{10... | collective-permute-start | bytes 98312 | tf_op jit(solution)/shard_map/ppermute | solution.py:28

commit v4 on v3

--- a/solution.py
+++ b/solution.py
@@ -57,16 +57,18 @@
     )(*arrays)
 
 
-def pack(heads, *refs):
-    ins, outs, sem = refs[:2], refs[2:-1], refs[-1]
+def pack(heads, count, *refs):
+    ins, outs, sem = refs[:count], refs[count:-1], refs[-1]
     me = lax.axis_index("head")
     width = ins[0].shape[1] // heads
     copies = []
-    for i, out in enumerate(outs):
+    for i, out in enumerate(outs[:heads]):
         columns = pl.ds(pl.multiple_of((me ^ i) * width, width), width)
-        for j, ref in enumerate(ins):
+        for j, ref in enumerate(ins[:2]):
             part = out.at[j] if len(out.shape) == 3 else out.at[:, j * width : (j + 1) * width]
             copies.append(pltpu.make_async_copy(ref.at[:, columns], part, sem.at[i, j]))
+    for n, (ref, out) in enumerate(zip(ins[2:], outs[heads:])):
+        copies.append(pltpu.make_async_copy(ref, out, sem.at[heads + n, 0]))
     for copy in copies:
         copy.start()
     for copy in copies:
@@ -81,14 +83,18 @@
         out[pl.ds(pl.multiple_of((me ^ i) * rows, rows), rows), :] = ref[...]
 
 
-def main_body(heads, inner, outer, rows_now, order_ref, *refs):
+def main_body(heads, inner, outer, rows_now, late, order_ref, *refs):
     it = iter(refs)
     qg = [next(it) for _ in range(heads)]
     bundles = [[next(it) for _ in range(inner)] for _ in range(outer)]
-    dq_outs = [next(it) for _ in range(heads)]
     same_out = next(it)
     other_outs = [next(it) for _ in range(outer - 1)]
-    keys, values, queries, grads, key_t, s_ref, p_ref, dk_ref, dv_ref, dq_ref = it
+    if late:
+        ds_out, keys, level_ref = next(it), next(it), next(it)
+        values, queries, grads, s_ref, p_ref, dk_ref, dv_ref = it
+    else:
+        ds_out, dq_outs = None, [next(it) for _ in range(heads)]
+        values, queries, grads, s_ref, p_ref, dk_ref, dv_ref, keys, key_t, dq_ref = it
 
     block = qg[0].shape[1]
     ranks = inner * outer
@@ -115,13 +121,15 @@
             queries[level_of[i], rows, :] = qg[i][0, :, cols]
             grads[level_of[i], rows, :] = qg[i][1, :, cols]
 
-    for c in range(heads):
-        key_t[:, c * chunk : (c + 1) * chunk] = keys[c * chunk : (c + 1) * chunk, :].T
-
-    dk_ref[...] = jnp.zeros_like(dk_ref)
-    dv_ref[...] = jnp.zeros_like(dv_ref)
+    if not late:
+        for c in range(heads):
+            key_t[:, c * chunk : (c + 1) * chunk] = keys[c * chunk : (c + 1) * chunk, :].T
+
     all_rows = GROUP * block
-    for level in range(heads):
+    if rows_now < all_rows:
+        dk_ref[...] = jnp.zeros_like(dk_ref)
+        dv_ref[...] = jnp.zeros_like(dv_ref)
+    for level in reversed(range(heads)):
         position = sum(jnp.where(level_of[i] == level, place[i], 0) for i in range(heads))
         shift = position * block - level * chunk
 
@@ -158,23 +166,30 @@
             for c in range(level + 1):
                 span = slice(c * chunk, (c + 1) * chunk)
                 p = s_ref[span, :] * inverse
-                dv_ref[span, :] += dot(g_t, p.astype(jnp.bfloat16), NT).T
+                first = level == heads - 1 and rows_now == all_rows
+                part = dot(g_t, p.astype(jnp.bfloat16), NT).T
+                dv_ref[span, :] = part if first else dv_ref[span, :] + part
                 ds = (p * (p_ref[span, :] - dots)).astype(jnp.bfloat16)
-                dk_ref[span, :] += dot(ds, q, NN)
+                part = dot(ds, q, NN)
+                dk_ref[span, :] = part if first else dk_ref[span, :] + part
+                if ds_out is not None:
+                    ds_out[level * (level + 1) // 2 + c] = ds
+                    continue
                 part = dot(key_t[:, span], ds, NN)
                 dq = part if dq is None else dq + part
-            dq_ref[level, here, :] = (dq * SCALE).T.astype(jnp.bfloat16)
+            if ds_out is None:
+                dq_ref[level, here, :] = (dq * SCALE).T.astype(jnp.bfloat16)
 
         if all_rows == rows_now:
             visit(0)
         else:
             pl.loop(0, all_rows // rows_now)(visit)
 
-    for i in range(heads):
-        for g in range(GROUP):
-            dq_outs[i][:, g * HEAD_DIM : (g + 1) * HEAD_DIM] = dq_ref[
-                level_of[i], g * block : (g + 1) * block, :
-            ]
+    if late:
+        for i in range(heads):
+            level_ref[i] = jnp.full(level_ref.shape[1:], level_of[i], jnp.int32)
+    else:
+        hand_out(dq_outs, dq_ref, level_of)
     for e in range(outer):
         out = same_out if e == 0 else other_outs[e - 1]
         for s in range(inner):
@@ -186,27 +201,73 @@
                 out[rows, HEAD_DIM:] = dv_ref[at, :].astype(out.dtype)
 
 
+def hand_out(dq_outs, dq_ref, level_of):
+    block = dq_outs[0].shape[0]
+    for out, level in zip(dq_outs, level_of):
+        for g in range(GROUP):
+            out[:, g * HEAD_DIM : (g + 1) * HEAD_DIM] = dq_ref[level, g * block : (g + 1) * block, :]
+
+
+def query_body(heads, ds_ref, keys, level_ref, *dq_outs):
+    chunk = ds_ref.shape[1]
+    block = dq_outs[0].shape[0]
+    by_level = []
+    key_t = [keys[c * chunk : (c + 1) * chunk, :].T for c in range(heads)]
+    for level in range(heads):
+        dq = None
+        for c in range(level + 1):
+            ds = ds_ref[level * (level + 1) // 2 + c]
+            part = dot(key_t[c], ds, NN)
+            dq = part if dq is None else dq + part
+        by_level.append((dq * SCALE).T)
+    for i, out in enumerate(dq_outs):
+        for g in range(GROUP):
+            rows = slice(g * block, (g + 1) * block)
+            piece = by_level[0][rows, :]
+            for level in range(1, heads):
+                piece = jnp.where(level_ref[i] == level, by_level[level][rows, :], piece)
+            out[:, g * HEAD_DIM : (g + 1) * HEAD_DIM] = piece.astype(out.dtype)
+
+
 def attend(qg, bundles, block_order, rows_now):
     heads, inner, outer = (lax.axis_size(n) for n in ("head", "inner", "outer"))
     block = qg[0].shape[1]
-    tokens = heads * inner * outer * block
+    chunk = inner * outer * block
+    tokens = heads * chunk
     rows = GROUP * block
+    steps = heads * (heads + 1) // 2
     bf16, f32, V = jnp.bfloat16, jnp.float32, pltpu.VMEM
-    return call(
-        functools.partial(main_body, heads, inner, outer, rows_now),
-        [((block, GROUP * HEAD_DIM), bf16, V)] * heads
-        + [((inner * heads * block, 2 * HEAD_DIM), bf16, V)] * outer,
+    late = rows_now == rows
+    dq_outs = [((block, GROUP * HEAD_DIM), bf16, V)] * heads
+    outs = [((inner * heads * block, 2 * HEAD_DIM), bf16, V)] * outer
+    kept = [
+        ((steps, chunk, rows), bf16, V), ((tokens, HEAD_DIM), bf16, V), ((heads, block, HEAD_DIM), jnp.int32, V)
+    ]
+    scratch = [
+        V((tokens, HEAD_DIM), bf16),
+        V((heads, rows, HEAD_DIM), bf16), V((heads, rows, HEAD_DIM), bf16),
+        V((tokens, rows_now), f32), V((tokens, rows_now), f32),
+        V((tokens, HEAD_DIM), f32), V((tokens, HEAD_DIM), f32),
+    ]
+    results = call(
+        functools.partial(main_body, heads, inner, outer, rows_now, late),
+        outs + (kept if late else dq_outs),
         [(block_order, pltpu.SMEM)] + [(x, V) for x in qg + bundles],
-        [
-            V((tokens, HEAD_DIM), bf16), V((tokens, HEAD_DIM), bf16),
-            V((heads, rows, HEAD_DIM), bf16), V((heads, rows, HEAD_DIM), bf16),
-            V((HEAD_DIM, tokens), bf16),
-            V((tokens, rows_now), f32), V((tokens, rows_now), f32),
-            V((tokens, HEAD_DIM), f32), V((tokens, HEAD_DIM), f32),
-            V((heads, rows, HEAD_DIM), bf16),
-        ],
+        scratch + ([] if late else [
+            V((tokens, HEAD_DIM), bf16), V((HEAD_DIM, tokens), bf16), V((heads, rows, HEAD_DIM), bf16)
+        ]),
         limit=24 if tokens <= 2048 else 44,
     )
+    if not late:
+        return results[:outer], lambda *after: results[outer:]
+
+    def query_grads(*after):
+        (ds, *others), _ = lax.optimization_barrier((results[outer:], after))
+        return call(
+            functools.partial(query_body, heads), dq_outs, [(x, V) for x in (ds, *others)]
+        )
+
+    return results[:outer], query_grads
 
 
 def sum_cores(parts, *refs):
@@ -268,13 +329,15 @@
 
     H = pltpu.HBM
     kv_packed = call(
-        functools.partial(pack, heads),
+        functools.partial(pack, heads, 2),
         [((block, pair), bf16, V)] * heads, [(keys, H), (values, H)], [dma((heads, 2))],
     )
     kv_packed, queries, grad_out = lax.optimization_barrier((kv_packed, queries, grad_out))
-    qg_packed = call(
-        functools.partial(pack, heads),
-        [((2, block, width), bf16, V)] * heads, [(queries, H), (grad_out, H)], [dma((heads, 2))],
+    *qg_packed, block_order = call(
+        functools.partial(pack, heads, 3),
+        [((2, block, width), bf16, V)] * heads + [(block_order.shape, block_order.dtype, V)],
+        [(queries, H), (grad_out, H), (block_order, H)],
+        [dma((heads + 1, 2))],
     )
     far_first = list(reversed(range(1, heads)))
     kv_got = trade(kv_packed, "head", far_first)
@@ -292,15 +355,15 @@
         bundles += [exchange(x, "outer", e) for x in [early] + same[1:]]
 
     rows_now = GROUP * block if chunk <= 512 else GROUP * block // 2
-    results = attend(qg, bundles, block_order, rows_now)
-    dq_parts, same_part, other_parts = results[:heads], results[heads], results[heads + 1 :]
-    core_parts = [same_part] + [exchange(x, "outer", e + 1) for e, x in enumerate(other_parts)]
+    shares, query_grads = attend(qg, bundles, block_order, rows_now)
+    core_parts = [shares[0]] + [exchange(x, "outer", e + 1) for e, x in enumerate(shares[1:])]
     sums = call(
         functools.partial(sum_cores, outer),
         [((heads * block, pair), bf16, V)] * inner,
         [(x, V) for x in core_parts],
     )
     inner_parts = [sums[0]] + [exchange(sums[s], "inner", s) for s in range(1, inner)]
+    dq_parts = query_grads(sums)
     dq_got = [dq_parts[0]] + [exchange(dq_parts[i], "head", i) for i in range(1, heads)]
     back = call(
         functools.partial(sum_inner, inner),

time: 60.4 us -> 59.8 us (0.990)
    pallas_call x8 -> x9, Pallas kernels: 14.1 us -> 14.5 us  [call(): pl.pallas_call(body, out_shape=shapes, in_specs=in_specs, out_specs=out_s...]
  transfers between devices with their start and end apart: 23 -> 23, of which waited for: 14 -> 13; matrix products, arithmetic and copies ran while one was open for 0% -> 0% of each run, Pallas kernels for 4% -> 6%
where the time goes in v4:
time: 59.8 us; the launch traced here: 59.6 us
  starting transfers between devices  25 us (42%)
  waiting for transfers between devices  19.4 us (32%)
  Pallas kernels  14.5 us (24%)
  between operations  0.72 us (1%)
    ppermute x23, starting transfers between devices, exchange(): return lax.ppermute(array, axis, [(i, i ^ by) for i in range(length)])  25 us
    ppermute x23, waiting for transfers between devices, exchange(): return lax.ppermute(array, axis, [(i, i ^ by) for i in range(length)])  19.4 us
    pallas_call x9, Pallas kernels, call(): pl.pallas_call(body, out_shape=shapes, in_specs=in_specs, out_specs=out_s...  14.5 us
  transfers between devices with their start and end apart: 23, of which 13 were waited for; matrix products, arithmetic and copies ran while one was open for 0% of the time, Pallas kernels for 6%

profile of v4, /device:TPU:0, one launch (start us, length us, event | category | flops | bytes accessed | tf_op | source)
XLA Modules:
  0.0 59.6 jit_solution(4319146938800881488)
XLA Ops:
  0.6 0.9 %shard_map.76 = (bf16[64,256]{1,0:T(8,128)(2,1)S(1)}, bf16[64,256]{1,0:T(8,128)(2,1)S(1)}, bf16[64,256]{1,0:T(8,128)(2,1)S(1)}, bf16[64,256]{1,0:T(8,128)(2,1)S(1)}) custom-call(bf16[64,512]{1,0:T(8,128)(2,1)} %refs_0_.1, bf16[64,512]{1,0:T(8,128)(2,1)} %refs_1_.1), custom_call_target="tpu_custom_call" | custom-call | tf_op jit(solution)/shard_map/pallas_call | solution.py:50
  1.6 3.0 %collective-permute-start = (bf16[64,256]{1,0:T(8,128)(2,1)S(1)}, bf16[64,256]{1,0:T(8,128)(2,1)S(1)}, u32[]{:S(2)}, u32[]{:S(2)}) collective-permute-start(bf16[64,256]{1,0:T(8,128)(2,1)S(1)} %get-tuple-element.61), channel_id=1, source_target_pairs={{0,8},{8,0},{16,24},{24,16},{1,9},{9,1},{17,25},{25,17},{2,10},{10... | collective-permute-start | bytes 98312 | tf_op jit(solution)/shard_map/ppermute | solution.py:28
  4.6 1.5 %collective-permute-start.1 = (bf16[64,256]{1,0:T(8,128)(2,1)S(1)}, bf16[64,256]{1,0:T(8,128)(2,1)S(1)}, u32[]{:S(2)}, u32[]{:S(2)}) collective-permute-start(bf16[64,256]{1,0:T(8,128)(2,1)S(1)} %get-tuple-element.62), channel_id=1, source_target_pairs={{0,16},{8,24},{16,0},{24,8},{1,17},{9,25},{17,1},{25,9},{2,18},{10... | collective-permute-start | bytes 98312 | tf_op jit(solution)/shard_map/ppermute | solution.py:28
  6.1 0.0 collective-permute-start.2
  6.1 1.4 %shard_map.77 = (bf16[2,64,1024]{2,1,0:T(8,128)(2,1)S(1)}, bf16[2,64,1024]{2,1,0:T(8,128)(2,1)S(1)}, bf16[2,64,1024]{2,1,0:T(8,128)(2,1)S(1)}, bf16[2,64,1024]{2,1,0:T(8,128)(2,1)S(1)}, s32[32]{0:T(128)S(1)}) custom-call(bf16[64,4096]{1,0:T(8,128)(2,1)} %refs_0_.2, bf16[64,4096]{1,0:T(8,128)(2,1)} %refs_1_.2, s32[32]{0:T(128)} %refs_2_.1), custom_call_target="tpu_custom_call" | custom-call | tf_op jit(solution)/shard_map/pallas_call | solution.py:50
  7.5 0.0 collective-permute-done.refs_1_
  7.5 1.0 %collective-permute-done.1.refs_2_ = bf16[64,256]{1,0:T(8,128)(2,1)S(1)} collective-permute-done((bf16[64,256]{1,0:T(8,128)(2,1)S(1)}, bf16[64,256]{1,0:T(8,128)(2,1)S(1)}, u32[]{:S(2)}, u32[]{:S(2)}) %collective-permute-start.1) | collective-permute-done | bytes 32800 | tf_op jit(solution)/shard_map/ppermute | solution.py:28
  8.5 2.4 %collective-permute-done.2.refs_3_ = bf16[64,256]{1,0:T(8,128)(2,1)S(1)} collective-permute-done((bf16[64,256]{1,0:T(8,128)(2,1)S(1)}, bf16[64,256]{1,0:T(8,128)(2,1)S(1)}, u32[]{:S(2)}, u32[]{:S(2)}) %collective-permute-start.2) | collective-permute-done | bytes 32800 | tf_op jit(solution)/shard_map/ppermute | solution.py:28
  10.9 0.5 collective-permute-start.3
  11.4 0.1 collective-permute-start.4
  11.5 4.1 %collective-permute-start.8 = (bf16[256,256]{1,0:T(8,128)(2,1)S(1)}, bf16[256,256]{1,0:T(8,128)(2,1)S(1)}, u32[]{:S(2)}, u32[]{:S(2)}) collective-permute-start(bf16[256,256]{1,0:T(8,128)(2,1)S(1)} %shard_map.78.refs_4_), channel_id=1, source_target_pairs={{0,6},{2,4},{4,2},{6,0},{1,7},{3,5},{5,3},{7,1},{8,14},{10,12},{12... | collective-permute-start | bytes 393224 | tf_op jit(solution)/shard_map/ppermute | solution.py:28
  15.6 0.0 collective-permute-start.7
  15.6 0.6 %collective-permute-start.6 = (bf16[256,256]{1,0:T(8,128)(2,1)S(1)}, bf16[256,256]{1,0:T(8,128)(2,1)S(1)}, u32[]{:S(2)}, u32[]{:S(2)}) collective-permute-start(bf16[256,256]{1,0:T(8,128)(2,1)S(1)} %shard_map.78.refs_4_), channel_id=1, source_target_pairs={{0,2},{2,0},{4,6},{6,4},{1,3},{3,1},{5,7},{7,5},{8,10},{10,8},{12,... | collective-permute-start | bytes 393224 | tf_op jit(solution)/shard_map/ppermute | solution.py:28
  16.3 1.0 %collective-permute-done.3.refs_1_ = bf16[2,64,1024]{2,1,0:T(8,128)(2,1)S(1)} collective-permute-done((bf16[2,64,1024]{2,1,0:T(8,128)(2,1)S(1)}, bf16[2,64,1024]{2,1,0:T(8,128)(2,1)S(1)}, u32[]{:S(2)}, u32[]{:S(2)}) %collective-permute-start.3) | collective-permute-done | bytes 262176 | tf_op jit(solution)/shard_map/ppermute | solution.py:28
  17.3 0.5 collective-permute-done.4.refs_2_
  17.8 1.4 %collective-permute-start.5 = (bf16[2,64,1024]{2,1,0:T(8,128)(2,1)S(1)}, bf16[2,64,1024]{2,1,0:T(8,128)(2,1)S(1)}, u32[]{:S(2)}, u32[]{:S(2)}) collective-permute-start(bf16[2,64,1024]{2,1,0:T(8,128)(2,1)S(1)} %get-tuple-element.75), channel_id=1, source_target_pairs={{0,24},{8,16},{16,8},{24,0},{1,25},{9,17},{17,9},{25,1},{2,26},{10... | collective-permute-start | bytes 786440 | tf_op jit(solution)/shard_map/ppermute | solution.py:28
  19.2 0.3 collective-permute-done.8.refs_7_
  19.6 0.0 collective-permute-start.12
  19.6 4.9 %collective-permute-done.7.refs_6_ = bf16[256,256]{1,0:T(8,128)(2,1)S(1)} collective-permute-done((bf16[256,256]{1,0:T(8,128)(2,1)S(1)}, bf16[256,256]{1,0:T(8,128)(2,1)S(1)}, u32[]{:S(2)}, u32[]{:S(2)}) %collective-permute-start.7) | collective-permute-done | bytes 131104 | tf_op jit(solution)/shard_map/ppermute | solution.py:28
  24.5 0.0 collective-permute-start.11
  24.5 0.5 collective-permute-start.10
  25.0 0.0 collective-permute-start.9
  25.0 0.0 collective-permute-done.12.refs_11_
  25.0 0.8 %collective-permute-done.11.refs_10_ = bf16[256,256]{1,0:T(8,128)(2,1)S(1)} collective-permute-done((bf16[256,256]{1,0:T(8,128)(2,1)S(1)}, bf16[256,256]{1,0:T(8,128)(2,1)S(1)}, u32[]{:S(2)}, u32[]{:S(2)}) %collective-permute-start.11) | collective-permute-done | bytes 131104 | tf_op jit(solution)/shard_map/ppermute | solution.py:28
  25.8 0.2 collective-permute-done.10.refs_9_
  26.0 0.3 collective-permute-done.9.refs_8_
  26.4 0.0 collective-permute-done.5.refs_3_
  26.4 9.4 %shard_map.79 = (bf16[1024,256]{1,0:T(8,128)(2,1)S(1)}, bf16[1024,256]{1,0:T(8,128)(2,1)S(1)}, bf16[10,512,512]{2,1,0:T(8,128)(2,1)S(1)}, bf16[2048,128]{1,0:T(8,128)(2,1)S(1)}, s32[4,64,128]{2,1,0:T(8,128)S(1)}) custom-call(s32[32]{0:T(128)S(1)} %get-tuple-element.59.order_ref, bf16[2,64,1024]{2,1,0:T(8,128)(2,1)S(1)} %get-tuple-element.72.refs_0_, ...), custom_call_target="tpu_custom_call" | custom-call | tf_op jit(solution)/shard_map/pallas_call | solution.py:50
  35.8 0.3 collective-permute-start.13
  36.0 1.7 %collective-permute-done.13.refs_1_ = bf16[1024,256]{1,0:T(8,128)(2,1)S(1)} collective-permute-done((bf16[1024,256]{1,0:T(8,128)(2,1)S(1)}, bf16[1024,256]{1,0:T(8,128)(2,1)S(1)}, u32[]{:S(2)}, u32[]{:S(2)}) %collective-permute-start.13) | collective-permute-done | bytes 524320 | tf_op jit(solution)/shard_map/ppermute | solution.py:28
  37.8 0.1 shard_map.80
  37.9 0.4 collective-permute-start.17
  38.3 2.7 %collective-permute-start.18 = (bf16[256,256]{1,0:T(8,128)(2,1)S(1)}, bf16[256,256]{1,0:T(8,128)(2,1)S(1)}, u32[]{:S(2)}, u32[]{:S(2)}) collective-permute-start(bf16[256,256]{1,0:T(8,128)(2,1)S(1)} %get-tuple-element.88), channel_id=1, source_target_pairs={{0,4},{2,6},{4,0},{6,2},{1,5},{3,7},{5,1},{7,3},{8,12},{10,14},{12... | collective-permute-start | bytes 393224 | tf_op jit(solution)/shard_map/ppermute | solution.py:28
  41.0 1.3 %collective-permute-start.19 = (bf16[256,256]{1,0:T(8,128)(2,1)S(1)}, bf16[256,256]{1,0:T(8,128)(2,1)S(1)}, u32[]{:S(2)}, u32[]{:S(2)}) collective-permute-start(bf16[256,256]{1,0:T(8,128)(2,1)S(1)} %get-tuple-element.89), channel_id=1, source_target_pairs={{0,6},{2,4},{4,2},{6,0},{1,7},{3,5},{5,3},{7,1},{8,14},{10,12},{12... | collective-permute-start | bytes 393224 | tf_op jit(solution)/shard_map/ppermute | solution.py:28
  42.3 1.0 %shard_map.81 = (bf16[64,1024]{1,0:T(8,128)(2,1)S(1)}, bf16[64,1024]{1,0:T(8,128)(2,1)S(1)}, bf16[64,1024]{1,0:T(8,128)(2,1)S(1)}, bf16[64,1024]{1,0:T(8,128)(2,1)S(1)}) custom-call(bf16[10,512,512]{2,1,0:T(8,128)(2,1)S(1)} %get-tuple-element.90.ds_ref, bf16[2048,128]{1,0:T(8,128)(2,1)S(1)} %get-tuple-element.91.keys, ...), custom_call_target="tpu_custom_call" | custom-call | tf_op jit(solution)/shard_map/pallas_call | solution.py:50
  43.4 1.5 %collective-permute-start.14 = (bf16[64,1024]{1,0:T(8,128)(2,1)S(1)}, bf16[64,1024]{1,0:T(8,128)(2,1)S(1)}, u32[]{:S(2)}, u32[]{:S(2)}) collective-permute-start(bf16[64,1024]{1,0:T(8,128)(2,1)S(1)} %get-tuple-element.94), channel_id=1, source_target_pairs={{0,8},{8,0},{16,24},{24,16},{1,9},{9,1},{17,25},{25,17},{2,10},{10... | collective-permute-start | bytes 393224 | tf_op jit(solution)/shard_map/ppermute | solution.py:28
  44.9 1.5 %collective-permute-start.15 = (bf16[64,1024]{1,0:T(8,128)(2,1)S(1)}, bf16[64,1024]{1,0:T(8,128)(2,1)S(1)}, u32[]{:S(2)}, u32[]{:S(2)}) collective-permute-start(bf16[64,1024]{1,0:T(8,128)(2,1)S(1)} %get-tuple-element.95), channel_id=1, source_target_pairs={{0,16},{8,24},{16,0},{24,8},{1,17},{9,25},{17,1},{25,9},{2,18},{10... | collective-permute-start | bytes 393224 | tf_op jit(solution)/shard_map/ppermute | solution.py:28
  46.4 1.8 %collective-permute-start.16 = (bf16[64,1024]{1,0:T(8,128)(2,1)S(1)}, bf16[64,1024]{1,0:T(8,128)(2,1)S(1)}, u32[]{:S(2)}, u32[]{:S(2)}) collective-permute-start(bf16[64,1024]{1,0:T(8,128)(2,1)S(1)} %get-tuple-element.96), channel_id=1, source_target_pairs={{0,24},{8,16},{16,8},{24,0},{1,25},{9,17},{17,9},{25,1},{2,26},{10... | collective-permute-start | bytes 393224 | tf_op jit(solution)/shard_map/ppermute | solution.py:28
  48.3 2.9 %collective-permute-done.18.refs_2_ = bf16[256,256]{1,0:T(8,128)(2,1)S(1)} collective-permute-done((bf16[256,256]{1,0:T(8,128)(2,1)S(1)}, bf16[256,256]{1,0:T(8,128)(2,1)S(1)}, u32[]{:S(2)}, u32[]{:S(2)}) %collective-permute-start.18) | collective-permute-done | bytes 131104 | tf_op jit(solution)/shard_map/ppermute | solution.py:28
  51.2 0.1 shard_map.83
  51.3 1.5 %collective-permute-start.20 = (bf16[64,256]{1,0:T(8,128)(2,1)S(1)}, bf16[64,256]{1,0:T(8,128)(2,1)S(1)}, u32[]{:S(2)}, u32[]{:S(2)}) collective-permute-start(bf16[64,256]{1,0:T(8,128)(2,1)S(1)} %get-tuple-element.98), channel_id=1, source_target_pairs={{0,8},{8,0},{16,24},{24,16},{1,9},{9,1},{17,25},{25,17},{2,10},{10... | collective-permute-start | bytes 98312 | tf_op jit(solution)/shard_map/ppermute | solution.py:28
  52.8 1.3 %collective-permute-start.21 = (bf16[64,256]{1,0:T(8,128)(2,1)S(1)}, bf16[64,256]{1,0:T(8,128)(2,1)S(1)}, u32[]{:S(2)}, u32[]{:S(2)}) collective-permute-start(bf16[64,256]{1,0:T(8,128)(2,1)S(1)} %get-tuple-element.99), channel_id=1, source_target_pairs={{0,16},{8,24},{16,0},{24,8},{1,17},{9,25},{17,1},{25,9},{2,18},{10... | collective-permute-start | bytes 98312 | tf_op jit(solution)/shard_map/ppermute | solution.py:28
  54.1 0.0 collective-permute-done.14.refs_1_
  54.1 0.8 %collective-permute-start.22 = (bf16[64,256]{1,0:T(8,128)(2,1)S(1)}, bf16[64,256]{1,0:T(8,128)(2,1)S(1)}, u32[]{:S(2)}, u32[]{:S(2)}) collective-permute-start(bf16[64,256]{1,0:T(8,128)(2,1)S(1)} %get-tuple-element.100), channel_id=1, source_target_pairs={{0,24},{8,16},{16,8},{24,0},{1,25},{9,17},{17,9},{25,1},{2,26},{10... | collective-permute-start | bytes 98312 | tf_op jit(solution)/shard_map/ppermute | solution.py:28
  54.8 0.8 %shard_map.82 = bf16[64,4096]{1,0:T(8,128)(2,1)} custom-call(bf16[64,1024]{1,0:T(8,128)(2,1)S(1)} %get-tuple-element.93.refs_0_, bf16[64,1024]{1,0:T(8,128)(2,1)S(1)} %collective-permute-done.14.refs_1_, bf16[64,1024]{1,0:T(8,128)(2,1)S(1)} %collective-permute-done.15.refs_2_, bf16[64,1024]{1,0:T(8,128)(2,1)S(1)} %collective-permute-done.16.refs_3_), custom_call_target="tpu_custom_call" | custom-call | tf_op jit(solution)/shard_map/pallas_call | solution.py:50
  55.7 1.0 %collective-permute-done.21.refs_2_ = bf16[64,256]{1,0:T(8,128)(2,1)S(1)} collective-permute-done((bf16[64,256]{1,0:T(8,128)(2,1)S(1)}, bf16[64,256]{1,0:T(8,128)(2,1)S(1)}, u32[]{:S(2)}, u32[]{:S(2)}) %collective-permute-start.21) | collective-permute-done | bytes 32800 | tf_op jit(solution)/shard_map/ppermute | solution.py:28
  56.7 2.2 %collective-permute-done.22.refs_3_ = bf16[64,256]{1,0:T(8,128)(2,1)S(1)} collective-permute-done((bf16[64,256]{1,0:T(8,128)(2,1)S(1)}, bf16[64,256]{1,0:T(8,128)(2,1)S(1)}, u32[]{:S(2)}, u32[]{:S(2)}) %collective-permute-start.22) | collective-permute-done | bytes 32800 | tf_op jit(solution)/shard_map/ppermute | solution.py:28
  58.9 0.7 %shard_map.84 = (bf16[64,512]{1,0:T(8,128)(2,1)}, bf16[64,512]{1,0:T(8,128)(2,1)}) custom-call(bf16[64,256]{1,0:T(8,128)(2,1)S(1)} %get-tuple-element.97.refs_0_, bf16[64,256]{1,0:T(8,128)(2,1)S(1)} %collective-permute-done.20.refs_1_, bf16[64,256]{1,0:T(8,128)(2,1)S(1)} %collective-permute-done.21.refs_2_, bf16[64,256]{1,0:T(8,128)(2,1)S(1)} %collective-permute-done.22.refs_3_), custom_call_target="tpu_custom_call" | custom-call | tf_op jit(solution)/shard_map/pallas_call | solution.py:50
  (7 shorter events, 0.0 us)
Async XLA Ops:
  1.6 5.9 %collective-permute-start = (bf16[64,256]{1,0:T(8,128)(2,1)S(1)}, bf16[64,256]{1,0:T(8,128)(2,1)S(1)}, u32[]{:S(2)}, u32[]{:S(2)}) collective-permute-start(bf16[64,256]{1,0:T(8,128)(2,1)S(1)} %get-tuple-element.61), channel_id=1, source_target_pairs={{0,8},{8,0},{16,24},{24,16},{1,9},{9,1},{17,25},{25,17},{2,10},{10... | collective-permute-start | bytes 98312 | tf_op jit(solution)/shard_map/ppermute | solution.py:28
  4.6 3.9 %collective-permute-start.1 = (bf16[64,256]{1,0:T(8,128)(2,1)S(1)}, bf16[64,256]{1,0:T(8,128)(2,1)S(1)}, u32[]{:S(2)}, u32[]{:S(2)}) collective-permute-start(bf16[64,256]{1,0:T(8,128)(2,1)S(1)} %get-tuple-element.62), channel_id=1, source_target_pairs={{0,16},{8,24},{16,0},{24,8},{1,17},{9,25},{17,1},{25,9},{2,18},{10... | collective-permute-start | bytes 98312 | tf_op jit(solution)/shard_map/ppermute | solution.py:28
  6.1 4.8 %collective-permute-start.2 = (bf16[64,256]{1,0:T(8,128)(2,1)S(1)}, bf16[64,256]{1,0:T(8,128)(2,1)S(1)}, u32[]{:S(2)}, u32[]{:S(2)}) collective-permute-start(bf16[64,256]{1,0:T(8,128)(2,1)S(1)} %get-tuple-element.63), channel_id=1, source_target_pairs={{0,24},{8,16},{16,8},{24,0},{1,25},{9,17},{17,9},{25,1},{2,26},{10... | collective-permute-start | bytes 98312 | tf_op jit(solution)/shard_map/ppermute | solution.py:28
  10.9 6.4 %collective-permute-start.3 = (bf16[2,64,1024]{2,1,0:T(8,128)(2,1)S(1)}, bf16[2,64,1024]{2,1,0:T(8,128)(2,1)S(1)}, u32[]{:S(2)}, u32[]{:S(2)}) collective-permute-start(bf16[2,64,1024]{2,1,0:T(8,128)(2,1)S(1)} %get-tuple-element.70), channel_id=1, source_target_pairs={{0,8},{8,0},{16,24},{24,16},{1,9},{9,1},{17,25},{25,17},{2,10},{10... | collective-permute-start | bytes 786440 | tf_op jit(solution)/shard_map/ppermute | solution.py:28
  11.4 6.4 %collective-permute-start.4 = (bf16[2,64,1024]{2,1,0:T(8,128)(2,1)S(1)}, bf16[2,64,1024]{2,1,0:T(8,128)(2,1)S(1)}, u32[]{:S(2)}, u32[]{:S(2)}) collective-permute-start(bf16[2,64,1024]{2,1,0:T(8,128)(2,1)S(1)} %get-tuple-element.71), channel_id=1, source_target_pairs={{0,16},{8,24},{16,0},{24,8},{1,17},{9,25},{17,1},{25,9},{2,18},{10... | collective-permute-start | bytes 786440 | tf_op jit(solution)/shard_map/ppermute | solution.py:28
  11.5 8.1 %collective-permute-start.8 = (bf16[256,256]{1,0:T(8,128)(2,1)S(1)}, bf16[256,256]{1,0:T(8,128)(2,1)S(1)}, u32[]{:S(2)}, u32[]{:S(2)}) collective-permute-start(bf16[256,256]{1,0:T(8,128)(2,1)S(1)} %shard_map.78.refs_4_), channel_id=1, source_target_pairs={{0,6},{2,4},{4,2},{6,0},{1,7},{3,5},{5,3},{7,1},{8,14},{10,12},{12... | collective-permute-start | bytes 393224 | tf_op jit(solution)/shard_map/ppermute | solution.py:28
  15.6 8.9 %collective-permute-start.7 = (bf16[256,256]{1,0:T(8,128)(2,1)S(1)}, bf16[256,256]{1,0:T(8,128)(2,1)S(1)}, u32[]{:S(2)}, u32[]{:S(2)}) collective-permute-start(bf16[256,256]{1,0:T(8,128)(2,1)S(1)} %shard_map.78.refs_4_), channel_id=1, source_target_pairs={{0,4},{2,6},{4,0},{6,2},{1,5},{3,7},{5,1},{7,3},{8,12},{10,14},{12... | collective-permute-start | bytes 393224 | tf_op jit(solution)/shard_map/ppermute | solution.py:28
  15.6 8.9 %collective-permute-start.6 = (bf16[256,256]{1,0:T(8,128)(2,1)S(1)}, bf16[256,256]{1,0:T(8,128)(2,1)S(1)}, u32[]{:S(2)}, u32[]{:S(2)}) collective-permute-start(bf16[256,256]{1,0:T(8,128)(2,1)S(1)} %shard_map.78.refs_4_), channel_id=1, source_target_pairs={{0,2},{2,0},{4,6},{6,4},{1,3},{3,1},{5,7},{7,5},{8,10},{10,8},{12,... | collective-permute-start | bytes 393224 | tf_op jit(solution)/shard_map/ppermute | solution.py:28
  17.8 8.6 %collective-permute-start.5 = (bf16[2,64,1024]{2,1,0:T(8,128)(2,1)S(1)}, bf16[2,64,1024]{2,1,0:T(8,128)(2,1)S(1)}, u32[]{:S(2)}, u32[]{:S(2)}) collective-permute-start(bf16[2,64,1024]{2,1,0:T(8,128)(2,1)S(1)} %get-tuple-element.75), channel_id=1, source_target_pairs={{0,24},{8,16},{16,8},{24,0},{1,25},{9,17},{17,9},{25,1},{2,26},{10... | collective-permute-start | bytes 786440 | tf_op jit(solution)/shard_map/ppermute | solution.py:28
  19.6 5.4 %collective-permute-start.12 = (bf16[256,256]{1,0:T(8,128)(2,1)S(1)}, bf16[256,256]{1,0:T(8,128)(2,1)S(1)}, u32[]{:S(2)}, u32[]{:S(2)}) collective-permute-start(bf16[256,256]{1,0:T(8,128)(2,1)S(1)} %collective-permute-done.8.refs_7_), channel_id=1, source_target_pairs={{0,1},{1,0},{2,3},{3,2},{4,5},{5,4},{6,7},{7,6},{8,9},{9,8},{10,11... | collective-permute-start | bytes 393224 | tf_op jit(solution)/shard_map/ppermute | solution.py:28
  24.5 1.3 %collective-permute-start.11 = (bf16[256,256]{1,0:T(8,128)(2,1)S(1)}, bf16[256,256]{1,0:T(8,128)(2,1)S(1)}, u32[]{:S(2)}, u32[]{:S(2)}) collective-permute-start(bf16[256,256]{1,0:T(8,128)(2,1)S(1)} %collective-permute-done.7.refs_6_), channel_id=1, source_target_pairs={{0,1},{1,0},{2,3},{3,2},{4,5},{5,4},{6,7},{7,6},{8,9},{9,8},{10,11... | collective-permute-start | bytes 393224 | tf_op jit(solution)/shard_map/ppermute | solution.py:28
  24.5 1.5 %collective-permute-start.10 = (bf16[256,256]{1,0:T(8,128)(2,1)S(1)}, bf16[256,256]{1,0:T(8,128)(2,1)S(1)}, u32[]{:S(2)}, u32[]{:S(2)}) collective-permute-start(bf16[256,256]{1,0:T(8,128)(2,1)S(1)} %collective-permute-done.6.refs_5_), channel_id=1, source_target_pairs={{0,1},{1,0},{2,3},{3,2},{4,5},{5,4},{6,7},{7,6},{8,9},{9,8},{10,11... | collective-permute-start | bytes 393224 | tf_op jit(solution)/shard_map/ppermute | solution.py:28
  25.0 1.3 %collective-permute-start.9 = (bf16[256,256]{1,0:T(8,128)(2,1)S(1)}, bf16[256,256]{1,0:T(8,128)(2,1)S(1)}, u32[]{:S(2)}, u32[]{:S(2)}) collective-permute-start(bf16[256,256]{1,0:T(8,128)(2,1)S(1)} %shard_map.78.refs_4_), channel_id=1, source_target_pairs={{0,1},{1,0},{2,3},{3,2},{4,5},{5,4},{6,7},{7,6},{8,9},{9,8},{10,11... | collective-permute-start | bytes 393224 | tf_op jit(solution)/shard_map/ppermute | solution.py:28
  35.8 2.0 %collective-permute-start.13 = (bf16[1024,256]{1,0:T(8,128)(2,1)S(1)}, bf16[1024,256]{1,0:T(8,128)(2,1)S(1)}, u32[]{:S(2)}, u32[]{:S(2)}) collective-permute-start(bf16[1024,256]{1,0:T(8,128)(2,1)S(1)} %get-tuple-element.85), channel_id=1, source_target_pairs={{0,1},{1,0},{2,3},{3,2},{4,5},{5,4},{6,7},{7,6},{8,9},{9,8},{10,11... | collective-permute-start | bytes 1572872 | tf_op jit(solution)/shard_map/ppermute | solution.py:28
  37.9 8.5 %collective-permute-start.17 = (bf16[256,256]{1,0:T(8,128)(2,1)S(1)}, bf16[256,256]{1,0:T(8,128)(2,1)S(1)}, u32[]{:S(2)}, u32[]{:S(2)}) collective-permute-start(bf16[256,256]{1,0:T(8,128)(2,1)S(1)} %get-tuple-element.87), channel_id=1, source_target_pairs={{0,2},{2,0},{4,6},{6,4},{1,3},{3,1},{5,7},{7,5},{8,10},{10,8},{12,... | collective-permute-start | bytes 393224 | tf_op jit(solution)/shard_map/ppermute | solution.py:28
  38.3 12.9 %collective-permute-start.18 = (bf16[256,256]{1,0:T(8,128)(2,1)S(1)}, bf16[256,256]{1,0:T(8,128)(2,1)S(1)}, u32[]{:S(2)}, u32[]{:S(2)}) collective-permute-start(bf16[256,256]{1,0:T(8,128)(2,1)S(1)} %get-tuple-element.88), channel_id=1, source_target_pairs={{0,4},{2,6},{4,0},{6,2},{1,5},{3,7},{5,1},{7,3},{8,12},{10,14},{12... | collective-permute-start | bytes 393224 | tf_op jit(solution)/shard_map/ppermute | solution.py:28
  41.0 10.2 %collective-permute-start.19 = (bf16[256,256]{1,0:T(8,128)(2,1)S(1)}, bf16[256,256]{1,0:T(8,128)(2,1)S(1)}, u32[]{:S(2)}, u32[]{:S(2)}) collective-permute-start(bf16[256,256]{1,0:T(8,128)(2,1)S(1)} %get-tuple-element.89), channel_id=1, source_target_pairs={{0,6},{2,4},{4,2},{6,0},{1,7},{3,5},{5,3},{7,1},{8,14},{10,12},{12... | collective-permute-start | bytes 393224 | tf_op jit(solution)/shard_map/ppermute | solution.py:28
  43.4 10.7 %collective-permute-start.14 = (bf16[64,1024]{1,0:T(8,128)(2,1)S(1)}, bf16[64,1024]{1,0:T(8,128)(2,1)S(1)}, u32[]{:S(2)}, u32[]{:S(2)}) collective-permute-start(bf16[64,1024]{1,0:T(8,128)(2,1)S(1)} %get-tuple-element.94), channel_id=1, source_target_pairs={{0,8},{8,0},{16,24},{24,16},{1,9},{9,1},{17,25},{25,17},{2,10},{10... | collective-permute-start | bytes 393224 | tf_op jit(solution)/shard_map/ppermute | solution.py:28
  44.9 9.9 %collective-permute-start.15 = (bf16[64,1024]{1,0:T(8,128)(2,1)S(1)}, bf16[64,1024]{1,0:T(8,128)(2,1)S(1)}, u32[]{:S(2)}, u32[]{:S(2)}) collective-permute-start(bf16[64,1024]{1,0:T(8,128)(2,1)S(1)} %get-tuple-element.95), channel_id=1, source_target_pairs={{0,16},{8,24},{16,0},{24,8},{1,17},{9,25},{17,1},{25,9},{2,18},{10... | collective-permute-start | bytes 393224 | tf_op jit(solution)/shard_map/ppermute | solution.py:28
  46.4 8.4 %collective-permute-start.16 = (bf16[64,1024]{1,0:T(8,128)(2,1)S(1)}, bf16[64,1024]{1,0:T(8,128)(2,1)S(1)}, u32[]{:S(2)}, u32[]{:S(2)}) collective-permute-start(bf16[64,1024]{1,0:T(8,128)(2,1)S(1)} %get-tuple-element.96), channel_id=1, source_target_pairs={{0,24},{8,16},{16,8},{24,0},{1,25},{9,17},{17,9},{25,1},{2,26},{10... | collective-permute-start | bytes 393224 | tf_op jit(solution)/shard_map/ppermute | solution.py:28
  51.3 4.4 %collective-permute-start.20 = (bf16[64,256]{1,0:T(8,128)(2,1)S(1)}, bf16[64,256]{1,0:T(8,128)(2,1)S(1)}, u32[]{:S(2)}, u32[]{:S(2)}) collective-permute-start(bf16[64,256]{1,0:T(8,128)(2,1)S(1)} %get-tuple-element.98), channel_id=1, source_target_pairs={{0,8},{8,0},{16,24},{24,16},{1,9},{9,1},{17,25},{25,17},{2,10},{10... | collective-permute-start | bytes 98312 | tf_op jit(solution)/shard_map/ppermute | solution.py:28
  52.8 3.9 %collective-permute-start.21 = (bf16[64,256]{1,0:T(8,128)(2,1)S(1)}, bf16[64,256]{1,0:T(8,128)(2,1)S(1)}, u32[]{:S(2)}, u32[]{:S(2)}) collective-permute-start(bf16[64,256]{1,0:T(8,128)(2,1)S(1)} %get-tuple-element.99), channel_id=1, source_target_pairs={{0,16},{8,24},{16,0},{24,8},{1,17},{9,25},{17,1},{25,9},{2,18},{10... | collective-permute-start | bytes 98312 | tf_op jit(solution)/shard_map/ppermute | solution.py:28
  54.1 4.8 %collective-permute-start.22 = (bf16[64,256]{1,0:T(8,128)(2,1)S(1)}, bf16[64,256]{1,0:T(8,128)(2,1)S(1)}, u32[]{:S(2)}, u32[]{:S(2)}) collective-permute-start(bf16[64,256]{1,0:T(8,128)(2,1)S(1)} %get-tuple-element.100), channel_id=1, source_target_pairs={{0,24},{8,16},{16,8},{24,0},{1,25},{9,17},{17,9},{25,1},{2,26},{10... | collective-permute-start | bytes 98312 | tf_op jit(solution)/shard_map/ppermute | solution.py:28

commit v5 on v4

--- a/solution.py
+++ b/solution.py
@@ -157,7 +157,7 @@
                 now = jnp.sum(e, axis=0, keepdims=True)
                 total = now if total is None else total + now
                 dp = dot(values[span, :], g, NT)
-                p_ref[span, :] = dp
+                p_ref[span, :] = dp.astype(jnp.bfloat16)
                 now = jnp.sum(e * dp, axis=0, keepdims=True)
                 dots = now if dots is None else dots + now
             inverse = 1.0 / total
@@ -169,7 +169,7 @@
                 first = level == heads - 1 and rows_now == all_rows
                 part = dot(g_t, p.astype(jnp.bfloat16), NT).T
                 dv_ref[span, :] = part if first else dv_ref[span, :] + part
-                ds = (p * (p_ref[span, :] - dots)).astype(jnp.bfloat16)
+                ds = (p * (p_ref[span, :].astype(jnp.float32) - dots)).astype(jnp.bfloat16)
                 part = dot(ds, q, NN)
                 dk_ref[span, :] = part if first else dk_ref[span, :] + part
                 if ds_out is not None:
@@ -246,7 +246,7 @@
     scratch = [
         V((tokens, HEAD_DIM), bf16),
         V((heads, rows, HEAD_DIM), bf16), V((heads, rows, HEAD_DIM), bf16),
-        V((tokens, rows_now), f32), V((tokens, rows_now), f32),
+        V((tokens, rows_now), f32), V((tokens, rows_now), bf16),
         V((tokens, HEAD_DIM), f32), V((tokens, HEAD_DIM), f32),
     ]
     results = call(

time: 59.8 us -> 59.5 us (level)
  no operation moved by 1% of the time
where the time goes in v5:
time: 59.5 us; the launch traced here: 59.3 us
  starting transfers between devices  25 us (42%)
  waiting for transfers between devices  19.4 us (33%)
  Pallas kernels  14.2 us (24%)
  between operations  0.72 us (1%)
    ppermute x23, starting transfers between devices, exchange(): return lax.ppermute(array, axis, [(i, i ^ by) for i in range(length)])  25 us
    ppermute x23, waiting for transfers between devices, exchange(): return lax.ppermute(array, axis, [(i, i ^ by) for i in range(length)])  19.4 us
    pallas_call x9, Pallas kernels, call(): pl.pallas_call(body, out_shape=shapes, in_specs=in_specs, out_specs=out_s...  14.2 us
  transfers between devices with their start and end apart: 23, of which 13 were waited for; matrix products, arithmetic and copies ran while one was open for 0% of the time, Pallas kernels for 6%

profile of v5, /device:TPU:0, one launch (start us, length us, event | category | flops | bytes accessed | tf_op | source)
XLA Modules:
  0.0 59.3 jit_solution(2442802376537664418)
XLA Ops:
  0.6 0.9 %shard_map.76 = (bf16[64,256]{1,0:T(8,128)(2,1)S(1)}, bf16[64,256]{1,0:T(8,128)(2,1)S(1)}, bf16[64,256]{1,0:T(8,128)(2,1)S(1)}, bf16[64,256]{1,0:T(8,128)(2,1)S(1)}) custom-call(bf16[64,512]{1,0:T(8,128)(2,1)} %refs_0_.1, bf16[64,512]{1,0:T(8,128)(2,1)} %refs_1_.1), custom_call_target="tpu_custom_call" | custom-call | tf_op jit(solution)/shard_map/pallas_call | solution.py:50
  1.6 3.0 %collective-permute-start = (bf16[64,256]{1,0:T(8,128)(2,1)S(1)}, bf16[64,256]{1,0:T(8,128)(2,1)S(1)}, u32[]{:S(2)}, u32[]{:S(2)}) collective-permute-start(bf16[64,256]{1,0:T(8,128)(2,1)S(1)} %get-tuple-element.61), channel_id=1, source_target_pairs={{0,8},{8,0},{16,24},{24,16},{1,9},{9,1},{17,25},{25,17},{2,10},{10... | collective-permute-start | bytes 98312 | tf_op jit(solution)/shard_map/ppermute | solution.py:28
  4.6 1.5 %collective-permute-start.1 = (bf16[64,256]{1,0:T(8,128)(2,1)S(1)}, bf16[64,256]{1,0:T(8,128)(2,1)S(1)}, u32[]{:S(2)}, u32[]{:S(2)}) collective-permute-start(bf16[64,256]{1,0:T(8,128)(2,1)S(1)} %get-tuple-element.62), channel_id=1, source_target_pairs={{0,16},{8,24},{16,0},{24,8},{1,17},{9,25},{17,1},{25,9},{2,18},{10... | collective-permute-start | bytes 98312 | tf_op jit(solution)/shard_map/ppermute | solution.py:28
  6.1 0.0 collective-permute-start.2
  6.1 1.4 %shard_map.77 = (bf16[2,64,1024]{2,1,0:T(8,128)(2,1)S(1)}, bf16[2,64,1024]{2,1,0:T(8,128)(2,1)S(1)}, bf16[2,64,1024]{2,1,0:T(8,128)(2,1)S(1)}, bf16[2,64,1024]{2,1,0:T(8,128)(2,1)S(1)}, s32[32]{0:T(128)S(1)}) custom-call(bf16[64,4096]{1,0:T(8,128)(2,1)} %refs_0_.2, bf16[64,4096]{1,0:T(8,128)(2,1)} %refs_1_.2, s32[32]{0:T(128)} %refs_2_.1), custom_call_target="tpu_custom_call" | custom-call | tf_op jit(solution)/shard_map/pallas_call | solution.py:50
  7.5 1.0 %collective-permute-done.1.refs_2_ = bf16[64,256]{1,0:T(8,128)(2,1)S(1)} collective-permute-done((bf16[64,256]{1,0:T(8,128)(2,1)S(1)}, bf16[64,256]{1,0:T(8,128)(2,1)S(1)}, u32[]{:S(2)}, u32[]{:S(2)}) %collective-permute-start.1) | collective-permute-done | bytes 32800 | tf_op jit(solution)/shard_map/ppermute | solution.py:28
  8.5 2.4 %collective-permute-done.2.refs_3_ = bf16[64,256]{1,0:T(8,128)(2,1)S(1)} collective-permute-done((bf16[64,256]{1,0:T(8,128)(2,1)S(1)}, bf16[64,256]{1,0:T(8,128)(2,1)S(1)}, u32[]{:S(2)}, u32[]{:S(2)}) %collective-permute-start.2) | collective-permute-done | bytes 32800 | tf_op jit(solution)/shard_map/ppermute | solution.py:28
  10.9 0.5 collective-permute-start.3
  11.4 0.1 collective-permute-start.4
  11.5 4.1 %collective-permute-start.8 = (bf16[256,256]{1,0:T(8,128)(2,1)S(1)}, bf16[256,256]{1,0:T(8,128)(2,1)S(1)}, u32[]{:S(2)}, u32[]{:S(2)}) collective-permute-start(bf16[256,256]{1,0:T(8,128)(2,1)S(1)} %shard_map.78.refs_4_), channel_id=1, source_target_pairs={{0,6},{2,4},{4,2},{6,0},{1,7},{3,5},{5,3},{7,1},{8,14},{10,12},{12... | collective-permute-start | bytes 393224 | tf_op jit(solution)/shard_map/ppermute | solution.py:28
  15.6 0.0 collective-permute-start.7
  15.6 0.6 %collective-permute-start.6 = (bf16[256,256]{1,0:T(8,128)(2,1)S(1)}, bf16[256,256]{1,0:T(8,128)(2,1)S(1)}, u32[]{:S(2)}, u32[]{:S(2)}) collective-permute-start(bf16[256,256]{1,0:T(8,128)(2,1)S(1)} %shard_map.78.refs_4_), channel_id=1, source_target_pairs={{0,2},{2,0},{4,6},{6,4},{1,3},{3,1},{5,7},{7,5},{8,10},{10,8},{12,... | collective-permute-start | bytes 393224 | tf_op jit(solution)/shard_map/ppermute | solution.py:28
  16.3 1.0 %collective-permute-done.3.refs_1_ = bf16[2,64,1024]{2,1,0:T(8,128)(2,1)S(1)} collective-permute-done((bf16[2,64,1024]{2,1,0:T(8,128)(2,1)S(1)}, bf16[2,64,1024]{2,1,0:T(8,128)(2,1)S(1)}, u32[]{:S(2)}, u32[]{:S(2)}) %collective-permute-start.3) | collective-permute-done | bytes 262176 | tf_op jit(solution)/shard_map/ppermute | solution.py:28
  17.3 0.5 collective-permute-done.4.refs_2_
  17.8 1.4 %collective-permute-start.5 = (bf16[2,64,1024]{2,1,0:T(8,128)(2,1)S(1)}, bf16[2,64,1024]{2,1,0:T(8,128)(2,1)S(1)}, u32[]{:S(2)}, u32[]{:S(2)}) collective-permute-start(bf16[2,64,1024]{2,1,0:T(8,128)(2,1)S(1)} %get-tuple-element.75), channel_id=1, source_target_pairs={{0,24},{8,16},{16,8},{24,0},{1,25},{9,17},{17,9},{25,1},{2,26},{10... | collective-permute-start | bytes 786440 | tf_op jit(solution)/shard_map/ppermute | solution.py:28
  19.2 0.3 collective-permute-done.8.refs_7_
  19.6 0.0 collective-permute-start.12
  19.6 4.9 %collective-permute-done.7.refs_6_ = bf16[256,256]{1,0:T(8,128)(2,1)S(1)} collective-permute-done((bf16[256,256]{1,0:T(8,128)(2,1)S(1)}, bf16[256,256]{1,0:T(8,128)(2,1)S(1)}, u32[]{:S(2)}, u32[]{:S(2)}) %collective-permute-start.7) | collective-permute-done | bytes 131104 | tf_op jit(solution)/shard_map/ppermute | solution.py:28
  24.5 0.0 collective-permute-start.11
  24.5 0.0 collective-permute-done.6.refs_5_
  24.5 0.5 collective-permute-start.10
  25.0 0.0 collective-permute-start.9
  25.0 0.8 %collective-permute-done.11.refs_10_ = bf16[256,256]{1,0:T(8,128)(2,1)S(1)} collective-permute-done((bf16[256,256]{1,0:T(8,128)(2,1)S(1)}, bf16[256,256]{1,0:T(8,128)(2,1)S(1)}, u32[]{:S(2)}, u32[]{:S(2)}) %collective-permute-start.11) | collective-permute-done | bytes 131104 | tf_op jit(solution)/shard_map/ppermute | solution.py:28
  25.8 0.2 collective-permute-done.10.refs_9_
  26.0 0.3 collective-permute-done.9.refs_8_
  26.4 0.0 collective-permute-done.5.refs_3_
  26.4 9.1 %shard_map.79 = (bf16[1024,256]{1,0:T(8,128)(2,1)S(1)}, bf16[1024,256]{1,0:T(8,128)(2,1)S(1)}, bf16[10,512,512]{2,1,0:T(8,128)(2,1)S(1)}, bf16[2048,128]{1,0:T(8,128)(2,1)S(1)}, s32[4,64,128]{2,1,0:T(8,128)S(1)}) custom-call(s32[32]{0:T(128)S(1)} %get-tuple-element.59.order_ref, bf16[2,64,1024]{2,1,0:T(8,128)(2,1)S(1)} %get-tuple-element.72.refs_0_, ...), custom_call_target="tpu_custom_call" | custom-call | tf_op jit(solution)/shard_map/pallas_call | solution.py:50
  35.5 0.3 collective-permute-start.13
  35.7 1.7 %collective-permute-done.13.refs_1_ = bf16[1024,256]{1,0:T(8,128)(2,1)S(1)} collective-permute-done((bf16[1024,256]{1,0:T(8,128)(2,1)S(1)}, bf16[1024,256]{1,0:T(8,128)(2,1)S(1)}, u32[]{:S(2)}, u32[]{:S(2)}) %collective-permute-start.13) | collective-permute-done | bytes 524320 | tf_op jit(solution)/shard_map/ppermute | solution.py:28
  37.5 0.1 shard_map.80
  37.6 0.4 collective-permute-start.17
  38.0 2.7 %collective-permute-start.18 = (bf16[256,256]{1,0:T(8,128)(2,1)S(1)}, bf16[256,256]{1,0:T(8,128)(2,1)S(1)}, u32[]{:S(2)}, u32[]{:S(2)}) collective-permute-start(bf16[256,256]{1,0:T(8,128)(2,1)S(1)} %get-tuple-element.88), channel_id=1, source_target_pairs={{0,4},{2,6},{4,0},{6,2},{1,5},{3,7},{5,1},{7,3},{8,12},{10,14},{12... | collective-permute-start | bytes 393224 | tf_op jit(solution)/shard_map/ppermute | solution.py:28
  40.7 1.3 %collective-permute-start.19 = (bf16[256,256]{1,0:T(8,128)(2,1)S(1)}, bf16[256,256]{1,0:T(8,128)(2,1)S(1)}, u32[]{:S(2)}, u32[]{:S(2)}) collective-permute-start(bf16[256,256]{1,0:T(8,128)(2,1)S(1)} %get-tuple-element.89), channel_id=1, source_target_pairs={{0,6},{2,4},{4,2},{6,0},{1,7},{3,5},{5,3},{7,1},{8,14},{10,12},{12... | collective-permute-start | bytes 393224 | tf_op jit(solution)/shard_map/ppermute | solution.py:28
  42.0 1.0 %shard_map.81 = (bf16[64,1024]{1,0:T(8,128)(2,1)S(1)}, bf16[64,1024]{1,0:T(8,128)(2,1)S(1)}, bf16[64,1024]{1,0:T(8,128)(2,1)S(1)}, bf16[64,1024]{1,0:T(8,128)(2,1)S(1)}) custom-call(bf16[10,512,512]{2,1,0:T(8,128)(2,1)S(1)} %get-tuple-element.90.ds_ref, bf16[2048,128]{1,0:T(8,128)(2,1)S(1)} %get-tuple-element.91.keys, ...), custom_call_target="tpu_custom_call" | custom-call | tf_op jit(solution)/shard_map/pallas_call | solution.py:50
  43.1 1.5 %collective-permute-start.14 = (bf16[64,1024]{1,0:T(8,128)(2,1)S(1)}, bf16[64,1024]{1,0:T(8,128)(2,1)S(1)}, u32[]{:S(2)}, u32[]{:S(2)}) collective-permute-start(bf16[64,1024]{1,0:T(8,128)(2,1)S(1)} %get-tuple-element.94), channel_id=1, source_target_pairs={{0,8},{8,0},{16,24},{24,16},{1,9},{9,1},{17,25},{25,17},{2,10},{10... | collective-permute-start | bytes 393224 | tf_op jit(solution)/shard_map/ppermute | solution.py:28
  44.6 1.5 %collective-permute-start.15 = (bf16[64,1024]{1,0:T(8,128)(2,1)S(1)}, bf16[64,1024]{1,0:T(8,128)(2,1)S(1)}, u32[]{:S(2)}, u32[]{:S(2)}) collective-permute-start(bf16[64,1024]{1,0:T(8,128)(2,1)S(1)} %get-tuple-element.95), channel_id=1, source_target_pairs={{0,16},{8,24},{16,0},{24,8},{1,17},{9,25},{17,1},{25,9},{2,18},{10... | collective-permute-start | bytes 393224 | tf_op jit(solution)/shard_map/ppermute | solution.py:28
  46.1 0.0 collective-permute-done.17.refs_1_
  46.1 1.8 %collective-permute-start.16 = (bf16[64,1024]{1,0:T(8,128)(2,1)S(1)}, bf16[64,1024]{1,0:T(8,128)(2,1)S(1)}, u32[]{:S(2)}, u32[]{:S(2)}) collective-permute-start(bf16[64,1024]{1,0:T(8,128)(2,1)S(1)} %get-tuple-element.96), channel_id=1, source_target_pairs={{0,24},{8,16},{16,8},{24,0},{1,25},{9,17},{17,9},{25,1},{2,26},{10... | collective-permute-start | bytes 393224 | tf_op jit(solution)/shard_map/ppermute | solution.py:28
  48.0 2.9 %collective-permute-done.18.refs_2_ = bf16[256,256]{1,0:T(8,128)(2,1)S(1)} collective-permute-done((bf16[256,256]{1,0:T(8,128)(2,1)S(1)}, bf16[256,256]{1,0:T(8,128)(2,1)S(1)}, u32[]{:S(2)}, u32[]{:S(2)}) %collective-permute-start.18) | collective-permute-done | bytes 131104 | tf_op jit(solution)/shard_map/ppermute | solution.py:28
  50.9 0.1 shard_map.83
  51.0 1.5 %collective-permute-start.20 = (bf16[64,256]{1,0:T(8,128)(2,1)S(1)}, bf16[64,256]{1,0:T(8,128)(2,1)S(1)}, u32[]{:S(2)}, u32[]{:S(2)}) collective-permute-start(bf16[64,256]{1,0:T(8,128)(2,1)S(1)} %get-tuple-element.98), channel_id=1, source_target_pairs={{0,8},{8,0},{16,24},{24,16},{1,9},{9,1},{17,25},{25,17},{2,10},{10... | collective-permute-start | bytes 98312 | tf_op jit(solution)/shard_map/ppermute | solution.py:28
  52.5 1.3 %collective-permute-start.21 = (bf16[64,256]{1,0:T(8,128)(2,1)S(1)}, bf16[64,256]{1,0:T(8,128)(2,1)S(1)}, u32[]{:S(2)}, u32[]{:S(2)}) collective-permute-start(bf16[64,256]{1,0:T(8,128)(2,1)S(1)} %get-tuple-element.99), channel_id=1, source_target_pairs={{0,16},{8,24},{16,0},{24,8},{1,17},{9,25},{17,1},{25,9},{2,18},{10... | collective-permute-start | bytes 98312 | tf_op jit(solution)/shard_map/ppermute | solution.py:28
  53.8 0.7 %collective-permute-start.22 = (bf16[64,256]{1,0:T(8,128)(2,1)S(1)}, bf16[64,256]{1,0:T(8,128)(2,1)S(1)}, u32[]{:S(2)}, u32[]{:S(2)}) collective-permute-start(bf16[64,256]{1,0:T(8,128)(2,1)S(1)} %get-tuple-element.100), channel_id=1, source_target_pairs={{0,24},{8,16},{16,8},{24,0},{1,25},{9,17},{17,9},{25,1},{2,26},{10... | collective-permute-start | bytes 98312 | tf_op jit(solution)/shard_map/ppermute | solution.py:28
  54.5 0.0 collective-permute-done.16.refs_3_
  54.5 0.8 %shard_map.82 = bf16[64,4096]{1,0:T(8,128)(2,1)} custom-call(bf16[64,1024]{1,0:T(8,128)(2,1)S(1)} %get-tuple-element.93.refs_0_, bf16[64,1024]{1,0:T(8,128)(2,1)S(1)} %collective-permute-done.14.refs_1_, bf16[64,1024]{1,0:T(8,128)(2,1)S(1)} %collective-permute-done.15.refs_2_, bf16[64,1024]{1,0:T(8,128)(2,1)S(1)} %collective-permute-done.16.refs_3_), custom_call_target="tpu_custom_call" | custom-call | tf_op jit(solution)/shard_map/pallas_call | solution.py:50
  55.4 1.0 %collective-permute-done.21.refs_2_ = bf16[64,256]{1,0:T(8,128)(2,1)S(1)} collective-permute-done((bf16[64,256]{1,0:T(8,128)(2,1)S(1)}, bf16[64,256]{1,0:T(8,128)(2,1)S(1)}, u32[]{:S(2)}, u32[]{:S(2)}) %collective-permute-start.21) | collective-permute-done | bytes 32800 | tf_op jit(solution)/shard_map/ppermute | solution.py:28
  56.4 2.2 %collective-permute-done.22.refs_3_ = bf16[64,256]{1,0:T(8,128)(2,1)S(1)} collective-permute-done((bf16[64,256]{1,0:T(8,128)(2,1)S(1)}, bf16[64,256]{1,0:T(8,128)(2,1)S(1)}, u32[]{:S(2)}, u32[]{:S(2)}) %collective-permute-start.22) | collective-permute-done | bytes 32800 | tf_op jit(solution)/shard_map/ppermute | solution.py:28
  58.6 0.7 %shard_map.84 = (bf16[64,512]{1,0:T(8,128)(2,1)}, bf16[64,512]{1,0:T(8,128)(2,1)}) custom-call(bf16[64,256]{1,0:T(8,128)(2,1)S(1)} %get-tuple-element.97.refs_0_, bf16[64,256]{1,0:T(8,128)(2,1)S(1)} %collective-permute-done.20.refs_1_, bf16[64,256]{1,0:T(8,128)(2,1)S(1)} %collective-permute-done.21.refs_2_, bf16[64,256]{1,0:T(8,128)(2,1)S(1)} %collective-permute-done.22.refs_3_), custom_call_target="tpu_custom_call" | custom-call | tf_op jit(solution)/shard_map/pallas_call | solution.py:50
  (7 shorter events, 0.0 us)
Async XLA Ops:
  1.6 5.9 %collective-permute-start = (bf16[64,256]{1,0:T(8,128)(2,1)S(1)}, bf16[64,256]{1,0:T(8,128)(2,1)S(1)}, u32[]{:S(2)}, u32[]{:S(2)}) collective-permute-start(bf16[64,256]{1,0:T(8,128)(2,1)S(1)} %get-tuple-element.61), channel_id=1, source_target_pairs={{0,8},{8,0},{16,24},{24,16},{1,9},{9,1},{17,25},{25,17},{2,10},{10... | collective-permute-start | bytes 98312 | tf_op jit(solution)/shard_map/ppermute | solution.py:28
  4.6 3.9 %collective-permute-start.1 = (bf16[64,256]{1,0:T(8,128)(2,1)S(1)}, bf16[64,256]{1,0:T(8,128)(2,1)S(1)}, u32[]{:S(2)}, u32[]{:S(2)}) collective-permute-start(bf16[64,256]{1,0:T(8,128)(2,1)S(1)} %get-tuple-element.62), channel_id=1, source_target_pairs={{0,16},{8,24},{16,0},{24,8},{1,17},{9,25},{17,1},{25,9},{2,18},{10... | collective-permute-start | bytes 98312 | tf_op jit(solution)/shard_map/ppermute | solution.py:28
  6.1 4.8 %collective-permute-start.2 = (bf16[64,256]{1,0:T(8,128)(2,1)S(1)}, bf16[64,256]{1,0:T(8,128)(2,1)S(1)}, u32[]{:S(2)}, u32[]{:S(2)}) collective-permute-start(bf16[64,256]{1,0:T(8,128)(2,1)S(1)} %get-tuple-element.63), channel_id=1, source_target_pairs={{0,24},{8,16},{16,8},{24,0},{1,25},{9,17},{17,9},{25,1},{2,26},{10... | collective-permute-start | bytes 98312 | tf_op jit(solution)/shard_map/ppermute | solution.py:28
  10.9 6.4 %collective-permute-start.3 = (bf16[2,64,1024]{2,1,0:T(8,128)(2,1)S(1)}, bf16[2,64,1024]{2,1,0:T(8,128)(2,1)S(1)}, u32[]{:S(2)}, u32[]{:S(2)}) collective-permute-start(bf16[2,64,1024]{2,1,0:T(8,128)(2,1)S(1)} %get-tuple-element.70), channel_id=1, source_target_pairs={{0,8},{8,0},{16,24},{24,16},{1,9},{9,1},{17,25},{25,17},{2,10},{10... | collective-permute-start | bytes 786440 | tf_op jit(solution)/shard_map/ppermute | solution.py:28
  11.4 6.4 %collective-permute-start.4 = (bf16[2,64,1024]{2,1,0:T(8,128)(2,1)S(1)}, bf16[2,64,1024]{2,1,0:T(8,128)(2,1)S(1)}, u32[]{:S(2)}, u32[]{:S(2)}) collective-permute-start(bf16[2,64,1024]{2,1,0:T(8,128)(2,1)S(1)} %get-tuple-element.71), channel_id=1, source_target_pairs={{0,16},{8,24},{16,0},{24,8},{1,17},{9,25},{17,1},{25,9},{2,18},{10... | collective-permute-start | bytes 786440 | tf_op jit(solution)/shard_map/ppermute | solution.py:28
  11.5 8.1 %collective-permute-start.8 = (bf16[256,256]{1,0:T(8,128)(2,1)S(1)}, bf16[256,256]{1,0:T(8,128)(2,1)S(1)}, u32[]{:S(2)}, u32[]{:S(2)}) collective-permute-start(bf16[256,256]{1,0:T(8,128)(2,1)S(1)} %shard_map.78.refs_4_), channel_id=1, source_target_pairs={{0,6},{2,4},{4,2},{6,0},{1,7},{3,5},{5,3},{7,1},{8,14},{10,12},{12... | collective-permute-start | bytes 393224 | tf_op jit(solution)/shard_map/ppermute | solution.py:28
  15.6 8.9 %collective-permute-start.7 = (bf16[256,256]{1,0:T(8,128)(2,1)S(1)}, bf16[256,256]{1,0:T(8,128)(2,1)S(1)}, u32[]{:S(2)}, u32[]{:S(2)}) collective-permute-start(bf16[256,256]{1,0:T(8,128)(2,1)S(1)} %shard_map.78.refs_4_), channel_id=1, source_target_pairs={{0,4},{2,6},{4,0},{6,2},{1,5},{3,7},{5,1},{7,3},{8,12},{10,14},{12... | collective-permute-start | bytes 393224 | tf_op jit(solution)/shard_map/ppermute | solution.py:28
  15.6 8.9 %collective-permute-start.6 = (bf16[256,256]{1,0:T(8,128)(2,1)S(1)}, bf16[256,256]{1,0:T(8,128)(2,1)S(1)}, u32[]{:S(2)}, u32[]{:S(2)}) collective-permute-start(bf16[256,256]{1,0:T(8,128)(2,1)S(1)} %shard_map.78.refs_4_), channel_id=1, source_target_pairs={{0,2},{2,0},{4,6},{6,4},{1,3},{3,1},{5,7},{7,5},{8,10},{10,8},{12,... | collective-permute-start | bytes 393224 | tf_op jit(solution)/shard_map/ppermute | solution.py:28
  17.8 8.6 %collective-permute-start.5 = (bf16[2,64,1024]{2,1,0:T(8,128)(2,1)S(1)}, bf16[2,64,1024]{2,1,0:T(8,128)(2,1)S(1)}, u32[]{:S(2)}, u32[]{:S(2)}) collective-permute-start(bf16[2,64,1024]{2,1,0:T(8,128)(2,1)S(1)} %get-tuple-element.75), channel_id=1, source_target_pairs={{0,24},{8,16},{16,8},{24,0},{1,25},{9,17},{17,9},{25,1},{2,26},{10... | collective-permute-start | bytes 786440 | tf_op jit(solution)/shard_map/ppermute | solution.py:28
  19.6 5.4 %collective-permute-start.12 = (bf16[256,256]{1,0:T(8,128)(2,1)S(1)}, bf16[256,256]{1,0:T(8,128)(2,1)S(1)}, u32[]{:S(2)}, u32[]{:S(2)}) collective-permute-start(bf16[256,256]{1,0:T(8,128)(2,1)S(1)} %collective-permute-done.8.refs_7_), channel_id=1, source_target_pairs={{0,1},{1,0},{2,3},{3,2},{4,5},{5,4},{6,7},{7,6},{8,9},{9,8},{10,11... | collective-permute-start | bytes 393224 | tf_op jit(solution)/shard_map/ppermute | solution.py:28
  24.5 1.3 %collective-permute-start.11 = (bf16[256,256]{1,0:T(8,128)(2,1)S(1)}, bf16[256,256]{1,0:T(8,128)(2,1)S(1)}, u32[]{:S(2)}, u32[]{:S(2)}) collective-permute-start(bf16[256,256]{1,0:T(8,128)(2,1)S(1)} %collective-permute-done.7.refs_6_), channel_id=1, source_target_pairs={{0,1},{1,0},{2,3},{3,2},{4,5},{5,4},{6,7},{7,6},{8,9},{9,8},{10,11... | collective-permute-start | bytes 393224 | tf_op jit(solution)/shard_map/ppermute | solution.py:28
  24.5 1.5 %collective-permute-start.10 = (bf16[256,256]{1,0:T(8,128)(2,1)S(1)}, bf16[256,256]{1,0:T(8,128)(2,1)S(1)}, u32[]{:S(2)}, u32[]{:S(2)}) collective-permute-start(bf16[256,256]{1,0:T(8,128)(2,1)S(1)} %collective-permute-done.6.refs_5_), channel_id=1, source_target_pairs={{0,1},{1,0},{2,3},{3,2},{4,5},{5,4},{6,7},{7,6},{8,9},{9,8},{10,11... | collective-permute-start | bytes 393224 | tf_op jit(solution)/shard_map/ppermute | solution.py:28
  25.0 1.3 %collective-permute-start.9 = (bf16[256,256]{1,0:T(8,128)(2,1)S(1)}, bf16[256,256]{1,0:T(8,128)(2,1)S(1)}, u32[]{:S(2)}, u32[]{:S(2)}) collective-permute-start(bf16[256,256]{1,0:T(8,128)(2,1)S(1)} %shard_map.78.refs_4_), channel_id=1, source_target_pairs={{0,1},{1,0},{2,3},{3,2},{4,5},{5,4},{6,7},{7,6},{8,9},{9,8},{10,11... | collective-permute-start | bytes 393224 | tf_op jit(solution)/shard_map/ppermute | solution.py:28
  35.5 2.0 %collective-permute-start.13 = (bf16[1024,256]{1,0:T(8,128)(2,1)S(1)}, bf16[1024,256]{1,0:T(8,128)(2,1)S(1)}, u32[]{:S(2)}, u32[]{:S(2)}) collective-permute-start(bf16[1024,256]{1,0:T(8,128)(2,1)S(1)} %get-tuple-element.85), channel_id=1, source_target_pairs={{0,1},{1,0},{2,3},{3,2},{4,5},{5,4},{6,7},{7,6},{8,9},{9,8},{10,11... | collective-permute-start | bytes 1572872 | tf_op jit(solution)/shard_map/ppermute | solution.py:28
  37.6 8.5 %collective-permute-start.17 = (bf16[256,256]{1,0:T(8,128)(2,1)S(1)}, bf16[256,256]{1,0:T(8,128)(2,1)S(1)}, u32[]{:S(2)}, u32[]{:S(2)}) collective-permute-start(bf16[256,256]{1,0:T(8,128)(2,1)S(1)} %get-tuple-element.87), channel_id=1, source_target_pairs={{0,2},{2,0},{4,6},{6,4},{1,3},{3,1},{5,7},{7,5},{8,10},{10,8},{12,... | collective-permute-start | bytes 393224 | tf_op jit(solution)/shard_map/ppermute | solution.py:28
  38.0 12.9 %collective-permute-start.18 = (bf16[256,256]{1,0:T(8,128)(2,1)S(1)}, bf16[256,256]{1,0:T(8,128)(2,1)S(1)}, u32[]{:S(2)}, u32[]{:S(2)}) collective-permute-start(bf16[256,256]{1,0:T(8,128)(2,1)S(1)} %get-tuple-element.88), channel_id=1, source_target_pairs={{0,4},{2,6},{4,0},{6,2},{1,5},{3,7},{5,1},{7,3},{8,12},{10,14},{12... | collective-permute-start | bytes 393224 | tf_op jit(solution)/shard_map/ppermute | solution.py:28
  40.7 10.2 %collective-permute-start.19 = (bf16[256,256]{1,0:T(8,128)(2,1)S(1)}, bf16[256,256]{1,0:T(8,128)(2,1)S(1)}, u32[]{:S(2)}, u32[]{:S(2)}) collective-permute-start(bf16[256,256]{1,0:T(8,128)(2,1)S(1)} %get-tuple-element.89), channel_id=1, source_target_pairs={{0,6},{2,4},{4,2},{6,0},{1,7},{3,5},{5,3},{7,1},{8,14},{10,12},{12... | collective-permute-start | bytes 393224 | tf_op jit(solution)/shard_map/ppermute | solution.py:28
  43.1 10.7 %collective-permute-start.14 = (bf16[64,1024]{1,0:T(8,128)(2,1)S(1)}, bf16[64,1024]{1,0:T(8,128)(2,1)S(1)}, u32[]{:S(2)}, u32[]{:S(2)}) collective-permute-start(bf16[64,1024]{1,0:T(8,128)(2,1)S(1)} %get-tuple-element.94), channel_id=1, source_target_pairs={{0,8},{8,0},{16,24},{24,16},{1,9},{9,1},{17,25},{25,17},{2,10},{10... | collective-permute-start | bytes 393224 | tf_op jit(solution)/shard_map/ppermute | solution.py:28
  44.6 9.9 %collective-permute-start.15 = (bf16[64,1024]{1,0:T(8,128)(2,1)S(1)}, bf16[64,1024]{1,0:T(8,128)(2,1)S(1)}, u32[]{:S(2)}, u32[]{:S(2)}) collective-permute-start(bf16[64,1024]{1,0:T(8,128)(2,1)S(1)} %get-tuple-element.95), channel_id=1, source_target_pairs={{0,16},{8,24},{16,0},{24,8},{1,17},{9,25},{17,1},{25,9},{2,18},{10... | collective-permute-start | bytes 393224 | tf_op jit(solution)/shard_map/ppermute | solution.py:28
  46.1 8.4 %collective-permute-start.16 = (bf16[64,1024]{1,0:T(8,128)(2,1)S(1)}, bf16[64,1024]{1,0:T(8,128)(2,1)S(1)}, u32[]{:S(2)}, u32[]{:S(2)}) collective-permute-start(bf16[64,1024]{1,0:T(8,128)(2,1)S(1)} %get-tuple-element.96), channel_id=1, source_target_pairs={{0,24},{8,16},{16,8},{24,0},{1,25},{9,17},{17,9},{25,1},{2,26},{10... | collective-permute-start | bytes 393224 | tf_op jit(solution)/shard_map/ppermute | solution.py:28
  51.0 4.4 %collective-permute-start.20 = (bf16[64,256]{1,0:T(8,128)(2,1)S(1)}, bf16[64,256]{1,0:T(8,128)(2,1)S(1)}, u32[]{:S(2)}, u32[]{:S(2)}) collective-permute-start(bf16[64,256]{1,0:T(8,128)(2,1)S(1)} %get-tuple-element.98), channel_id=1, source_target_pairs={{0,8},{8,0},{16,24},{24,16},{1,9},{9,1},{17,25},{25,17},{2,10},{10... | collective-permute-start | bytes 98312 | tf_op jit(solution)/shard_map/ppermute | solution.py:28
  52.5 3.9 %collective-permute-start.21 = (bf16[64,256]{1,0:T(8,128)(2,1)S(1)}, bf16[64,256]{1,0:T(8,128)(2,1)S(1)}, u32[]{:S(2)}, u32[]{:S(2)}) collective-permute-start(bf16[64,256]{1,0:T(8,128)(2,1)S(1)} %get-tuple-element.99), channel_id=1, source_target_pairs={{0,16},{8,24},{16,0},{24,8},{1,17},{9,25},{17,1},{25,9},{2,18},{10... | collective-permute-start | bytes 98312 | tf_op jit(solution)/shard_map/ppermute | solution.py:28
  53.8 4.8 %collective-permute-start.22 = (bf16[64,256]{1,0:T(8,128)(2,1)S(1)}, bf16[64,256]{1,0:T(8,128)(2,1)S(1)}, u32[]{:S(2)}, u32[]{:S(2)}) collective-permute-start(bf16[64,256]{1,0:T(8,128)(2,1)S(1)} %get-tuple-element.100), channel_id=1, source_target_pairs={{0,24},{8,16},{16,8},{24,0},{1,25},{9,17},{17,9},{25,1},{2,26},{10... | collective-permute-start | bytes 98312 | tf_op jit(solution)/shard_map/ppermute | solution.py:28
